TPU v7x, 32 devices: a whole 2x2x4 slice. The times are simulated.
32 devices in a mesh: ctx: 4 (over y, x), expert: 8 (over z, core).
Axes of the slice: x: 2, y: 2, z: 4, core: 2. Of those that a mesh axis runs over, the one named last changes fastest.
Arguments:
- tokens: bfloat16 [8, 1024, 2048], P('expert', 'ctx'), may hold values from -6 to 6
- query_weight: bfloat16 [2048, 4096], P(('ctx', 'expert')), may hold values from -0.125 to 0.125
- key_weight: bfloat16 [2048, 512], P(('ctx', 'expert')), may hold values from -0.125 to 0.125
- value_weight: bfloat16 [2048, 512], P(('ctx', 'expert')), may hold values from -0.125 to 0.125
- output_weight: bfloat16 [4096, 2048], P(('ctx', 'expert')), may hold values from -1.5 to 1.5
- norm_gains: bfloat16 [2, 2048], P(None, ('ctx', 'expert')), may hold values from 0.5 to 1.5
- head_gains: bfloat16 [2, 128], P(None, ('ctx', 'expert')), may hold values from 0.5 to 1.5
- expert_gate: bfloat16 [32, 2048, 768], P(('ctx', 'expert')), may hold values from -0.125 to 0.125
- expert_up: bfloat16 [32, 2048, 768], P(('ctx', 'expert')), may hold values from -0.125 to 0.125
- expert_down: bfloat16 [32, 768, 2048], P(('ctx', 'expert')), may hold values from -0.625 to 0.625
- routes: int32 [8, 1024, 8], P('expert', 'ctx'), may hold values from 0 to 31, all different within a row; in each aligned block of 256 rows (0 to 255, 256 to 511, ..., all dimensions but the last counted through in order) at most 80 rows name the same one
- route_gates: float32 [8, 1024, 8], P('expert', 'ctx'), may hold values from 0.06 to 0.19
- cotangent: bfloat16 [8, 1024, 2048], P('expert', 'ctx'), may hold values from -6 to 6
Outputs:
- mixed_out: bfloat16 [8, 1024, 2048], P('expert', 'ctx')
- grad_tokens: bfloat16 [8, 1024, 2048], P('expert', 'ctx')
- grad_query_weight: float32 [2048, 4096], P(('ctx', 'expert'))
- grad_key_weight: float32 [2048, 512], P(('ctx', 'expert'))
- grad_value_weight: float32 [2048, 512], P(('ctx', 'expert'))
- grad_output_weight: float32 [4096, 2048], P(('ctx', 'expert'))
- grad_norm_gains: float32 [2, 2048], P(None, ('ctx', 'expert'))
- grad_head_gains: float32 [2, 128], P(None, ('ctx', 'expert'))
- grad_expert_gate: float32 [32, 2048, 768], P(('ctx', 'expert'))
- grad_expert_up: float32 [32, 2048, 768], P(('ctx', 'expert'))
- grad_expert_down: float32 [32, 768, 2048], P(('ctx', 'expert'))
Inputs may be any that keep to these rules, and one draw needn't show every extreme that they name: `routes`: each token names 8 different experts; among the 256 rows of one device no expert is named by more than 80 rows, and in some such blocks one is named by exactly 80.
All inputs are finite; a program needn't handle non-finite values.
Results may differ from a plain program's by a relative error of at most 0.02.
Values may be sent and summed in bfloat16 or wider, within the bound.
A program may use at most 320 MiB of HBM per device.

v0:
```python
import jax
import jax.numpy as jnp
from jax import lax
from jax.sharding import PartitionSpec as P

HQ = 32
HK = 4
HD = 128


epsilon = 1e-06
rope_base = 1000000.0
masked_value = -1e30


def rms_scale(values, scale_gain):
    return (
        values * lax.rsqrt(jnp.mean(values * values, axis=-1, keepdims=True) + epsilon) * scale_gain
    )


def rotate(values, positions):
    half_size = values.shape[-1] // 2
    frequency = rope_base ** (-jnp.arange(half_size, dtype=jnp.float32) / half_size)
    angles = positions.astype(jnp.float32)[:, None] * frequency[None, :]
    cosine = jnp.cos(angles)[:, None, :]
    sine_part = jnp.sin(angles)[:, None, :]
    first_half = values[..., :half_size]
    second_half = values[..., half_size:]
    return jnp.concatenate(
        [
            first_half * cosine - second_half * sine_part,
            second_half * cosine + first_half * sine_part,
        ],
        axis=-1,
    )


def body(
    tokens,
    query_weight,
    key_weight,
    value_weight,
    output_weight,
    norm_gains,
    head_gains,
    expert_gate,
    expert_up,
    expert_down,
    routes,
    route_gates,
    cotangent,
):
    seq_rows = tokens.shape[1]
    width = tokens.shape[2]
    groups = HQ // HK
    kv_width = HK * HD
    scale = HD ** (-0.5)
    positions = lax.axis_index("ctx") * seq_rows + jnp.arange(seq_rows, dtype=jnp.int32)
    last_pos = lax.axis_index("ctx") * seq_rows + seq_rows - 1
    rows_in = tokens.reshape(seq_rows, width).astype(jnp.float32)
    full_q, full_k, full_v, full_o, gains, head_gain = (
        lax.all_gather(query_weight, ("ctx", "expert"), axis=0, tiled=True),
        lax.all_gather(key_weight, ("ctx", "expert"), axis=0, tiled=True),
        lax.all_gather(value_weight, ("ctx", "expert"), axis=0, tiled=True),
        lax.all_gather(output_weight, ("ctx", "expert"), axis=0, tiled=True),
        lax.all_gather(norm_gains, ("ctx", "expert"), axis=1, tiled=True),
        lax.all_gather(head_gains, ("ctx", "expert"), axis=1, tiled=True),
    )

    def head_prep(raw_heads, gain_vec):
        return rotate(rms_scale(raw_heads, gain_vec), positions)

    normed = rms_scale(rows_in, gains[0].astype(jnp.float32)).astype(jnp.bfloat16)
    query_raw = jnp.dot(normed, full_q, preferred_element_type=jnp.float32).reshape(
        seq_rows, HQ, HD
    )
    key_raw = jnp.dot(normed, full_k, preferred_element_type=jnp.float32).reshape(seq_rows, HK, HD)
    value_rows = jnp.dot(normed, full_v, preferred_element_type=jnp.float32).astype(jnp.bfloat16)
    query_gain = head_gain[0].astype(jnp.float32)
    key_gain = head_gain[1].astype(jnp.float32)
    queries = head_prep(query_raw, query_gain).astype(jnp.bfloat16)
    keys_rot = head_prep(key_raw, key_gain).astype(jnp.bfloat16)
    kv_rows = jnp.concatenate([keys_rot.reshape(seq_rows, kv_width), value_rows], axis=1)
    grouped = queries.reshape(seq_rows, HK, groups, HD)

    def scores_for(key_block, base_row):
        scores = (
            jnp.einsum("qhgd,khd->hgqk", grouped, key_block, preferred_element_type=jnp.float32)
            * scale
        )
        key_pos = base_row + jnp.arange(key_block.shape[0], dtype=jnp.int32)
        allowed = key_pos[None, :] <= positions[:, None]
        return (scores, allowed)

    start_state = (
        jnp.full((HK, groups, seq_rows), masked_value, jnp.float32),
        jnp.zeros((HK, groups, seq_rows), jnp.float32),
        jnp.zeros((HK, groups, seq_rows, HD), jnp.float32),
    )
    shard_rows = lax.all_gather(kv_rows, "ctx", axis=0, tiled=True)
    blocks = shard_rows.reshape(shard_rows.shape[0] // seq_rows, seq_rows, 2 * kv_width)

    def step(state_now, element):
        block_index, block_rows = element
        base_row = block_index * seq_rows

        def step_visit(state_in):
            largest, total_sum, accum = state_in
            key_block = block_rows[:, :kv_width].reshape(seq_rows, HK, HD)
            value_block = block_rows[:, kv_width:].reshape(seq_rows, HK, HD)
            scores, allowed = scores_for(key_block, base_row)
            scores = jnp.where(allowed, scores, masked_value)
            new_largest = jnp.maximum(largest, jnp.max(scores, axis=-1))
            weights = jnp.where(allowed, jnp.exp(scores - new_largest[..., None]), 0.0)
            factor = jnp.exp(largest - new_largest)
            total_sum = total_sum * factor + jnp.sum(weights, axis=-1)
            accum = accum * factor[..., None] + jnp.einsum(
                "hgqk,khd->hgqd",
                weights.astype(jnp.bfloat16),
                value_block,
                preferred_element_type=jnp.float32,
            )
            return (new_largest, total_sum, accum)

        def step_skip(state_in):
            return state_in

        return (lax.cond(base_row <= last_pos, step_visit, step_skip, state_now), None)

    final_state, unused = lax.scan(
        step, start_state, (jnp.arange(blocks.shape[0], dtype=jnp.int32), blocks)
    )
    largest, total_sum, accum = final_state
    attended = (accum / total_sum[..., None]).transpose(2, 0, 1, 3).reshape(seq_rows, HQ * HD)
    log_total = largest + jnp.log(total_sum)
    attended_low = attended.astype(jnp.bfloat16)
    hidden = rows_in + jnp.dot(attended_low, full_o, preferred_element_type=jnp.float32)
    normed_mlp = rms_scale(hidden, gains[1].astype(jnp.float32)).astype(jnp.bfloat16)
    devices = lax.axis_size(("ctx", "expert"))
    local_experts = expert_gate.shape[0]
    experts = local_experts * devices
    topk = routes.shape[2]
    capacity = max(2, 5 * seq_rows * topk // (4 * experts))
    route_ids = routes.reshape(seq_rows * topk)
    onehot = (route_ids[:, None] == jnp.arange(experts, dtype=jnp.int32)[None, :]).astype(jnp.int32)
    slots = jnp.sum((jnp.cumsum(onehot, axis=0) - 1) * onehot, axis=1)
    target = route_ids * capacity + slots
    owner_row = jnp.arange(seq_rows * topk, dtype=jnp.int32) // topk
    gate_rows = route_gates.reshape(seq_rows, topk)

    def to_slots(row_block):
        buffer = (
            jnp.zeros((experts * capacity, row_block.shape[1]), row_block.dtype)
            .at[target]
            .set(row_block)
        )
        return buffer.reshape(devices, local_experts * capacity, row_block.shape[1])

    def to_experts(arrived):
        return (
            arrived.reshape(devices, local_experts, capacity, -1)
            .transpose(1, 0, 2, 3)
            .reshape(local_experts, devices * capacity, -1)
        )

    def from_experts(expert_rows):
        return (
            expert_rows.reshape(local_experts, devices, capacity, -1)
            .transpose(1, 0, 2, 3)
            .reshape(devices, local_experts * capacity, -1)
        )

    arrived = to_experts(
        lax.all_to_all(
            to_slots(normed_mlp[owner_row]),
            ("ctx", "expert"),
            split_axis=0,
            concat_axis=0,
            tiled=True,
        )
    )
    gate_pre = jnp.einsum("erd,edf->erf", arrived, expert_gate, preferred_element_type=jnp.float32)
    up_pre = jnp.einsum("erd,edf->erf", arrived, expert_up, preferred_element_type=jnp.float32)
    sigmoid_gate = jax.nn.sigmoid(gate_pre)
    swish_gate = gate_pre * sigmoid_gate
    activated = (swish_gate * up_pre).astype(jnp.bfloat16)
    produced = jnp.einsum(
        "erf,efd->erd", activated, expert_down, preferred_element_type=jnp.float32
    ).astype(jnp.bfloat16)
    returned = lax.all_to_all(
        from_experts(produced), ("ctx", "expert"), split_axis=0, concat_axis=0, tiled=True
    ).reshape(experts * capacity, width)
    expert_out = returned[target].astype(jnp.float32).reshape(seq_rows, topk, width)
    mixed = hidden + jnp.sum(gate_rows[:, :, None] * expert_out, axis=1)
    full_q, full_k, full_v, full_o, gains, head_gain = (
        lax.all_gather(query_weight, ("ctx", "expert"), axis=0, tiled=True),
        lax.all_gather(key_weight, ("ctx", "expert"), axis=0, tiled=True),
        lax.all_gather(value_weight, ("ctx", "expert"), axis=0, tiled=True),
        lax.all_gather(output_weight, ("ctx", "expert"), axis=0, tiled=True),
        lax.all_gather(norm_gains, ("ctx", "expert"), axis=1, tiled=True),
        lax.all_gather(head_gains, ("ctx", "expert"), axis=1, tiled=True),
    )
    grad_out = cotangent.reshape(seq_rows, width).astype(jnp.float32)
    grad_rows = (
        (gate_rows[:, :, None] * grad_out[:, None, :])
        .astype(jnp.bfloat16)
        .reshape(seq_rows * topk, width)
    )
    grad_arrived = to_experts(
        lax.all_to_all(
            to_slots(grad_rows), ("ctx", "expert"), split_axis=0, concat_axis=0, tiled=True
        )
    )
    grad_down = jnp.einsum(
        "erf,erd->efd", activated, grad_arrived, preferred_element_type=jnp.float32
    )
    grad_act = jnp.einsum(
        "erd,efd->erf", grad_arrived, expert_down, preferred_element_type=jnp.float32
    )
    grad_up_pre = (grad_act * swish_gate).astype(jnp.bfloat16)
    grad_gate_pre = (
        grad_act * up_pre * sigmoid_gate * (1.0 + gate_pre * (1.0 - sigmoid_gate))
    ).astype(jnp.bfloat16)
    grad_gate = jnp.einsum(
        "erd,erf->edf", arrived, grad_gate_pre, preferred_element_type=jnp.float32
    )
    grad_up = jnp.einsum("erd,erf->edf", arrived, grad_up_pre, preferred_element_type=jnp.float32)
    grad_inputs = jnp.einsum(
        "erf,edf->erd", grad_gate_pre, expert_gate, preferred_element_type=jnp.float32
    )
    grad_inputs = (
        grad_inputs
        + jnp.einsum("erf,edf->erd", grad_up_pre, expert_up, preferred_element_type=jnp.float32)
    ).astype(jnp.bfloat16)
    grad_back = lax.all_to_all(
        from_experts(grad_inputs), ("ctx", "expert"), split_axis=0, concat_axis=0, tiled=True
    ).reshape(experts * capacity, width)
    grad_normed_mlp = jnp.sum(
        grad_back[target].astype(jnp.float32).reshape(seq_rows, topk, width), axis=1
    )
    unused_norm, norm_pull = jax.vjp(rms_scale, hidden, gains[1].astype(jnp.float32))
    grad_hidden_norm, grad_gain_mlp = norm_pull(grad_normed_mlp)
    grad_hidden = grad_out + grad_hidden_norm
    grad_branch = grad_hidden.astype(jnp.bfloat16)
    grad_wo = jnp.einsum("qa,qd->ad", attended_low, grad_branch, preferred_element_type=jnp.float32)
    grad_attended = jnp.einsum(
        "qd,ad->qa", grad_branch, full_o, preferred_element_type=jnp.float32
    ).astype(jnp.bfloat16)
    all_kv = lax.all_gather(kv_rows, "ctx", axis=0, tiled=True)
    grad_grouped = grad_attended.reshape(seq_rows, HK, groups, HD)
    delta = jnp.einsum(
        "qhgd,qhgd->hgq",
        grad_grouped.astype(jnp.float32),
        attended.reshape(seq_rows, HK, groups, HD),
    )
    kv_blocks = all_kv.reshape(-1, seq_rows, 2 * kv_width)

    def back_step(grad_query, element):
        block_index, block_rows = element
        base_row = block_index * seq_rows

        def back_visit(grad_in):
            key_block = block_rows[:, :kv_width].reshape(seq_rows, HK, HD)
            value_block = block_rows[:, kv_width:].reshape(seq_rows, HK, HD)
            scores, allowed = scores_for(key_block, base_row)
            probs = jnp.where(allowed, jnp.exp(scores - log_total[..., None]), 0.0)
            grad_probs = jnp.einsum(
                "qhgd,khd->hgqk", grad_grouped, value_block, preferred_element_type=jnp.float32
            )
            grad_scores = (probs * (grad_probs - delta[..., None])).astype(jnp.bfloat16)
            grad_next = grad_in + jnp.einsum(
                "hgqk,khd->qhgd", grad_scores, key_block, preferred_element_type=jnp.float32
            )
            grad_keys = (
                jnp.einsum(
                    "hgqk,qhgd->khd", grad_scores, grouped, preferred_element_type=jnp.float32
                )
                * scale
            )
            grad_values = jnp.einsum(
                "hgqk,qhgd->khd",
                probs.astype(jnp.bfloat16),
                grad_grouped,
                preferred_element_type=jnp.float32,
            )
            joined = jnp.concatenate(
                [grad_keys.reshape(seq_rows, kv_width), grad_values.reshape(seq_rows, kv_width)],
                axis=1,
            )
            return (grad_next, joined)

        def back_skip(grad_in):
            return (grad_in, jnp.zeros((seq_rows, 2 * kv_width), jnp.float32))

        return lax.cond(base_row <= last_pos, back_visit, back_skip, grad_query)

    grad_query, grad_kv_terms = lax.scan(
        back_step,
        jnp.zeros((seq_rows, HK, groups, HD), jnp.float32),
        (jnp.arange(kv_blocks.shape[0], dtype=jnp.int32), kv_blocks),
    )
    grad_query = grad_query * scale
    grad_kv = lax.psum_scatter(
        grad_kv_terms.reshape(-1, 2 * kv_width).astype(jnp.bfloat16),
        "ctx",
        scatter_dimension=0,
        tiled=True,
    ).astype(jnp.float32)
    unused_query, pull_query = jax.vjp(head_prep, query_raw, query_gain)
    grad_query_raw, grad_query_gain = pull_query(grad_query.reshape(seq_rows, HQ, HD))
    unused_key, pull_key = jax.vjp(head_prep, key_raw, key_gain)
    grad_key_raw, grad_key_gain = pull_key(grad_kv[:, :kv_width].reshape(seq_rows, HK, HD))
    grad_q_low = grad_query_raw.reshape(seq_rows, HQ * HD).astype(jnp.bfloat16)
    grad_k_low = grad_key_raw.reshape(seq_rows, kv_width).astype(jnp.bfloat16)
    grad_v_low = grad_kv[:, kv_width:].astype(jnp.bfloat16)
    grad_wq = jnp.einsum("qd,qa->da", normed, grad_q_low, preferred_element_type=jnp.float32)
    grad_wk = jnp.einsum("qd,qa->da", normed, grad_k_low, preferred_element_type=jnp.float32)
    grad_wv = jnp.einsum("qd,qa->da", normed, grad_v_low, preferred_element_type=jnp.float32)
    grad_normed = jnp.einsum("qa,da->qd", grad_q_low, full_q, preferred_element_type=jnp.float32)
    grad_normed = grad_normed + jnp.einsum(
        "qa,da->qd", grad_k_low, full_k, preferred_element_type=jnp.float32
    )
    grad_normed = grad_normed + jnp.einsum(
        "qa,da->qd", grad_v_low, full_v, preferred_element_type=jnp.float32
    )
    unused_attn, pull_attn = jax.vjp(rms_scale, rows_in, gains[0].astype(jnp.float32))
    grad_rows_norm, grad_gain_attn = pull_attn(grad_normed)
    grad_input = grad_hidden + grad_rows_norm
    gain_grads = jnp.stack([grad_gain_attn, grad_gain_mlp])
    head_grads = jnp.stack([grad_query_gain, grad_key_gain])
    sum_q, sum_k, sum_v, sum_o, sum_gain, sum_head = (
        lax.psum_scatter(grad_wq, ("ctx", "expert"), scatter_dimension=0, tiled=True),
        lax.psum_scatter(grad_wk, ("ctx", "expert"), scatter_dimension=0, tiled=True),
        lax.psum_scatter(grad_wv, ("ctx", "expert"), scatter_dimension=0, tiled=True),
        lax.psum_scatter(grad_wo, ("ctx", "expert"), scatter_dimension=0, tiled=True),
        lax.psum_scatter(gain_grads, ("ctx", "expert"), scatter_dimension=1, tiled=True),
        lax.psum_scatter(head_grads, ("ctx", "expert"), scatter_dimension=1, tiled=True),
    )
    return (
        mixed.astype(jnp.bfloat16).reshape(tokens.shape),
        grad_input.astype(jnp.bfloat16).reshape(tokens.shape),
        sum_q,
        sum_k,
        sum_v,
        sum_o,
        sum_gain,
        sum_head,
        grad_gate,
        grad_up,
        grad_down,
    )


def solution(mesh):
    return jax.shard_map(
        body,
        mesh=mesh,
        in_specs=(
            P("expert", "ctx", None),
            P(("ctx", "expert"), None),
            P(("ctx", "expert"), None),
            P(("ctx", "expert"), None),
            P(("ctx", "expert"), None),
            P(None, ("ctx", "expert")),
            P(None, ("ctx", "expert")),
            P(("ctx", "expert"), None, None),
            P(("ctx", "expert"), None, None),
            P(("ctx", "expert"), None, None),
            P("expert", "ctx", None),
            P("expert", "ctx", None),
            P("expert", "ctx", None),
        ),
        out_specs=(
            P("expert", "ctx", None),
            P("expert", "ctx", None),
            P(("ctx", "expert"), None),
            P(("ctx", "expert"), None),
            P(("ctx", "expert"), None),
            P(("ctx", "expert"), None),
            P(None, ("ctx", "expert")),
            P(None, ("ctx", "expert")),
            P(("ctx", "expert"), None, None),
            P(("ctx", "expert"), None, None),
            P(("ctx", "expert"), None, None),
        ),
        check_vma=False,
    )
```

profile of v0, /device:TPU:16, one launch (start us, length us, event | category | flops | bytes accessed | tf_op | source)
XLA Modules:
  0.0 2779.7 jit_solution(2273612461330958351)
XLA Ops:
  8.7 37.1 %all-gather = bf16[32,64,2]{1,2,0:T(2,128)(2,1)S(1)} all-gather(bf16[1,64,2]{1,2,0:T(2,128)(2,1)} %bitcast.346), channel_id=1, replica_groups=mesh['ctx'=4,'expert'=8] {'ctx','expert'}, dimensions={0}, use_global_device_ids=true | all-gather | bytes 8448 | tf_op jit(solution)/shard_map/all_gather | solution.py:67
  45.9 36.6 %all-gather.1 = bf16[32,4,2]{1,2,0:T(2,128)(2,1)S(1)} all-gather(bf16[1,4,2]{1,2,0:T(2,128)(2,1)} %bitcast.347), channel_id=1, replica_groups=mesh['ctx'=4,'expert'=8] {'ctx','expert'}, dimensions={0}, use_global_device_ids=true | all-gather | bytes 528 | tf_op jit(solution)/shard_map/all_gather | solution.py:68
  93.7 31.7 %all-gather.10.cloned.1.call-done = bf16[2048,512]{1,0:T(8,128)(2,1)} async-done(((bf16[64,512]{1,0:T(8,128)(2,1)}), bf16[2048,512]{1,0:T(8,128)(2,1)}) %all-gather.10.cloned.1.call-update) | async-done | bytes 2097168 | tf_op jit(solution)/shard_map/all_gather | solution.py:65
  132.5 15.9 reduce-window.6
  159.4 5.6 all-gather.12.cloned.1.call-done
  168.9 112.9 %all-gather.14.cloned.1.call-done = bf16[2048,4096]{1,0:T(8,128)(2,1)} async-done(((bf16[64,4096]{1,0:T(8,128)(2,1)}), bf16[2048,4096]{1,0:T(8,128)(2,1)}) %all-gather.14.cloned.1.call-update) | async-done | bytes 16777232 | tf_op jit(solution)/shard_map/all_gather | solution.py:63
  281.9 22.8 copy.83
  304.6 8.9 multiply_reduce_fusion.3
  324.2 17.5 while.31
  325.4 12.4 conditional.6
  341.7 5.7 copy.86
  351.8 46.1 %all-gather.16.cloned.1.call-done = bf16[4096,2048]{1,0:T(8,128)(2,1)} async-done(((bf16[128,2048]{1,0:T(8,128)(2,1)}), bf16[4096,2048]{1,0:T(8,128)(2,1)}) %all-gather.16.cloned.1.call-update) | async-done | bytes 16777232 | tf_op jit(solution)/shard_map/all_gather | solution.py:66
  397.8 11.2 multiply_reduce_fusion.6
  411.6 46.1 %scatter_custom_fusion = bf16[2560,2048]{1,0:T(8,128)(2,1)} fusion(s32[2048]{0:T(1024)S(1)} %bitcast.337, bf16[256,2048]{1,0:T(8,128)(2,1)} %multiply_convert_fusion.3, s32[2048]{0:T(1024)S(1)} %broadcast_clamp_fusion.1, bf16[]{:T(256)} %constant.119.clone.1), kind=kCustom, calls=%fused_computation.56 | custom fusion | bytes 10486272 | tf_op jit(solution)/shard_map/scatter | solution.py:156
  465.9 19.2 scatter_custom_fusion.1
  485.1 203.3 %all-to-all-done = bf16[32,80,2048]{2,1,0:T(8,128)(2,1)} async-done(((bf16[32,80,2048]{2,1,0:T(8,128)(2,1)}), bf16[32,80,2048]{2,1,0:T(8,128)(2,1)}, u32[]{:S(2)}, u32[]{:S(2)}) %all-to-all-start) | async-done | bytes 10485792 | tf_op jit(solution)/shard_map/all_to_all | solution.py:175
  688.4 8.4 all-to-all-start.2
  696.8 14.0 fusion.46
  710.8 13.0 fusion.50
  723.8 198.4 %all-to-all-done.2 = bf16[32,80,2048]{2,1,0:T(8,128)(2,1)} async-done(((bf16[32,80,2048]{2,1,0:T(8,128)(2,1)}), bf16[32,80,2048]{2,1,0:T(8,128)(2,1)}, u32[]{:S(2)}, u32[]{:S(2)}) %all-to-all-start.2) | async-done | bytes 10485792 | tf_op jit(solution)/shard_map/all_to_all | solution.py:211
  922.2 19.7 multiply_convert_fusion
  941.9 15.5 fusion.48
  957.4 16.5 add_convert_fusion
  973.9 8.1 all-to-all-start.3
  982.0 13.0 convolution_convert_fusion
  995.0 212.5 %all-to-all-done.3 = bf16[32,80,2048]{2,1,0:T(8,128)(2,1)} async-done(((bf16[32,80,2048]{2,1,0:T(8,128)(2,1)}), bf16[32,80,2048]{2,1,0:T(8,128)(2,1)}, u32[]{:S(2)}, u32[]{:S(2)}) %all-to-all-start.3) | async-done | bytes 10485792 | tf_op jit(solution)/shard_map/all_to_all | solution.py:236
  1207.5 8.2 all-to-all-start.1
  1216.1 21.7 gather_fusion.1
  1237.8 203.4 %all-to-all-done.1 = bf16[32,80,2048]{2,1,0:T(8,128)(2,1)} async-done(((bf16[32,80,2048]{2,1,0:T(8,128)(2,1)}), bf16[32,80,2048]{2,1,0:T(8,128)(2,1)}, u32[]{:S(2)}, u32[]{:S(2)}) %all-to-all-start.1) | async-done | bytes 10485792 | tf_op jit(solution)/shard_map/all_to_all | solution.py:191
  1441.2 21.7 gather_fusion
  1462.9 15.1 convert_reduce_fusion
  1481.8 12.3 fusion.68
  1501.5 5.3 copy.117
  1513.8 32.0 %while.32 = (s32[]{:T(128)}, f32[256,4,8,128]{3,0,2,1:T(8,128)}, bf16[4,256,1024]{2,1,0:T(8,128)(2,1)}, s32[4]{0:T(128)S(1)}, s32[]{:T(128)}, /*index=5*/bf16[4,...) while((s32[]{:T(128)}, f32[256,4,8,128]{3,0,2,1:T(8,128)}, ...), condition=%wide.region_21.22_spmd.clone, body=%wide.region_18.21_spmd.clone.sunk | while | flops 2707751424 | bytes 103324512 | solution.py:298
  1515.4 14.8 conditional.7
  1550.6 5.5 copy.96
  1564.1 12.3 fusion.102
  1576.4 50.6 %reduce-scatter.10.cloned.1.call-done = bf16[256,1024]{1,0:T(8,128)(2,1)} async-done(((bf16[1024,1024]{1,0:T(8,128)(2,1)}), bf16[256,1024]{1,0:T(8,128)(2,1)}) %reduce-scatter.10.cloned.1.call-update) | async-done | bytes 524304 | tf_op jit(solution)/shard_map/reduce_scatter | solution.py:304
  1645.3 14.8 fusion.80
  1661.6 13.3 fusion.77
  1674.9 14.1 convolution_bitcast_fusion.1
  1689.0 13.4 convolution_bitcast_fusion.2
  1702.4 13.7 convolution_bitcast_fusion.3
  1716.1 39.4 %all-reduce.4 = f32[2,128]{1,0:T(2,128)S(1)} all-reduce(f32[2,128]{1,0:T(2,128)S(1)} %pad_maximum_fusion.4), channel_id=8, replica_groups=mesh['ctx'=4,'expert'=8] {'ctx','expert'}, use_global_device_ids=true, to_apply=%region_35.36.clone | all-reduce | flops 256 | bytes 2048
  1762.5 140.0 %reduce-scatter.14.cloned.1.call-done = f32[64,512]{1,0:T(8,128)} async-done(((f32[2048,512]{1,0:T(8,128)}), f32[64,512]{1,0:T(8,128)}) %reduce-scatter.14.cloned.1.call-update) | async-done | bytes 131088 | tf_op jit(solution)/shard_map/reduce_scatter | solution.py:334
  1902.5 142.5 %reduce-scatter.16.cloned.1.call-done = f32[64,512]{1,0:T(8,128)} async-done(((f32[2048,512]{1,0:T(8,128)}), f32[64,512]{1,0:T(8,128)}) %reduce-scatter.16.cloned.1.call-update) | async-done | bytes 131088 | tf_op jit(solution)/shard_map/reduce_scatter | solution.py:335
  2044.9 367.5 %reduce-scatter.18.cloned.1.call-done = f32[128,2048]{1,0:T(8,128)} async-done(((f32[4096,2048]{1,0:T(8,128)}), f32[128,2048]{1,0:T(8,128)}) %reduce-scatter.18.cloned.1.call-update) | async-done | bytes 1048592 | tf_op jit(solution)/shard_map/reduce_scatter | solution.py:336
  2412.4 360.5 %reduce-scatter.12.cloned.1.call-done = f32[64,4096]{1,0:T(8,128)} async-done(((f32[2048,4096]{1,0:T(8,128)}), f32[64,4096]{1,0:T(8,128)}) %reduce-scatter.12.cloned.1.call-update) | async-done | bytes 1048592 | tf_op jit(solution)/shard_map/reduce_scatter | solution.py:333
  (286 shorter events, 161.7 us)
Async XLA Ops:
  7.2 915.0 %copy-start = (bf16[1,768,2048]{2,1,0:T(8,128)(2,1)S(1)}, bf16[1,768,2048]{2,1,0:T(8,128)(2,1)}, u32[]{:S(2)}) copy-start(bf16[1,768,2048]{2,1,0:T(8,128)(2,1)} %param.30) | copy-start | bytes 9437188
  7.2 77.9 %all-gather.8.cloned.1.call-start = ((), (), s32[]{:S(2)}) async-start(), calls=%async_computation.10 | async-start | bytes 2162688 | tf_op jit(solution)/shard_map/all_gather | solution.py:64
  7.9 117.5 %all-gather.10.cloned.1.call-start = ((), (), s32[]{:S(2)}) async-start(), calls=%async_computation.11 | async-start | bytes 2162688 | tf_op jit(solution)/shard_map/all_gather | solution.py:65
  8.7 156.3 %all-gather.12.cloned.1.call-start = ((), (), s32[]{:S(2)}) async-start(), calls=%async_computation.12 | async-start | bytes 2621440 | tf_op jit(solution)/shard_map/all_gather | solution.py:101
  84.7 7.2 copy-start.54
  84.7 7.1 copy-start.40
  85.1 229.9 %copy-start.25 = (f32[256,64]{0,1:T(8,128)}, f32[256,64]{0,1:T(8,128)S(1)}, u32[]{:S(2)}) copy-start(f32[256,64]{0,1:T(8,128)S(1)} %get-tuple-element.419) | copy-start | bytes 196612
  85.1 229.9 %copy-start.27 = (f32[256,64]{0,1:T(8,128)}, f32[256,64]{0,1:T(8,128)S(1)}, u32[]{:S(2)}) copy-start(f32[256,64]{0,1:T(8,128)S(1)} %get-tuple-element.420) | copy-start | bytes 196612
  85.1 219.5 %copy-start.31 = (f32[1,2048]{1,0:T(1,128)}, f32[1,2048]{1,0:T(1,128)S(1)}, u32[]{:S(2)}) copy-start(f32[1,2048]{1,0:T(1,128)S(1)} %get-tuple-element.418) | copy-start | bytes 24580
  85.1 324.0 %copy-start.36 = (f32[1,2048]{1,0:T(1,128)}, f32[1,2048]{1,0:T(1,128)S(1)}, u32[]{:S(2)}) copy-start(f32[1,2048]{1,0:T(1,128)S(1)} %get-tuple-element.417) | copy-start | bytes 24580
  93.7 34.4 %copy-start.33 = (bf16[256,512]{1,0:T(8,128)(2,1)S(1)}, bf16[256,512]{1,0:T(8,128)(2,1)}, u32[]{:S(2)}) copy-start(bf16[256,512]{1,0:T(8,128)(2,1)} %copy.82) | copy-start | bytes 786436
  129.0 152.9 %all-gather.14.cloned.1.call-start = ((), (), s32[]{:S(2)}) async-start(), calls=%async_computation.13 | async-start | bytes 17301504 | tf_op jit(solution)/shard_map/all_gather | solution.py:63
  129.6 268.3 %all-gather.16.cloned.1.call-start = ((), (), s32[]{:S(2)}) async-start(), calls=%async_computation.14 | async-start | bytes 17301504 | tf_op jit(solution)/shard_map/all_gather | solution.py:66
  281.9 22.8 copy-start.41
  304.6 9.6 copy-start.56
  341.7 5.8 copy-start.17
  341.7 5.8 copy-start.20
  409.1 48.7 %copy-start.52 = (f32[256]{0:T(256)}, f32[256]{0:T(256)S(1)}, u32[]{:S(2)}) copy-start(f32[256]{0:T(256)S(1)} %get-tuple-element.427) | copy-start | bytes 3076
  409.1 48.6 %copy-start.48 = (f32[256]{0:T(256)}, f32[256]{0:T(256)S(1)}, u32[]{:S(2)}) copy-start(f32[256]{0:T(256)S(1)} %fusion.94) | copy-start | bytes 3076
  457.7 5.1 copy-start.45
  457.7 230.6 %all-to-all-start = ((bf16[32,80,2048]{2,1,0:T(8,128)(2,1)}), bf16[32,80,2048]{2,1,0:T(8,128)(2,1)}, u32[]{:S(2)}, u32[]{:S(2)}) async-start(bf16[32,80,2048]{2,1,0:T(8,128)(2,1)} %bitcast.290), calls=%async_computation | async-start | bytes 20971520 | tf_op jit(solution)/shard_map/all_to_all | solution.py:175
  688.4 233.8 %all-to-all-start.2 = ((bf16[32,80,2048]{2,1,0:T(8,128)(2,1)}), bf16[32,80,2048]{2,1,0:T(8,128)(2,1)}, u32[]{:S(2)}, u32[]{:S(2)}) async-start(bf16[32,80,2048]{2,1,0:T(8,128)(2,1)} %bitcast.291), calls=%async_computation.2 | async-start | bytes 20971520 | tf_op jit(solution)/shard_map/all_to_all | solution.py:211
  696.8 14.0 copy-start.58
  973.9 233.6 %all-to-all-start.3 = ((bf16[32,80,2048]{2,1,0:T(8,128)(2,1)}), bf16[32,80,2048]{2,1,0:T(8,128)(2,1)}, u32[]{:S(2)}, u32[]{:S(2)}) async-start(bf16[32,80,2048]{2,1,0:T(8,128)(2,1)} %bitcast.302), calls=%async_computation.3 | async-start | bytes 20971520 | tf_op jit(solution)/shard_map/all_to_all | solution.py:236
  1207.5 8.6 copy-start.18
  1207.5 8.6 copy-start.21
  1207.5 233.7 %all-to-all-start.1 = ((bf16[32,80,2048]{2,1,0:T(8,128)(2,1)}), bf16[32,80,2048]{2,1,0:T(8,128)(2,1)}, u32[]{:S(2)}, u32[]{:S(2)}) async-start(bf16[32,80,2048]{2,1,0:T(8,128)(2,1)} %bitcast.301), calls=%async_computation.1 | async-start | bytes 20971520 | tf_op jit(solution)/shard_map/all_to_all | solution.py:191
  1215.7 411.3 %reduce-scatter.10.cloned.1.call-start = ((), (), s32[]{:S(2)}) async-start(), calls=%async_computation.15 | async-start | bytes 2621440 | tf_op jit(solution)/shard_map/reduce_scatter | solution.py:304
  1462.9 15.2 copy-start.9
  1462.9 15.2 copy-start.37
  1462.9 15.2 copy-start.49
  1545.8 215.4 %reduce-scatter.20.cloned.1.call-start = ((), (), s32[]{:S(2)}) async-start(), calls=%async_computation.20 | async-start | bytes 1081344
  1550.6 5.5 copy-start.26
  1550.6 5.5 copy-start.28
  1556.1 3.5 copy-start.7
  1564.1 66.1 %copy-start.16 = (f32[256,4,128]{0,2,1:T(8,128)S(1)}, f32[256,4,128]{0,2,1:T(8,128)}, u32[]{:S(2)}) copy-start(f32[256,4,128]{0,2,1:T(8,128)} %copy-done.15) | copy-start | bytes 1572868
  1564.1 66.1 %copy-start.44 = (f32[256,4]{0,1:T(4,128)S(1)}, f32[256,4]{0,1:T(4,128)}, u32[]{:S(2)}) copy-start(f32[256,4]{0,1:T(4,128)} %copy-done.43) | copy-start | bytes 12292
  1564.1 66.1 %copy-start.55 = (f32[128]{0:T(128)S(1)}, f32[128]{0:T(128)}, u32[]{:S(2)}) copy-start(f32[128]{0:T(128)} %copy-done.54) | copy-start | bytes 1540
  1564.1 66.3 %copy-start.47 = (f32[256,4]{0,1:T(4,128)S(1)}, f32[256,4]{0,1:T(4,128)}, u32[]{:S(2)}) copy-start(f32[256,4]{0,1:T(4,128)} %copy-done.46) | copy-start | bytes 12292
  1576.4 55.3 %copy-start.13 = (bf16[2048,512]{1,0:T(8,128)(2,1)S(1)}, bf16[2048,512]{1,0:T(8,128)(2,1)}, u32[]{:S(2)}) copy-start(bf16[2048,512]{1,0:T(8,128)(2,1)} %all-gather.8.cloned.1.call-done) | copy-start | bytes 6291460
  1636.6 265.9 %reduce-scatter.14.cloned.1.call-start = ((), (), s32[]{:S(2)}) async-start(), calls=%async_computation.17 | async-start | bytes 4325376 | tf_op jit(solution)/shard_map/reduce_scatter | solution.py:334
  1639.7 405.2 %reduce-scatter.16.cloned.1.call-start = ((), (), s32[]{:S(2)}) async-start(), calls=%async_computation.18 | async-start | bytes 4325376 | tf_op jit(solution)/shard_map/reduce_scatter | solution.py:335
  1643.7 768.7 %reduce-scatter.18.cloned.1.call-start = ((), (), s32[]{:S(2)}) async-start(), calls=%async_computation.19 | async-start | bytes 34603008 | tf_op jit(solution)/shard_map/reduce_scatter | solution.py:336
  1660.1 1112.8 %reduce-scatter.12.cloned.1.call-start = ((), (), s32[]{:S(2)}) async-start(), calls=%async_computation.16 | async-start | bytes 34603008 | tf_op jit(solution)/shard_map/reduce_scatter | solution.py:333
  1674.9 14.1 copy-start.60
  1689.0 13.4 copy-start.59
  1702.4 53.7 %copy-start.51 = (f32[256]{0:T(256)S(1)}, f32[256]{0:T(256)}, u32[]{:S(2)}) copy-start(f32[256]{0:T(256)} %copy-done.50) | copy-start | bytes 3076
  1702.4 1070.5 %copy-start.1 = (bf16[1,768,2048]{2,1,0:T(8,128)(2,1)S(1)}, bf16[1,768,2048]{2,1,0:T(8,128)(2,1)}, u32[]{:S(2)}) copy-start(bf16[1,768,2048]{2,1,0:T(8,128)(2,1)} %param.30) | copy-start | bytes 9437188
  (28 other events, 52.0 us)
Sparse Core Ops, SparseCore 0:
  11.0 55.9 all-gather.7
  70.0 55.3 all-gather.9
  129.1 35.8 all-gather.11
  167.8 113.9 all-gather.13
  284.7 113.0 all-gather.15
  1545.9 81.0 reduce-scatter.9
  1636.7 124.3 reduce-scatter.19
  1764.0 138.4 reduce-scatter.13
  1905.3 139.5 reduce-scatter.15
  2047.6 364.6 reduce-scatter.17
  2415.3 357.5 reduce-scatter.11
where the time goes:
time: 2790 us; the launch traced here: 2780 us
  waiting for transfers between devices  2080 us (75%)
  matrix products  238 us (9%)
  local copies, waits for them, and re-layouts  196 us (7%)
  blocking collectives  113 us (4%)
  other arithmetic  103 us (4%)
  starting transfers between devices  30.8 us (1%)
    reduce_scatter x1, waiting for transfers between devices, body(): lax.psum_scatter(grad_wo, ('ctx', 'expert'), scatter_dimension=0, tiled=T...  367 us
    reduce_scatter x1, waiting for transfers between devices, body(): lax.psum_scatter(grad_wq, ('ctx', 'expert'), scatter_dimension=0, tiled=T...  361 us
    all_to_all x1, waiting for transfers between devices, body(): lax.all_to_all(from_experts(grad_inputs), ('ctx', 'expert'), split_axis=0...  213 us
    all_to_all x1, waiting for transfers between devices, body(): lax.all_to_all(from_experts(produced), ('ctx', 'expert'), split_axis=0, c...  203 us
    all_to_all x1, waiting for transfers between devices, body(): lax.all_to_all(to_slots(normed_mlp[owner_row]), ('ctx', 'expert'), split_...  203 us
    all_to_all x1, waiting for transfers between devices, body(): lax.all_to_all(to_slots(grad_rows), ('ctx', 'expert'), split_axis=0, conc...  198 us
    reduce_scatter x1, waiting for transfers between devices, body(): lax.psum_scatter(grad_wv, ('ctx', 'expert'), scatter_dimension=0, tiled=T...  142 us
    reduce_scatter x1, waiting for transfers between devices, body(): lax.psum_scatter(grad_wk, ('ctx', 'expert'), scatter_dimension=0, tiled=T...  140 us
  transfers between devices with their start and end apart: 15, of which 14 were waited for; matrix products, arithmetic and copies ran while one was open for 11% of the time, Pallas kernels for 0%

commit v1 on v0

--- a/solution.py
+++ b/solution.py
@@ -1,6 +1,10 @@
+import functools
+
 import jax
 import jax.numpy as jnp
 from jax import lax
+from jax.experimental import pallas as pl
+from jax.experimental.pallas import tpu as pltpu
 from jax.sharding import PartitionSpec as P
 
 HQ = 32
@@ -352,9 +356,980 @@
     )
 
 
+MESH = pl.DeviceIdType.MESH
+VMEM_BYTES = 58 * 2**20
+ANY = pl.BlockSpec(memory_space=pl.ANY)
+IN_VMEM = pl.BlockSpec(memory_space=pltpu.VMEM)
+f32, bf16 = jnp.float32, jnp.bfloat16
+
+
+class Place:
+    def __init__(self):
+        self.c = lax.axis_index("ctx")
+        self.e = lax.axis_index("expert")
+        self.k = lax.rem(self.e, 2)
+        self.z = lax.div(self.e, 2)
+        self.cx = self.c + 1 - 2 * lax.rem(self.c, 2)
+        self.cy = lax.rem(self.c + 2, 4)
+        self.cd = lax.rem(self.cx + 2, 4)
+        self.dx = (self.cx, self.e)
+        self.dy = (self.cy, self.e)
+        self.dd = (self.cd, self.e)
+        self.pair = (self.c, self.e + 1 - 2 * self.k)
+        self.up = (self.c, self.e + 2)
+        self.down = (self.c, self.e - 2)
+
+
+def greet(p, nz, line=True, pair=True, diagonal=False):
+    barrier = pltpu.get_barrier_semaphore()
+
+    def tell(device):
+        pl.semaphore_signal(barrier, inc=1, device_id=device, device_id_type=MESH)
+
+    friends = [p.dx, p.dy] + [p.pair] * pair + [p.dd] * diagonal
+    for device in friends:
+        tell(device)
+    count = len(friends)
+    if line:
+        for there, device in ((p.z > 0, p.down), (p.z < nz - 1, p.up)):
+
+            @pl.when(there)
+            def _():
+                tell(device)
+
+            count = count + there.astype(jnp.int32)
+    pl.semaphore_wait(barrier, count)
+
+
+def remote(src, dst, send, recv, device):
+    return pltpu.make_async_remote_copy(
+        src_ref=src,
+        dst_ref=dst,
+        send_sem=send,
+        recv_sem=recv,
+        device_id=device,
+        device_id_type=MESH,
+    )
+
+
+class Spread:
+    def __init__(self, p, nz, mine, block, half, send, recv, line=True, side=True, pair=True):
+        self.p, self.nz, self.mine, self.block, self.half = p, nz, mine, block, half
+        self.send, self.recv = send, recv
+        self.line, self.side, self.pair = line, side, pair
+
+    def ref(self, c, z, k, h=None):
+        whole = self.block(c, z, k)
+        return whole if h is None else whole.at[pl.ds(h * self.half, self.half)]
+
+    def copy(self, kind, z, own=False):
+        p = self.p
+        at = functools.partial(self.ref, z=z, k=p.k)
+        src, i, j, device = {
+            "x": lambda: (at(p.c), 0, 1, p.dx),
+            "y": lambda: (at(p.c), 1, 2, p.dy),
+            "up": lambda: (at(p.c), 2, 0, p.up),
+            "down": lambda: (at(p.c), 3, 0, p.down),
+            "via_y": lambda: (at(p.cx, h=0), 4, 3, p.dy),
+            "via_x": lambda: (at(p.cy, h=1), 5, 4, p.dx),
+            "pair0": lambda: (at(p.c), 6, 5, p.pair),
+            "pair1": lambda: (at(p.cx), 7, 6, p.pair),
+            "pair2": lambda: (at(p.cy), 8, 7, p.pair),
+            "pair3": lambda: (at(p.cd, h=0), 9, 8, p.pair),
+            "pair4": lambda: (at(p.cd, h=1), 10, 9, p.pair),
+        }[kind]()
+        return remote(
+            self.mine if own else src, src, self.send.at[z, i], self.recv.at[z, j], device
+        )
+
+    def got(self, j, z):
+        p = self.p
+        k = p.k if j < 5 else 1 - p.k
+        c, h = ((p.c, None), (p.cx, None), (p.cy, None), (p.cd, 0), (p.cd, 1))[j % 5]
+        ref = self.ref(c, z, k, h)
+        remote(ref, ref, self.send.at[z, 0], self.recv.at[z, j], p.pair).wait_recv()
+
+    def each(self, far, act):
+        if far == 0:
+            act(self.p.z, 0)
+            return
+        for way in (-1, 1):
+            z = self.p.z + way * far
+
+            @pl.when((z >= 0) & (z < self.nz))
+            def _():
+                act(z, way)
+
+    def onward(self, z, way, act):
+        if self.line and way >= 0:
+
+            @pl.when(self.p.z > 0)
+            def _():
+                act(self.copy("down", z, way == 0))
+
+        if self.line and way <= 0:
+
+            @pl.when(self.p.z < self.nz - 1)
+            def _():
+                act(self.copy("up", z, way == 0))
+
+    def direct(self):
+        return ["x", "y"] * self.side + ["pair0"] * self.pair
+
+    def along(self, far):
+        def act(z, way):
+            if way:
+                self.got(0, z)
+            self.onward(z, way, lambda copy: copy.start())
+            for kind in self.direct():
+                self.copy(kind, z, way == 0).start()
+
+        self.each(far, act)
+
+    def beside(self, far):
+        def act(z, way):
+            for j, kinds in ((1, ["via_y", "pair1"]), (2, ["via_x", "pair2"])):
+                self.got(j, z)
+                for kind in kinds[: 1 + self.pair]:
+                    self.copy(kind, z).start()
+
+        if self.side:
+            self.each(far, act)
+
+    def across(self, far):
+        def act(z, way):
+            for j, kind in ((3, "pair3"), (4, "pair4")):
+                self.got(j, z)
+                if self.pair:
+                    self.copy(kind, z).start()
+
+        if self.side:
+            self.each(far, act)
+
+    def step(self, far):
+        reach = self.nz if self.line else 1
+        if far < reach:
+            self.along(far)
+        if 1 <= far <= reach:
+            self.beside(far - 1)
+        if 2 <= far <= reach + 1:
+            self.across(far - 2)
+
+    def finish(self):
+        def act(z, way):
+            if self.pair:
+                for j in range(5, 10 if self.side else 6):
+                    self.got(j, z)
+            self.onward(z, way, lambda copy: copy.wait_send())
+            for kind in self.direct():
+                self.copy(kind, z, way == 0).wait_send()
+            if self.side:
+                for kind in ["via_y", "via_x"] + ["pair1", "pair2", "pair3", "pair4"] * self.pair:
+                    self.copy(kind, z).wait_send()
+
+        for far in range(self.nz if self.line else 1):
+            self.each(far, act)
+
+
+def by_device(ref, nz):
+    return lambda c, z, k: ref.at[c * (2 * nz) + z * 2 + k]
+
+
+def spread_sems(nz):
+    return [pltpu.SemaphoreType.DMA((nz, 11)), pltpu.SemaphoreType.DMA((nz, 10))]
+
+
+def first_kernel(nz, pack, wo, tok, cot, meta, packs, wos, toks, cots, metas, *sems):
+    pair_sems, (a_send, a_recv, local) = sems[:10], sems[10:]
+    p = Place()
+    greet(p, nz, diagonal=True)
+    own = [
+        pltpu.make_async_copy(src, dst, local.at[i])
+        for i, (src, dst) in enumerate(
+            (
+                (pack.at[p.c], packs.at[p.c, p.e]),
+                (wo, wos.at[p.e]),
+                (tok, toks.at[p.c]),
+                (cot, cots.at[p.c * (2 * nz) + p.e]),
+                (meta, metas.at[p.c * (2 * nz) + p.e]),
+            )
+        )
+    ]
+    for copy in own:
+        copy.start()
+    swaps = [
+        remote(pack.at[c], packs.at[p.c, p.e], a_send.at[i], a_recv.at[i], device)
+        for i, (c, device) in enumerate(((p.cx, p.dx), (p.cy, p.dy), (p.cd, p.dd)))
+    ]
+    for copy in swaps:
+        copy.start()
+    s = lambda i: (pair_sems[2 * i], pair_sems[2 * i + 1])
+    j_tok = Spread(p, nz, tok, lambda c, z, k: toks.at[c], tok.shape[0] // 2, *s(0), False, True, False)
+    j_meta = Spread(p, nz, meta, by_device(metas, nz), meta.shape[0] // 2, *s(1))
+    j_cot = Spread(p, nz, cot, by_device(cots, nz), cot.shape[0] // 2, *s(2))
+    j_wo = Spread(p, nz, wo, lambda c, z, k: wos.at[z * 2 + k], 0, *s(3), True, False, True)
+    own_pack = packs.at[:, p.e]
+    j_pack = Spread(
+        p, nz, own_pack, lambda c, z, k: packs.at[:, z * 2 + k], 0, *s(4), True, False, True
+    )
+    j_tok.step(0)
+    j_meta.step(0)
+    for i, c in enumerate((p.cx, p.cy, p.cd)):
+        ref = packs.at[c, p.e]
+        remote(ref, ref, a_send.at[i], a_recv.at[i], p.dx).wait_recv()
+    own[0].wait()
+    j_pack.step(0)
+    j_wo.step(0)
+    j_cot.step(0)
+    for far in range(1, nz + 2):
+        for job in (j_tok, j_meta, j_pack, j_wo, j_cot):
+            job.step(far)
+    for copy in own[1:]:
+        copy.wait()
+    for copy in swaps:
+        copy.wait_send()
+    for job in (j_tok, j_meta, j_pack, j_wo, j_cot):
+        job.finish()
+
+
+def gather_first(nz, pack, wo, tok, cot, meta):
+    blocks = 8 * nz
+    shape = jax.ShapeDtypeStruct
+    return pl.pallas_call(
+        functools.partial(first_kernel, nz),
+        out_shape=[
+            shape((4, 2 * nz) + pack.shape[1:], pack.dtype),
+            shape((2 * nz,) + wo.shape, wo.dtype),
+            shape((4,) + tok.shape, tok.dtype),
+            shape((blocks,) + cot.shape, cot.dtype),
+            shape((blocks,) + meta.shape, meta.dtype),
+        ],
+        in_specs=[ANY] * 5,
+        out_specs=[ANY] * 5,
+        scratch_shapes=spread_sems(nz) * 5 + [pltpu.SemaphoreType.DMA((n,)) for n in (3, 3, 5)],
+        compiler_params=pltpu.CompilerParams(collective_id=1, has_side_effects=True),
+    )(pack, wo, tok, cot, meta)
+
+
+def spread_kernel(nz, everywhere, mine, out, send, recv, local):
+    p = Place()
+    greet(p, nz, line=everywhere, pair=everywhere)
+    block = by_device(out, nz) if everywhere else (lambda c, z, k: out.at[c])
+    keep = pltpu.make_async_copy(mine, block(p.c, p.z, p.k), local)
+    keep.start()
+    job = Spread(
+        p, nz, mine, block, mine.shape[0] // 2, send, recv, everywhere, True, everywhere
+    )
+    for far in range(nz + 2 if everywhere else 3):
+        job.step(far)
+    keep.wait()
+    job.finish()
+
+
+def gather_rows(nz, everywhere, mine, collective_id):
+    blocks = 8 * nz if everywhere else 4
+    return pl.pallas_call(
+        functools.partial(spread_kernel, nz, everywhere),
+        out_shape=jax.ShapeDtypeStruct((blocks,) + mine.shape, mine.dtype),
+        in_specs=[ANY],
+        out_specs=ANY,
+        scratch_shapes=spread_sems(nz) + [pltpu.SemaphoreType.DMA],
+        compiler_params=pltpu.CompilerParams(collective_id=collective_id, has_side_effects=True),
+    )(mine)
+
+
+def far_first(nz):
+    return [sorted(range(nz), key=lambda to: (-abs(to - z), to)) for z in range(nz)]
+
+
+def pick_order(p, nz):
+    table = far_first(nz)
+    return [
+        sum(jnp.where(p.z == z, table[z][i], 0) for z in range(nz)) for i in range(nz)
+    ]
+
+
+def combine_kernel(nz, cap, rows, w, out, rbuf, sd, sx, sy, sz, h0, h1, bx, by, bz, *sems):
+    pair_send, pair_recv, load, s_h0, s_h1, s_x, s_y, s_z, r_h0, r_h1, r_x, r_y, r_z = sems
+    p = Place()
+    order = pick_order(p, nz)
+    seq = w.shape[2]
+    half = seq // 2
+    width = rbuf.shape[3]
+    tile = min(512, width)
+
+    @pl.when(p.z == 0)
+    def _():
+        bz[pl.ds(0, nz)] = jnp.zeros((nz,) + bz.shape[1:], bz.dtype)
+
+    @pl.when(p.z == nz - 1)
+    def _():
+        bz[pl.ds(0, nz - 1)] = jnp.zeros((nz - 1,) + bz.shape[1:], bz.dtype)
+        bz[nz] = jnp.zeros(bz.shape[1:], bz.dtype)
+
+    greet(p, nz)
+    rel = (p.cd, p.cx, p.cy, p.c)
+
+    def pair_copy(c, z):
+        other = c * (2 * nz) + z * 2 + 1 - p.k
+        return remote(
+            rows.at[other],
+            rbuf.at[c, z, pl.ds(cap, cap)],
+            pair_send.at[c, z],
+            pair_recv.at[c, z],
+            p.pair,
+        )
+
+    def load_copy(c, z):
+        return pltpu.make_async_copy(
+            rows.at[c * (2 * nz) + z * 2 + p.k], rbuf.at[c, z, pl.ds(0, cap)], load.at[c, z]
+        )
+
+    for z in order:
+        for c in rel:
+            load_copy(c, z).start()
+            pair_copy(c, z).start()
+
+    def ready(c, z):
+        load_copy(c, z).wait()
+        pair_copy(c, z).wait_recv()
+
+    def fill(c, z, low, high, store):
+        for first, adds in ((0, low), (half, high)):
+
+            @pl.loop(0, width // tile)
+            def _(t):
+                cols = pl.ds(pl.multiple_of(t * tile, tile), tile)
+                total = jnp.dot(
+                    w[c, z, pl.ds(first, half)],
+                    rbuf[c, z, :, cols],
+                    preferred_element_type=f32,
+                )
+                for ref, start in adds:
+                    total = total + ref[pl.ds(start, half), cols].astype(f32)
+                store(pl.ds(first, half), cols, total)
+
+    def into(buf, z):
+        def store(lines, cols, total):
+            buf[z, lines, cols] = total.astype(buf.dtype)
+
+        return store
+
+    def copy_h0(z):
+        return remote(sd.at[z, pl.ds(0, half)], h0.at[z], s_h0.at[z], r_h0.at[z], p.dx)
+
+    def copy_h1(z):
+        return remote(sd.at[z, pl.ds(half, half)], h1.at[z], s_h1.at[z], r_h1.at[z], p.dy)
+
+    def copy_x(z):
+        return remote(sx.at[z], bx.at[z], s_x.at[z], r_x.at[z], p.dx)
+
+    def copy_y(z):
+        return remote(sy.at[z], by.at[z], s_y.at[z], r_y.at[z], p.dy)
+
+    def copy_up(z):
+        return remote(sz.at[z], bz.at[z], s_z.at[z], r_z.at[z], p.up)
+
+    def copy_down(z):
+        slot = jnp.where(z == p.z - 1, nz, z)
+        return remote(sz.at[z], bz.at[slot], s_z.at[z], r_z.at[slot], p.down)
+
+    def line_recv(slot):
+        remote(bz.at[slot], bz.at[slot], s_z.at[0], r_z.at[slot], p.pair).wait_recv()
+
+    def diagonal(z):
+        ready(p.cd, z)
+        fill(p.cd, z, [], [], into(sd, z))
+        copy_h0(z).start()
+        copy_h1(z).start()
+
+    def sides(z):
+        ready(p.cx, z)
+        copy_h1(z).wait_recv()
+        fill(p.cx, z, [], [(h1.at[z], 0)], into(sx, z))
+        copy_x(z).start()
+        ready(p.cy, z)
+        copy_h0(z).wait_recv()
+        fill(p.cy, z, [(h0.at[z], 0)], [], into(sy, z))
+        copy_y(z).start()
+
+    def mine(z, last):
+        ready(p.c, z)
+        copy_x(z).wait_recv()
+        copy_y(z).wait_recv()
+        arrived = [bx.at[z], by.at[z], bz.at[z]]
+        if last:
+
+            @pl.when(p.z > 0)
+            def _():
+                line_recv(z)
+
+            @pl.when(p.z < nz - 1)
+            def _():
+                line_recv(nz)
+
+            def store(lines, cols, total):
+                out[lines, cols] = total
+
+            arrived.append(bz.at[nz])
+        else:
+
+            @pl.when(((z > p.z) & (p.z > 0)) | ((z < p.z) & (p.z < nz - 1)))
+            def _():
+                line_recv(z)
+
+            store = into(sz, z)
+        fill(
+            p.c, z, [(ref, 0) for ref in arrived], [(ref, half) for ref in arrived], store
+        )
+        if not last:
+
+            @pl.when(z > p.z)
+            def _():
+                copy_up(z).start()
+
+            @pl.when(z < p.z)
+            def _():
+                copy_down(z).start()
+
+    diagonal(order[0])
+    if nz > 1:
+        diagonal(order[1])
+    for i in range(nz):
+        sides(order[i])
+        if i + 2 < nz:
+            diagonal(order[i + 2])
+        if i > 0:
+            mine(order[i - 1], False)
+    mine(order[nz - 1], True)
+
+    for i, z in enumerate(order):
+        for c in rel:
+            pair_copy(c, z).wait_send()
+        for copy in (copy_h0(z), copy_h1(z), copy_x(z), copy_y(z)):
+            copy.wait_send()
+        if i < nz - 1:
+            copy_up(z).wait_send()
+
+
+def combine(nz, rows, w, collective_id):
+    blocks, cap, width = rows.shape
+    seq = w.shape[2]
+    dma = pltpu.SemaphoreType.DMA
+    buf = lambda n, r: pltpu.VMEM((n, r, width), bf16)
+    return pl.pallas_call(
+        functools.partial(combine_kernel, nz, cap),
+        out_shape=jax.ShapeDtypeStruct((seq, width), f32),
+        in_specs=[ANY, IN_VMEM],
+        out_specs=IN_VMEM,
+        scratch_shapes=[pltpu.VMEM((4, nz, 2 * cap, width), bf16)]
+        + [buf(nz, seq)] * 4
+        + [buf(nz, seq // 2)] * 2
+        + [buf(nz, seq)] * 2
+        + [buf(nz + 1, seq)]
+        + [dma((4, nz))] * 3
+        + [dma((nz,))] * 9
+        + [dma((nz + 1,))],
+        compiler_params=pltpu.CompilerParams(
+            collective_id=collective_id, has_side_effects=True, vmem_limit_bytes=VMEM_BYTES
+        ),
+    )(rows, w)
+
+
+def fold_kernel(parts, out, sx, sy, h0, h1, bx, by, send, recv):
+    p = Place()
+    greet(p, 1, line=False, pair=False)
+    half = out.shape[0] // 2
+    low, high = pl.ds(0, half), pl.ds(half, half)
+    to_x = remote(parts.at[p.cd, low], h0, send.at[0], recv.at[0], p.dx)
+    to_y = remote(parts.at[p.cd, high], h1, send.at[1], recv.at[1], p.dy)
+    x_low = remote(parts.at[p.cx, low], bx.at[low], send.at[2], recv.at[2], p.dx)
+    y_high = remote(parts.at[p.cy, high], by.at[high], send.at[3], recv.at[3], p.dy)
+    x_high = remote(sx, bx.at[high], send.at[4], recv.at[4], p.dx)
+    y_low = remote(sy, by.at[low], send.at[5], recv.at[5], p.dy)
+    copies = (to_x, to_y, x_low, y_high, x_high, y_low)
+    for copy in copies[:4]:
+        copy.start()
+    to_y.wait_recv()
+    sx[...] = (parts[p.cx, high].astype(f32) + h1[...].astype(f32)).astype(sx.dtype)
+    x_high.start()
+    to_x.wait_recv()
+    sy[...] = (parts[p.cy, low].astype(f32) + h0[...].astype(f32)).astype(sy.dtype)
+    y_low.start()
+    x_low.wait_recv()
+    y_low.wait_recv()
+    out[low] = parts[p.c, low].astype(f32) + bx[low].astype(f32) + by[low].astype(f32)
+    y_high.wait_recv()
+    x_high.wait_recv()
+    out[high] = parts[p.c, high].astype(f32) + bx[high].astype(f32) + by[high].astype(f32)
+    for copy in copies:
+        copy.wait_send()
+
+
+def fold(parts, collective_id):
+    _, seq, width = parts.shape
+    buf = lambda r: pltpu.VMEM((r, width), parts.dtype)
+    return pl.pallas_call(
+        fold_kernel,
+        out_shape=jax.ShapeDtypeStruct((seq, width), f32),
+        in_specs=[IN_VMEM],
+        out_specs=IN_VMEM,
+        scratch_shapes=[buf(seq // 2)] * 4
+        + [buf(seq)] * 2
+        + [pltpu.SemaphoreType.DMA((6,))] * 2,
+        compiler_params=pltpu.CompilerParams(
+            collective_id=collective_id, has_side_effects=True, vmem_limit_bytes=VMEM_BYTES
+        ),
+    )(parts)
+
+
+def last_kernel(nz, gq, go, gains, oq, ok, ov, oo, all_gains, *scratch):
+    own_q, own_o, sib_q, sib_o, s_q, s_o, b_q, b_o, swap_s, swap_r, scratch = (
+        *scratch[:10],
+        scratch[10:],
+    )
+    load, pair_s, pair_r, line_s, line_r, a_send, a_recv, g_send, g_recv, local = scratch
+    p = Place()
+    order = pick_order(p, nz)
+
+    @pl.when(p.z == 0)
+    def _():
+        for ref in (b_q, b_o):
+            ref[pl.ds(0, nz)] = jnp.zeros((nz,) + ref.shape[1:], ref.dtype)
+
+    @pl.when(p.z == nz - 1)
+    def _():
+        for ref in (b_q, b_o):
+            ref[pl.ds(0, nz - 1)] = jnp.zeros((nz - 1,) + ref.shape[1:], ref.dtype)
+            ref[nz] = jnp.zeros(ref.shape[1:], ref.dtype)
+
+    greet(p, nz, diagonal=True)
+    keep = pltpu.make_async_copy(gains, all_gains.at[p.c * (2 * nz) + p.e], local)
+    keep.start()
+    job = Spread(p, nz, gains, by_device(all_gains, nz), gains.shape[0] // 2, g_send, g_recv)
+    arrays = (
+        (0, lambda z, k: gq.at[:, z * 2 + k], own_q, sib_q, s_q, b_q),
+        (1, lambda z, k: go.at[z * 2 + k], own_o, sib_o, s_o, b_o),
+    )
+
+    def load_copy(i, z):
+        _, part, own, _, _, _ = arrays[i]
+        return pltpu.make_async_copy(part(z, p.k), own.at[z], load.at[i, z])
+
+    def pair_copy(i, z):
+        _, part, _, sib, _, _ = arrays[i]
+        return remote(part(z, 1 - p.k), sib.at[z], pair_s.at[i, z], pair_r.at[i, z], p.pair)
+
+    def copy_up(i, z):
+        _, _, _, _, s, b = arrays[i]
+        return remote(s.at[z], b.at[z], line_s.at[i, z], line_r.at[i, z], p.up)
+
+    def copy_down(i, z):
+        _, _, _, _, s, b = arrays[i]
+        slot = jnp.where(z == p.z - 1, nz, z)
+        return remote(s.at[z], b.at[slot], line_s.at[i, z], line_r.at[i, slot], p.down)
+
+    def line_recv(i, slot):
+        b = arrays[i][5]
+        remote(b.at[slot], b.at[slot], line_s.at[i, 0], line_r.at[i, slot], p.pair).wait_recv()
+
+    for z in order:
+        for i in (0, 1):
+            pair_copy(i, z).start()
+            load_copy(i, z).start()
+    for far in range(nz + 2):
+        job.step(far)
+        if far >= nz:
+            continue
+        z, last = order[far], far == nz - 1
+        for i in (0, 1):
+            _, _, own, sib, s, b = arrays[i]
+            load_copy(i, z).wait()
+            pair_copy(i, z).wait_recv()
+            if last:
+
+                @pl.when(p.z > 0)
+                def _():
+                    line_recv(i, z)
+
+                @pl.when(p.z < nz - 1)
+                def _():
+                    line_recv(i, nz)
+
+                total = own[z].astype(f32) + sib[z].astype(f32) + b[z].astype(f32)
+                total = total + b[nz].astype(f32)
+                if i:
+                    oo[...] = total
+                else:
+                    swap_s[...] = total.astype(swap_s.dtype)
+            else:
+
+                @pl.when(((z > p.z) & (p.z > 0)) | ((z < p.z) & (p.z < nz - 1)))
+                def _():
+                    line_recv(i, z)
+
+                total = own[z].astype(f32) + sib[z].astype(f32) + b[z].astype(f32)
+                s[z] = total.astype(s.dtype)
+
+                @pl.when(z > p.z)
+                def _():
+                    copy_up(i, z).start()
+
+                @pl.when(z < p.z)
+                def _():
+                    copy_down(i, z).start()
+
+            if last and i == 0:
+                swaps = [
+                    remote(
+                        swap_s.at[c], swap_r.at[p.c], a_send.at[n], a_recv.at[n], device
+                    )
+                    for n, (c, device) in enumerate(((p.cx, p.dx), (p.cy, p.dy), (p.cd, p.dd)))
+                ]
+                for copy in swaps:
+                    copy.start()
+                swap_r[p.c] = swap_s[p.c]
+    for n, c in enumerate((p.cx, p.cy, p.cd)):
+        ref = swap_r.at[c]
+        remote(ref, ref, a_send.at[n], a_recv.at[n], p.dx).wait_recv()
+    heads = oq.shape[1] // 4
+    kv = ok.shape[1] // 4
+    for c in range(4):
+        oq[:, pl.ds(c * heads, heads)] = swap_r[c, :, pl.ds(0, heads)].astype(f32)
+        ok[:, pl.ds(c * kv, kv)] = swap_r[c, :, pl.ds(heads, kv)].astype(f32)
+        ov[:, pl.ds(c * kv, kv)] = swap_r[c, :, pl.ds(heads + kv, kv)].astype(f32)
+    for copy in swaps:
+        copy.wait_send()
+    for n, z in enumerate(order):
+        for i in (0, 1):
+            pair_copy(i, z).wait_send()
+            if n < nz - 1:
+                copy_up(i, z).wait_send()
+    keep.wait()
+    job.finish()
+
+
+def reduce_last(nz, gq, go, gains):
+    _, _, rows_q, wide = gq.shape
+    _, rows_o, width = go.shape
+    kv = HD
+    heads = wide - 2 * kv
+    dma = pltpu.SemaphoreType.DMA
+    shape = jax.ShapeDtypeStruct
+    q = lambda *n: pltpu.VMEM(n + (4, rows_q, wide), bf16)
+    o = lambda *n: pltpu.VMEM(n + (rows_o, width), bf16)
+    return pl.pallas_call(
+        functools.partial(last_kernel, nz),
+        out_shape=[
+            shape((rows_q, 4 * heads), f32),
+            shape((rows_q, 4 * kv), f32),
+            shape((rows_q, 4 * kv), f32),
+            shape((rows_o, width), f32),
+            shape((8 * nz,) + gains.shape, f32),
+        ],
+        in_specs=[ANY] * 3,
+        out_specs=[IN_VMEM] * 4 + [ANY],
+        scratch_shapes=[q(nz), o(nz), q(nz), o(nz), q(nz), o(nz), q(nz + 1), o(nz + 1), q(), q()]
+        + [dma((2, nz))] * 4
+        + [dma((2, nz + 1))]
+        + [dma((3,))] * 2
+        + spread_sems(nz)
+        + [dma],
+        compiler_params=pltpu.CompilerParams(
+            collective_id=9, has_side_effects=True, vmem_limit_bytes=VMEM_BYTES
+        ),
+    )(gq, go, gains)
+
+
+def attend_kernel(scale, span, q, k, vt, ot, lse):
+    for i in range(q.shape[1] // span):
+        keys = (i + 1) * span
+        here = pl.ds(i * span, span)
+        s = lax.dot_general(
+            k[pl.ds(0, keys)], q[0, here], (((1,), (1,)), ((), ())), preferred_element_type=f32
+        )
+        s = s * scale
+        key_pos = lax.broadcasted_iota(jnp.int32, s.shape, 0)
+        query_pos = lax.broadcasted_iota(jnp.int32, s.shape, 1) + i * span
+        s = jnp.where(key_pos <= query_pos, s, masked_value)
+        largest = jnp.max(s, axis=0, keepdims=True)
+        weights = jnp.exp(s - largest)
+        total = jnp.sum(weights, axis=0, keepdims=True)
+        o = jnp.dot(vt[:, pl.ds(0, keys)], weights.astype(bf16), preferred_element_type=f32)
+        ot[0, :, here] = (o / total).astype(bf16)
+        lse[0, :, here] = largest + jnp.log(total)
+
+
+def attend(q, k, vt, scale):
+    heads, length, hd = q.shape
+    shape = jax.ShapeDtypeStruct
+    return pl.pallas_call(
+        functools.partial(attend_kernel, scale, length // 4),
+        grid=(heads,),
+        out_shape=[shape((heads, hd, length), bf16), shape((heads, 1, length), f32)],
+        in_specs=[
+            pl.BlockSpec((1, length, hd), lambda h: (h, 0, 0)),
+            pl.BlockSpec((length, hd), lambda h: (0, 0)),
+            pl.BlockSpec((hd, length), lambda h: (0, 0)),
+        ],
+        out_specs=[
+            pl.BlockSpec((1, hd, length), lambda h: (h, 0, 0)),
+            pl.BlockSpec((1, 1, length), lambda h: (h, 0, 0)),
+        ],
+        compiler_params=pltpu.CompilerParams(vmem_limit_bytes=32 * 2**20),
+    )(q, k, vt)
+
+
+def attend_back_kernel(scale, span, q, k, kt, v, do, lse, dq, dk, dv):
+    @pl.when(pl.program_id(0) == 0)
+    def _():
+        dk[...] = jnp.zeros(dk.shape, f32)
+        dv[...] = jnp.zeros(dv.shape, f32)
+
+    for i in range(q.shape[1] // span):
+        keys = pl.ds(0, (i + 1) * span)
+        here = pl.ds(i * span, span)
+        nt = (((1,), (1,)), ((), ()))
+        s = lax.dot_general(k[keys], q[0, here], nt, preferred_element_type=f32) * scale
+        key_pos = lax.broadcasted_iota(jnp.int32, s.shape, 0)
+        query_pos = lax.broadcasted_iota(jnp.int32, s.shape, 1) + i * span
+        probs = jnp.where(key_pos <= query_pos, jnp.exp(s - lse[0, :, here]), 0.0)
+        dp = lax.dot_general(v[keys], do[here], nt, preferred_element_type=f32)
+        delta = jnp.sum(probs * dp, axis=0, keepdims=True)
+        ds = (probs * (dp - delta)).astype(bf16)
+        dk[keys] += jnp.dot(ds, q[0, here], preferred_element_type=f32) * scale
+        dv[keys] += jnp.dot(probs.astype(bf16), do[here], preferred_element_type=f32)
+        part = jnp.dot(kt[:, keys], ds, preferred_element_type=f32) * scale
+        dq[here] = part.T
+
+
+def attend_back(q, k, v, do, lse, scale):
+    heads, length, hd = q.shape
+    shape = jax.ShapeDtypeStruct
+    whole = pl.BlockSpec((length, hd), lambda h: (0, 0))
+    column = pl.BlockSpec((length, hd), lambda h: (0, h))
+    return pl.pallas_call(
+        functools.partial(attend_back_kernel, scale, length // 4),
+        grid=(heads,),
+        out_shape=[
+            shape((length, heads * hd), f32),
+            shape((length, hd), f32),
+            shape((length, hd), f32),
+        ],
+        in_specs=[
+            pl.BlockSpec((1, length, hd), lambda h: (h, 0, 0)),
+            whole,
+            pl.BlockSpec((hd, length), lambda h: (0, 0)),
+            whole,
+            column,
+            pl.BlockSpec((1, 1, length), lambda h: (h, 0, 0)),
+        ],
+        out_specs=[column, whole, whole],
+        compiler_params=pltpu.CompilerParams(vmem_limit_bytes=32 * 2**20),
+    )(q, k, k.T, v, do, lse)
+
+
+def mm(a, b, contract, kind=f32):
+    return lax.dot_general(a, b, ((contract[:1], contract[1:]), ((), ())), preferred_element_type=f32).astype(kind)
+
+
+def fast_body(
+    tokens,
+    query_weight,
+    key_weight,
+    value_weight,
+    output_weight,
+    norm_gains,
+    head_gains,
+    expert_gate,
+    expert_up,
+    expert_down,
+    routes,
+    route_gates,
+    cotangent,
+):
+    seq, width = tokens.shape[1:]
+    nz = lax.axis_size("expert") // 2
+    devices = lax.axis_size(("ctx", "expert"))
+    length = 4 * seq
+    topk = routes.shape[2]
+    cap = max(2, 5 * seq * topk // (4 * devices))
+    heads = HQ // 4
+    wq = heads * HD
+    scale = HD ** (-0.5)
+    c = lax.axis_index("ctx")
+    e = lax.axis_index("expert")
+    k = lax.rem(e, 2)
+    me = c * (2 * nz) + e
+    rows_in = tokens.reshape(seq, width).astype(f32)
+    rows_q = query_weight.shape[0]
+
+    def cols(weight):
+        return weight.reshape(rows_q, 4, -1).transpose(1, 0, 2)
+
+    pack = jnp.concatenate([cols(query_weight), cols(key_weight), cols(value_weight)], axis=2)
+    share = norm_gains.shape[1]
+    head_share = head_gains.shape[1]
+    parts = [
+        routes.astype(f32).reshape(-1),
+        route_gates.reshape(-1),
+        norm_gains.astype(f32).reshape(-1),
+        head_gains.astype(f32).reshape(-1),
+    ]
+    flat = jnp.concatenate(parts)
+    lines = -(-flat.shape[0] // (128 * 16)) * 16
+    meta = jnp.pad(flat, (0, lines * 128 - flat.shape[0])).reshape(lines, 128)
+    weight, wo, toks, cots, metas = gather_first(
+        nz,
+        pack,
+        output_weight,
+        tokens.reshape(seq, width),
+        cotangent.reshape(seq, width),
+        meta,
+    )
+    weight = weight.reshape(width, -1)
+    wo = wo.reshape(-1, width)
+    metas = metas.reshape(devices, -1)
+    n = seq * topk
+    all_routes = metas[:, :n].reshape(devices, seq, topk)
+    all_gates = metas[:, n : 2 * n].reshape(devices, seq, topk)
+    at = 2 * n
+    gains = metas[:, at : at + 2 * share].reshape(devices, 2, share).transpose(1, 0, 2)
+    gains = gains.reshape(2, width)
+    at += 2 * share
+    head_gain = metas[:, at : at + 2 * head_share].reshape(devices, 2, head_share)
+    head_gain = head_gain.transpose(1, 0, 2).reshape(2, HD)
+
+    positions = jnp.arange(length, dtype=jnp.int32)
+    normed = rms_scale(toks.reshape(length, width).astype(f32), gains[0]).astype(bf16)
+    raw = mm(normed, weight, (1, 0))
+    query_raw = raw[:, :wq].reshape(length, heads, HD)
+    key_raw = raw[:, wq : wq + HD].reshape(length, 1, HD)
+    values = raw[:, wq + HD :].astype(bf16)
+
+    def head_prep(raw_heads, gain_vec):
+        return rotate(rms_scale(raw_heads, gain_vec), positions)
+
+    queries = head_prep(query_raw, head_gain[0]).astype(bf16).transpose(1, 0, 2)
+    keys = head_prep(key_raw, head_gain[1]).astype(bf16).reshape(length, HD)
+    attended, lse = attend(queries, keys, values.T, scale)
+    attended = attended.reshape(wq, length)
+    hidden = rows_in + fold(mm(attended, wo, (0, 0), bf16).reshape(4, seq, width), 2)
+    normed_mlp = rms_scale(hidden, gains[1]).astype(bf16)
+
+    all_rows = gather_rows(nz, True, normed_mlp, 3)
+
+    def picks(expert):
+        named = all_routes == expert.astype(f32)
+        member = jnp.any(named, axis=2)
+        weight_of = jnp.sum(jnp.where(named, all_gates, 0.0), axis=2)
+        upto = jnp.arange(seq)[:, None] <= jnp.arange(seq)[None, :]
+        rank = jnp.dot(member.astype(bf16), upto.astype(bf16), preferred_element_type=f32)
+        slot = jnp.where(member, rank.astype(jnp.int32) - 1, -1)
+        return slot, weight_of
+
+    slot, weight_of = picks(me)
+    slot_pair, weight_pair = picks(me + 1 - 2 * k)
+    chosen = (slot[:, None, :] == jnp.arange(cap, dtype=jnp.int32)[None, :, None])
+    row_gate = jnp.sum(jnp.where(chosen, weight_of[:, None, :], 0.0), axis=2)
+    chosen = chosen.astype(bf16)
+
+    def plane(a):
+        a = a.reshape(4, nz, 2, seq)
+        return jnp.where(k == 0, a[:, :, 0], a[:, :, 1])
+
+    slots2 = jnp.stack([plane(slot), plane(slot_pair)], axis=-1)
+    back = slots2[..., None] == jnp.arange(cap, dtype=jnp.int32)
+    gate2 = jnp.stack([plane(weight_of), plane(weight_pair)], axis=-1)
+    back_gate = jnp.where(back, gate2[..., None], 0.0).astype(bf16).reshape(4, nz, seq, 2 * cap)
+    back_one = back.astype(bf16).reshape(4, nz, seq, 2 * cap)
+
+    def pick(rows):
+        return lax.dot_general(
+            chosen, rows, (((2,), (1,)), ((0,), (0,))), preferred_element_type=f32
+        ).reshape(devices * cap, width)
+
+    gate_w, up_w, down_w = expert_gate[0], expert_up[0], expert_down[0]
+    arrived = pick(all_rows).astype(bf16)
+    grad_arrived = (row_gate.reshape(-1, 1) * pick(cots).astype(bf16).astype(f32)).astype(bf16)
+    gate_pre = mm(arrived, gate_w, (1, 0))
+    up_pre = mm(arrived, up_w, (1, 0))
+    sigmoid_gate = jax.nn.sigmoid(gate_pre)
+    swish_gate = gate_pre * sigmoid_gate
+    activated = (swish_gate * up_pre).astype(bf16)
+    produced = mm(activated, down_w, (1, 0), bf16)
+    grad_act = mm(grad_arrived, down_w, (1, 1))
+    grad_up_pre = (grad_act * swish_gate).astype(bf16)
+    grad_gate_pre = (
+        grad_act * up_pre * sigmoid_gate * (1.0 + gate_pre * (1.0 - sigmoid_gate))
+    ).astype(bf16)
+    grad_inputs = (mm(grad_gate_pre, gate_w, (1, 1)) + mm(grad_up_pre, up_w, (1, 1))).astype(bf16)
+    grad_normed_mlp = combine(nz, grad_inputs.reshape(devices, cap, width), back_one, 4)
+    mixed = hidden + combine(nz, produced.reshape(devices, cap, width), back_gate, 5)
+    grad_down = mm(activated, grad_arrived, (0, 0))
+    grad_gate = mm(arrived, grad_gate_pre, (0, 0))
+    grad_up = mm(arrived, grad_up_pre, (0, 0))
+
+    grad_out = cotangent.reshape(seq, width).astype(f32)
+    _, norm_pull = jax.vjp(rms_scale, hidden, gains[1])
+    grad_hidden_norm, grad_gain_mlp = norm_pull(grad_normed_mlp)
+    grad_hidden = grad_out + grad_hidden_norm
+    branch = gather_rows(nz, False, grad_hidden.astype(bf16), 6).reshape(length, width)
+    grad_wo = mm(attended, branch, (1, 0), bf16)
+    grad_attended = mm(branch, wo, (1, 1), bf16)
+    grad_query, grad_key, grad_value = attend_back(
+        queries, keys, values, grad_attended, lse, scale
+    )
+    _, pull_query = jax.vjp(head_prep, query_raw, head_gain[0])
+    grad_query_raw, grad_query_gain = pull_query(grad_query.reshape(length, heads, HD))
+    _, pull_key = jax.vjp(head_prep, key_raw, head_gain[1])
+    grad_key_raw, grad_key_gain = pull_key(grad_key.reshape(length, 1, HD))
+    low = jnp.concatenate(
+        [
+            grad_query_raw.reshape(length, wq).astype(bf16),
+            grad_key_raw.reshape(length, HD).astype(bf16),
+            grad_value.astype(bf16),
+        ],
+        axis=1,
+    )
+    grad_weight = mm(normed, low, (0, 0), bf16)
+    grad_normed = fold(mm(low, weight, (1, 1), bf16).reshape(4, seq, width), 7)
+    _, pull_attn = jax.vjp(rms_scale, rows_in, gains[0])
+    grad_rows_norm, grad_gain_attn = pull_attn(grad_normed)
+    grad_input = grad_hidden + grad_rows_norm
+    gain_parts = jnp.concatenate(
+        [grad_gain_attn, grad_gain_mlp, grad_query_gain, grad_key_gain]
+    ).reshape(-1, 128)
+    extra = -gain_parts.shape[0] % 16
+    gain_parts = jnp.pad(gain_parts, ((0, extra), (0, 0)))
+    sum_q, sum_k, sum_v, sum_o, all_gain_parts = reduce_last(
+        nz,
+        grad_weight.reshape(4, 2 * nz, rows_q, -1),
+        grad_wo.reshape(2 * nz, -1, width),
+        gain_parts,
+    )
+    gain_sums = jnp.sum(all_gain_parts, axis=0).reshape(-1)
+    norm_sums = gain_sums[: 2 * width].reshape(2, width)
+    head_sums = gain_sums[2 * width : 2 * width + 2 * HD].reshape(2, HD)
+    return (
+        mixed.astype(bf16).reshape(tokens.shape),
+        grad_input.astype(bf16).reshape(tokens.shape),
+        sum_q,
+        sum_k,
+        sum_v,
+        sum_o,
+        lax.dynamic_slice_in_dim(norm_sums, me * share, share, 1),
+        lax.dynamic_slice_in_dim(head_sums, me * head_share, head_share, 1),
+        grad_gate[None],
+        grad_up[None],
+        grad_down[None],
+    )
+
+
 def solution(mesh):
+    small = mesh.shape["ctx"] == HK and mesh.shape["expert"] % 2 == 0 and mesh.size <= 32
     return jax.shard_map(
-        body,
+        fast_body if small else body,
         mesh=mesh,
         in_specs=(
             P("expert", "ctx", None),

time: 2790 us -> 1310 us (0.47)
  waiting for transfers between devices: 2080 us -> 0 us
  Pallas kernels: 0 us -> 892 us
  blocking collectives: 113 us -> 0 us
  local copies, waits for them, and re-layouts: 196 us -> 96.3 us
  starting transfers between devices: 30.8 us -> 0 us
    reduce_scatter x5 -> x0, waiting for transfers between devices: 1060 us -> none  [the longest x1 367 us: body(): lax.psum_scatter(grad_wo, ('ctx', 'expert'), scatter_dimension=0, tiled=T...]
    pallas_call x0 -> x10, Pallas kernels: none -> 892 us  [the longest x2 301 us: combine(): pl.pallas_call(functools.partial(combine_kernel, nz, cap), out_shape=jax....]
    all_to_all x4 -> x0, waiting for transfers between devices: 818 us -> none  [the longest x1 213 us: body(): lax.all_to_all(from_experts(grad_inputs), ('ctx', 'expert'), split_axis=0...]
    all_gather x5 -> x0, waiting for transfers between devices: 196 us -> none  [the longest x1 113 us: body(): lax.all_gather(query_weight, ('ctx', 'expert'), axis=0, tiled=True)]
    all_gather x2 -> x0, blocking collectives: 73.6 us -> none  [the longest x1 37.1 us: body(): lax.all_gather(norm_gains, ('ctx', 'expert'), axis=1, tiled=True)]
    scatter x1 -> x0, local copies, waits for them, and re-layouts: 46.1 us -> none  [to_slots(): buffer = jnp.zeros((experts * capacity, row_block.shape[1]), row_block.dt...]
    gather x2 -> x0, local copies, waits for them, and re-layouts: 43.4 us -> none  [the longest x1 21.7 us: body(): grad_back[target].astype(jnp.float32).reshape(seq_rows, topk, width)]
    unnamed x1 -> x0, blocking collectives: 39.4 us -> none
  transfers between devices with their start and end apart: 15 -> 0, of which waited for: 14 -> 0; matrix products, arithmetic and copies ran while one was open for 11% -> 0% of each run, Pallas kernels for 0% -> 0%
where the time goes in v1:
time: 1310 us; the launch traced here: 1290 us
  Pallas kernels  892 us (68%)
  matrix products  217 us (17%)
  local copies, waits for them, and re-layouts  96.3 us (7%)
  other arithmetic  87.3 us (7%)
    pallas_call x2, Pallas kernels, combine(): pl.pallas_call(functools.partial(combine_kernel, nz, cap), out_shape=jax....  301 us
    pallas_call x2, Pallas kernels, gather_rows(): pl.pallas_call(functools.partial(spread_kernel, nz, everywhere), out_shap...  200 us
    pallas_call x1, Pallas kernels, gather_first(): pl.pallas_call(functools.partial(first_kernel, nz), out_shape=[shape((4,...  189 us
    dot_general x15, matrix products, mm(): lax.dot_general(a, b, ((contract[:1], contract[1:]), ((), ())), preferred...  169 us
    pallas_call x1, Pallas kernels, reduce_last(): pl.pallas_call(functools.partial(last_kernel, nz), out_shape=[shape((rows...  85.1 us
    pallas_call x2, Pallas kernels, fold(): pl.pallas_call(fold_kernel, out_shape=jax.ShapeDtypeStruct((seq, width),...  79.7 us
    dot_general x2, matrix products, pick(): lax.dot_general(chosen, rows, (((2,), (1,)), ((0,), (0,))), preferred_ele...  47.1 us
    unnamed x165, local copies, waits for them, and re-layouts  32.1 us

profile of v1, /device:TPU:16, one launch (start us, length us, event | category | flops | bytes accessed | tf_op | source)
XLA Modules:
  0.0 1294.3 jit_solution(12121476240716975595)
XLA Ops:
  8.4 3.0 multiply_cosine_fusion
  11.4 189.0 %shard_map.212 = (bf16[4,8,64,1280]{3,2,1,0:T(8,128)(2,1)}, bf16[8,128,2048]{2,1,0:T(8,128)(2,1)}, bf16[4,256,2048]{2,1,0:T(8,128)(2,1)}, bf16[32,256,2048]{2,1,0:T(8,128)(2,1)}, f32[32,48,128]{2,1,0:T(8,128)}) custom-call(bf16[4,64,1280]{2,1,0:T(8,128)(2,1)} %pad_maximum_fusion.3.pack, bf16[128,2048]{1,0:T(8,128)(2,1)} %wo.1, bf16[256,2048]{1,0:T(8,128)(2,1)} %bitcast.190, ...), custom_call_target="tpu_custom_call" | custom-call | tf_op jit(solution)/shard_map/pallas_call | solution.py:598
  201.8 3.4 multiply_reduce_fusion
  214.4 3.5 fusion.30
  224.7 29.0 %multiply_convert_fusion = (bf16[32,80,2048]{2,1,0:T(8,128)(2,1)}, f32[32,80,2048]{2,1,0:T(8,128)}) fusion(f32[32,80]{1,0:T(8,128)S(1)} %select_reduce_fusion, bf16[32,256,2048]{2,1,0:T(8,128)(2,1)} %get-tuple-element.31, s32[32,256]{1,0:T(8,128)S(1)} %fusion.27), kind=kOutput, calls=%fused_computation.3 | convolution fusion | flops 2705981440 | bytes 65054720 | tf_op jit(solution)/shard_map/dot_general | solution.py:1248
  255.7 4.0 copy.115
  261.3 4.8 copy.111
  266.2 4.6 fusion.66
  273.7 3.0 fusion.2
  277.9 5.6 fusion.70
  290.4 4.8 slice.113
  297.3 5.5 copy.99
  310.1 5.3 copy.100
  315.5 3.7 multiply_multiply_fusion
  321.9 14.1 %shard_map.213 = (bf16[8,128,1024]{2,1,0:T(8,128)(2,1)S(1)}, f32[8,1,1024]{2,1,0:T(1,128)S(1)}) custom-call(bf16[8,1024,128]{2,1,0:T(8,128)(2,1)S(1)} %maximum_bitcast_fusion.q, bf16[1024,128]{1,0:T(8,128)(2,1)S(1)} %copy.105.k, bf16[128,1024]{1,0:T(8,128)(2,1)S(1)} %copy-done.6), custom_call_target="tpu_custom_call" | custom-call | tf_op jit(solution)/shard_map/pallas_call | solution.py:1066
  336.0 6.1 bitcast_convert_fusion
  342.2 40.8 %shard_map.214 = f32[256,2048]{1,0:T(8,128)} custom-call(bf16[4,256,2048]{2,1,0:T(8,128)(2,1)} %bitcast.201), custom_call_target="tpu_custom_call" | custom-call | tf_op jit(solution)/shard_map/pallas_call | solution.py:872
  387.6 12.6 fusion
  400.2 160.4 %shard_map.215 = bf16[32,256,2048]{2,1,0:T(8,128)(2,1)} custom-call(bf16[256,2048]{1,0:T(8,128)(2,1)} %multiply_convert_fusion.5.mine), custom_call_target="tpu_custom_call" | custom-call | tf_op jit(solution)/shard_map/pallas_call | solution.py:631
  560.6 18.1 %convolution_convert_fusion.2 = bf16[32,80,2048]{2,1,0:T(8,128)(2,1)} fusion(bf16[32,256,2048]{2,1,0:T(8,128)(2,1)} %shard_map.215, s32[32,256]{1,0:T(8,128)S(1)} %fusion.27), kind=kOutput, calls=%fused_computation.19 | convolution fusion | flops 2690252800 | bytes 44072960 | tf_op jit(solution)/shard_map/dot_general | solution.py:1248
  578.7 14.3 %fusion.9 = f32[2560,768]{1,0:T(8,128)} fusion(bf16[2560,2048]{1,0:T(8,128)(2,1)} %bitcast.184, bf16[1,2048,768]{2,1,0:T(8,128)(2,1)} %param.21), kind=kOutput, calls=%fused_computation.45 | convolution fusion | flops 8053063680 | bytes 21495808 | tf_op jit(solution)/shard_map/dot_general | solution.py:1133
  593.0 10.6 fusion.13
  603.6 20.0 %multiply_convert_fusion.2 = (bf16[2560,768]{1,0:T(8,128)(2,1)}, bf16[2560,768]{1,0:T(8,128)(2,1)}, bf16[2560,768]{1,0:T(8,128)(2,1)}) fusion(f32[2560,768]{1,0:T(8,128)} %fusion.13, f32[2560,768]{1,0:T(8,128)} %fusion.9, bf16[2560,2048]{1,0:T(8,128)(2,1)} %bitcast.183, bf16[1,768,2048]{2,1,0:T(8,128)(2,1)S(1)} %copy-done), kind=kOutput, calls=%fused_computation.12 | convolution fusion | flops 8082554880 | bytes 41156608 | tf_op jit(solution)/shard_map/dot_general | solution.py:1133
  623.6 14.1 %convolution_bitcast_fusion = f32[1,768,2048]{2,1,0:T(8,128)} fusion(bf16[2560,768]{1,0:T(8,128)(2,1)} %get-tuple-element.61, bf16[2560,2048]{1,0:T(8,128)(2,1)} %fusion), kind=kOutput, calls=%fused_computation.36 | convolution fusion | flops 8053063680 | bytes 20709376 | tf_op jit(solution)/shard_map/dot_general | solution.py:1133
  637.7 13.4 %convolution_bitcast_fusion.1 = f32[1,2048,768]{2,1,0:T(8,128)} fusion(bf16[2560,2048]{1,0:T(8,128)(2,1)} %bitcast.185, bf16[2560,768]{1,0:T(8,128)(2,1)S(1)} %copy-done.70), kind=kOutput, calls=%fused_computation.37 | convolution fusion | flops 8053063680 | bytes 20709376 | tf_op jit(solution)/shard_map/dot_general | solution.py:1133
  651.1 11.2 convolution_bitcast_fusion.2
  662.3 10.5 convolution_convert_fusion
  672.8 150.8 %shard_map.216 = f32[256,2048]{1,0:T(8,128)} custom-call(bf16[32,80,2048]{2,1,0:T(8,128)(2,1)} %bitcast.193, bf16[4,4,256,160]{3,2,1,0:T(8,128)(2,1)} %select_convert_fusion.w), custom_call_target="tpu_custom_call" | custom-call | tf_op jit(solution)/shard_map/pallas_call | solution.py:820
  823.6 15.3 %fusion.11 = f32[2560,2048]{1,0:T(8,128)} fusion(bf16[2560,768]{1,0:T(8,128)(2,1)} %get-tuple-element.60, bf16[1,2048,768]{2,1,0:T(8,128)(2,1)} %param.20), kind=kOutput, calls=%fused_computation.47 | convolution fusion | flops 8053063680 | bytes 28049408 | tf_op jit(solution)/shard_map/dot_general | solution.py:1133
  838.9 16.6 %add_convert_fusion = bf16[2560,2048]{1,0:T(8,128)(2,1)} fusion(f32[2560,2048]{1,0:T(8,128)} %fusion.11, bf16[2560,768]{1,0:T(8,128)(2,1)} %get-tuple-element.59, bf16[1,2048,768]{2,1,0:T(8,128)(2,1)} %param.21), kind=kOutput, calls=%fused_computation.2 | convolution fusion | flops 8063549440 | bytes 38535168 | tf_op jit(solution)/shard_map/dot_general | solution.py:1133
  855.5 149.8 %shard_map.217 = f32[256,2048]{1,0:T(8,128)} custom-call(bf16[32,80,2048]{2,1,0:T(8,128)(2,1)} %bitcast.192, bf16[4,4,256,160]{3,2,1,0:T(8,128)(2,1)} %get-tuple-element.53.w), custom_call_target="tpu_custom_call" | custom-call | tf_op jit(solution)/shard_map/pallas_call | solution.py:820
  1009.6 39.2 %shard_map.218 = bf16[4,256,2048]{2,1,0:T(8,128)(2,1)} custom-call(bf16[256,2048]{1,0:T(8,128)(2,1)} %fusion.65.mine), custom_call_target="tpu_custom_call" | custom-call | tf_op jit(solution)/shard_map/pallas_call | solution.py:631
  1048.8 8.1 convolution_convert_fusion.5.do
  1057.0 6.1 convolution_convert_fusion.4
  1063.0 23.7 %shard_map.219 = (f32[1024,1024]{1,0:T(8,128)S(1)}, f32[1024,128]{1,0:T(8,128)S(1)}, f32[1024,128]{1,0:T(8,128)S(1)}) custom-call(bf16[8,1024,128]{2,1,0:T(8,128)(2,1)S(1)} %copy-done.2, bf16[1024,128]{1,0:T(8,128)(2,1)S(1)} %copy.105.k, bf16[128,1024]{1,0:T(8,128)(2,1)S(1)} %copy-done.4, bf16[1024,128]{1,0:T(8,128)(2,1)S(1)} %copy-done.5, ...), custom_call_target="tpu_custom_call" | custom-call | tf_op jit(solution)/shard_map/pallas_call | solution.py:1111
  1090.3 5.4 copy.118
  1095.7 4.9 fusion.67
  1108.1 3.8 copy.131
  1111.9 3.9 copy.132
  1115.8 5.1 multiply_add_fusion.1
  1120.9 3.6 multiply_reduce_fusion.1
  1124.6 4.8 fusion.4
  1129.4 3.9 copy.123
  1133.4 9.9 convolution_convert_fusion.3
  1143.3 7.7 convolution_convert_fusion.1
  1150.9 38.9 %shard_map.220 = f32[256,2048]{1,0:T(8,128)} custom-call(bf16[4,256,2048]{2,1,0:T(8,128)(2,1)} %bitcast.200), custom_call_target="tpu_custom_call" | custom-call | tf_op jit(solution)/shard_map/pallas_call | solution.py:872
  1192.6 5.3 fusion.29
  1198.6 85.1 %shard_map.221 = (f32[64,4096]{1,0:T(8,128)}, f32[64,512]{1,0:T(8,128)}, f32[64,512]{1,0:T(8,128)}, f32[128,2048]{1,0:T(8,128)}, f32[32,48,128]{2,1,0:T(8,128)}) custom-call(bf16[4,8,64,1280]{3,2,1,0:T(8,128)(2,1)} %bitcast.197, bf16[8,128,2048]{2,1,0:T(8,128)(2,1)} %bitcast.203, f32[48,128]{1,0:T(8,128)} %pad.25.gains), custom_call_target="tpu_custom_call" | custom-call | tf_op jit(solution)/shard_map/pallas_call | solution.py:1021
  (255 shorter events, 85.0 us)
Async XLA Ops:
  0.6 602.9 %copy-start = (bf16[1,768,2048]{2,1,0:T(8,128)(2,1)S(1)}, bf16[1,768,2048]{2,1,0:T(8,128)(2,1)}, u32[]{:S(2)}) copy-start(bf16[1,768,2048]{2,1,0:T(8,128)(2,1)} %param.22) | copy-start | bytes 9437188
  0.7 201.1 %copy-start.62 = (f32[64]{0:T(128)}, f32[64]{0:T(128)S(1)}, u32[]{:S(2)}) copy-start(f32[64]{0:T(128)S(1)} %multiply_power_fusion) | copy-start | bytes 772
  3.0 198.8 %copy-start.40 = (f32[1024]{0:T(1024)}, f32[1024]{0:T(1024)S(1)}, u32[]{:S(2)}) copy-start(f32[1024]{0:T(1024)S(1)} %iota_convert_fusion) | copy-start | bytes 12292
  210.7 175.0 %copy-start.36 = (f32[2048]{0:T(1024)}, f32[2048]{0:T(1024)S(1)}, u32[]{:S(2)}) copy-start(f32[2048]{0:T(1024)S(1)} %mul.593) | copy-start | bytes 24580
  210.8 65.9 %copy-start.38 = (f32[2048]{0:T(1024)}, f32[2048]{0:T(1024)S(1)}, u32[]{:S(2)}) copy-start(f32[2048]{0:T(1024)S(1)} %mul.557) | copy-start | bytes 24580
  224.7 29.8 %copy-start.45 = (bf16[4,4,256,2]{2,3,1,0:T(2,128)(2,1)S(1)}, bf16[4,4,256,2]{2,3,1,0:T(2,128)(2,1)}, u32[]{:S(2)}) copy-start(bf16[4,4,256,2]{2,3,1,0:T(2,128)(2,1)} %pad_maximum_fusion.5) | copy-start | bytes 49156
  259.6 6.5 copy-start.65
  304.0 11.5 copy-start.47
  304.0 11.5 copy-start.43
  306.8 8.7 copy-start.31
  310.1 5.4 copy-start.60
  320.7 15.3 %copy-start.66 = (bf16[8,128,2048]{2,1,0:T(8,128)(2,1)S(1)}, bf16[8,128,2048]{2,1,0:T(8,128)(2,1)}, u32[]{:S(2)}) copy-start(bf16[8,128,2048]{2,1,0:T(8,128)(2,1)} %get-tuple-element.30) | copy-start | bytes 12582916
  321.9 20.3 %copy-start.1 = (bf16[8,1024,128]{2,1,0:T(8,128)(2,1)}, bf16[8,1024,128]{2,1,0:T(8,128)(2,1)S(1)}, u32[]{:S(2)}) copy-start(bf16[8,1024,128]{2,1,0:T(8,128)(2,1)S(1)} %maximum_bitcast_fusion.q) | copy-start | bytes 6291460
  336.0 6.1 copy-start.10
  342.2 40.8 %copy-start.20 = (bf16[1,256,2048]{2,1,0:T(8,128)(2,1)S(1)}, bf16[1,256,2048]{2,1,0:T(8,128)(2,1)}, u32[]{:S(2)}) copy-start(bf16[1,256,2048]{2,1,0:T(8,128)(2,1)} %param.13) | copy-start | bytes 3145732
  385.1 15.1 %copy-start.54 = (f32[256]{0:T(256)}, f32[256]{0:T(256)S(1)}, u32[]{:S(2)}) copy-start(f32[256]{0:T(256)S(1)} %get-tuple-element.70) | copy-start | bytes 3076
  385.1 15.1 %copy-start.56 = (f32[256]{0:T(256)}, f32[256]{0:T(256)S(1)}, u32[]{:S(2)}) copy-start(f32[256]{0:T(256)S(1)} %get-tuple-element.57) | copy-start | bytes 3076
  385.1 15.0 %copy-start.49 = (f32[256]{0:T(256)}, f32[256]{0:T(256)S(1)}, u32[]{:S(2)}) copy-start(f32[256]{0:T(256)S(1)} %fusion.59) | copy-start | bytes 3076
  578.7 14.3 %copy-start.19 = (bf16[32,80,2048]{2,1,0:T(8,128)(2,1)S(1)}, bf16[32,80,2048]{2,1,0:T(8,128)(2,1)}, u32[]{:S(2)}) copy-start(bf16[32,80,2048]{2,1,0:T(8,128)(2,1)} %convolution_convert_fusion.2) | copy-start | bytes 31457284
  578.7 14.3 %copy-start.67 = (bf16[1,2048,768]{2,1,0:T(8,128)(2,1)S(1)}, bf16[1,2048,768]{2,1,0:T(8,128)(2,1)}, u32[]{:S(2)}) copy-start(bf16[1,2048,768]{2,1,0:T(8,128)(2,1)} %param.20) | copy-start | bytes 9437188
  623.6 14.1 %copy-start.70 = (bf16[2560,768]{1,0:T(8,128)(2,1)S(1)}, bf16[2560,768]{1,0:T(8,128)(2,1)}, u32[]{:S(2)}) copy-start(bf16[2560,768]{1,0:T(8,128)(2,1)} %get-tuple-element.59) | copy-start | bytes 11796484
  623.6 27.5 %slice-start = ((s8[10485760]{0:T(1024)(128)(4,1)}), s8[4194304]{0:T(1024)(128)(4,1)S(1)}, s32[]{:S(2)}) async-start(s8[10485760]{0:T(1024)(128)(4,1)} %bitcast.187), calls=%async_computation | async-start | bytes 8388608
  623.6 27.5 %slice-start.1 = ((s8[10485760]{0:T(1024)(128)(4,1)}), s8[4194304]{0:T(1024)(128)(4,1)S(1)}, s32[]{:S(2)}) async-start(s8[10485760]{0:T(1024)(128)(4,1)} %bitcast.187), calls=%async_computation.1 | async-start | bytes 8388608
  637.7 13.4 %slice-start.2 = ((s8[10485760]{0:T(1024)(128)(4,1)}), s8[2097152]{0:T(1024)(128)(4,1)S(1)}, s32[]{:S(2)}) async-start(s8[10485760]{0:T(1024)(128)(4,1)} %bitcast.187), calls=%async_computation.2 | async-start | bytes 4194304
  637.7 13.4 %copy-start.69 = (bf16[2560,768]{1,0:T(8,128)(2,1)S(1)}, bf16[2560,768]{1,0:T(8,128)(2,1)}, u32[]{:S(2)}) copy-start(bf16[2560,768]{1,0:T(8,128)(2,1)} %get-tuple-element.60) | copy-start | bytes 11796484
  651.1 11.2 copy-start.68
  855.5 149.8 %copy-start.14 = (f32[256,2048]{1,0:T(8,128)S(1)}, f32[256,2048]{1,0:T(8,128)}, u32[]{:S(2)}) copy-start(f32[256,2048]{1,0:T(8,128)} %copy-done.13) | copy-start | bytes 6291460
  855.5 149.8 %copy-start.37 = (f32[2048]{0:T(1024)S(1)}, f32[2048]{0:T(1024)}, u32[]{:S(2)}) copy-start(f32[2048]{0:T(1024)} %copy-done.36) | copy-start | bytes 24580
  855.5 149.8 %copy-start.50 = (f32[256]{0:T(256)S(1)}, f32[256]{0:T(256)}, u32[]{:S(2)}) copy-start(f32[256]{0:T(256)} %copy-done.49) | copy-start | bytes 3076
  1048.8 8.2 copy-start.11
  1048.8 8.2 copy-start.27
  1056.9 6.1 copy-start.2
  1056.9 6.1 copy-start.4
  1057.0 6.1 copy-start.5
  1095.7 7.8 copy-start.42
  1095.7 7.8 copy-start.64
  1095.7 10.0 copy-start.44
  1095.7 10.0 copy-start.59
  1100.6 6.3 copy-start.48
  1115.8 5.1 copy-start.32
  1115.8 5.1 copy-start.61
  1133.3 9.9 copy-start.28
  1133.3 9.9 copy-start.30
  1133.3 9.9 copy-start.35
  1150.9 38.9 %copy-start.39 = (f32[2048]{0:T(1024)S(1)}, f32[2048]{0:T(1024)}, u32[]{:S(2)}) copy-start(f32[2048]{0:T(1024)} %copy-done.38) | copy-start | bytes 24580
  1150.9 38.9 %copy-start.53 = (f32[256]{0:T(256)S(1)}, f32[256]{0:T(256)}, u32[]{:S(2)}) copy-start(f32[256]{0:T(256)} %fusion.60) | copy-start | bytes 3076
  1150.9 41.6 %copy-start.55 = (f32[256]{0:T(256)S(1)}, f32[256]{0:T(256)}, u32[]{:S(2)}) copy-start(f32[256]{0:T(256)} %copy-done.54) | copy-start | bytes 3076
  1150.9 41.7 %copy-start.15 = (f32[256,2048]{1,0:T(8,128)S(1)}, f32[256,2048]{1,0:T(8,128)}, u32[]{:S(2)}) copy-start(f32[256,2048]{1,0:T(8,128)} %copy-done.13) | copy-start | bytes 6291460
  (28 other events, 85.8 us)

commit v2 on v1

--- a/solution.py
+++ b/solution.py
@@ -412,11 +412,25 @@
     )
 
 
+def far_first(nz, z):
+    return sorted(range(nz), key=lambda to: (-abs(to - z), to))
+
+
+def near_first(nz, z):
+    return sorted(range(nz), key=lambda to: (abs(to - z), to))
+
+
+def pick_order(p, nz, order=far_first):
+    tables = [order(nz, z) for z in range(nz)]
+    return [sum(jnp.where(p.z == z, tables[z][i], 0) for z in range(nz)) for i in range(nz)]
+
+
 class Spread:
     def __init__(self, p, nz, mine, block, half, send, recv, line=True, side=True, pair=True):
         self.p, self.nz, self.mine, self.block, self.half = p, nz, mine, block, half
         self.send, self.recv = send, recv
         self.line, self.side, self.pair = line, side, pair
+        self.order = pick_order(p, nz, near_first) if line else [p.z]
 
     def ref(self, c, z, k, h=None):
         whole = self.block(c, z, k)
@@ -486,40 +500,36 @@
 
         self.each(far, act)
 
-    def beside(self, far):
+    def beside(self, z):
+        for j, kinds in ((1, ["via_y", "pair1"]), (2, ["via_x", "pair2"])):
+            self.got(j, z)
+            for kind in kinds[: 1 + self.pair]:
+                self.copy(kind, z).start()
+
+    def across(self, z):
+        for j, kind in ((3, "pair3"), (4, "pair4")):
+            self.got(j, z)
+            if self.pair:
+                self.copy(kind, z).start()
+
+    def from_pair(self, z):
+        if self.pair:
+            for j in range(5, 10 if self.side else 6):
+                self.got(j, z)
+
+    def step(self, i):
+        reach = self.nz if self.line else 1
+        if i < reach:
+            self.along(i)
+        if self.side and 1 <= i <= reach:
+            self.beside(self.order[i - 1])
+        if self.side and 2 <= i <= reach + 1:
+            self.across(self.order[i - 2])
+
+    def finish(self, pair=True):
         def act(z, way):
-            for j, kinds in ((1, ["via_y", "pair1"]), (2, ["via_x", "pair2"])):
-                self.got(j, z)
-                for kind in kinds[: 1 + self.pair]:
-                    self.copy(kind, z).start()
-
-        if self.side:
-            self.each(far, act)
-
-    def across(self, far):
-        def act(z, way):
-            for j, kind in ((3, "pair3"), (4, "pair4")):
-                self.got(j, z)
-                if self.pair:
-                    self.copy(kind, z).start()
-
-        if self.side:
-            self.each(far, act)
-
-    def step(self, far):
-        reach = self.nz if self.line else 1
-        if far < reach:
-            self.along(far)
-        if 1 <= far <= reach:
-            self.beside(far - 1)
-        if 2 <= far <= reach + 1:
-            self.across(far - 2)
-
-    def finish(self):
-        def act(z, way):
-            if self.pair:
-                for j in range(5, 10 if self.side else 6):
-                    self.got(j, z)
+            if pair:
+                self.from_pair(z)
             self.onward(z, way, lambda copy: copy.wait_send())
             for kind in self.direct():
                 self.copy(kind, z, way == 0).wait_send()
@@ -638,24 +648,14 @@
     )(mine)
 
 
-def far_first(nz):
-    return [sorted(range(nz), key=lambda to: (-abs(to - z), to)) for z in range(nz)]
-
-
-def pick_order(p, nz):
-    table = far_first(nz)
-    return [
-        sum(jnp.where(p.z == z, table[z][i], 0) for z in range(nz)) for i in range(nz)
-    ]
-
-
-def combine_kernel(nz, cap, rows, w, out, rbuf, sd, sx, sy, sz, h0, h1, bx, by, bz, *sems):
+def combine_kernel(nz, cap, rows, slots, gates, out, rbuf, w, sd, sx, sy, sz, h0, h1, bx, by, bz, *sems):
     pair_send, pair_recv, load, s_h0, s_h1, s_x, s_y, s_z, r_h0, r_h1, r_x, r_y, r_z = sems
     p = Place()
     order = pick_order(p, nz)
     seq = w.shape[2]
     half = seq // 2
     width = rbuf.shape[3]
+    names = lax.broadcasted_iota(jnp.int32, (cap, seq), 0)
     tile = min(512, width)
 
     @pl.when(p.z == 0)
@@ -691,23 +691,21 @@
             pair_copy(c, z).start()
 
     def ready(c, z):
+        b = c * (2 * nz) + z * 2 + p.k
+        both = [jnp.where(names == slots[n, b], gates[n, b], 0.0) for n in (0, 1)]
+        w[c, z] = jnp.concatenate(both, axis=0).T.astype(bf16)
         load_copy(c, z).wait()
         pair_copy(c, z).wait_recv()
 
     def fill(c, z, low, high, store):
-        for first, adds in ((0, low), (half, high)):
-
-            @pl.loop(0, width // tile)
-            def _(t):
-                cols = pl.ds(pl.multiple_of(t * tile, tile), tile)
-                total = jnp.dot(
-                    w[c, z, pl.ds(first, half)],
-                    rbuf[c, z, :, cols],
-                    preferred_element_type=f32,
-                )
+        for t in range(width // tile):
+            cols = pl.ds(t * tile, tile)
+            total = jnp.dot(w[c, z], rbuf[c, z, :, cols], preferred_element_type=f32)
+            for first, adds in ((0, low), (half, high)):
+                part = total[first : first + half]
                 for ref, start in adds:
-                    total = total + ref[pl.ds(start, half), cols].astype(f32)
-                store(pl.ds(first, half), cols, total)
+                    part = part + ref[pl.ds(start, half), cols].astype(f32)
+                store(pl.ds(first, half), cols, part)
 
     def into(buf, z):
         def store(lines, cols, total):
@@ -812,17 +810,20 @@
             copy_up(z).wait_send()
 
 
-def combine(nz, rows, w, collective_id):
+def combine(nz, rows, slots, gates, collective_id):
     blocks, cap, width = rows.shape
-    seq = w.shape[2]
+    seq = slots.shape[3]
     dma = pltpu.SemaphoreType.DMA
     buf = lambda n, r: pltpu.VMEM((n, r, width), bf16)
     return pl.pallas_call(
         functools.partial(combine_kernel, nz, cap),
         out_shape=jax.ShapeDtypeStruct((seq, width), f32),
-        in_specs=[ANY, IN_VMEM],
+        in_specs=[ANY, IN_VMEM, IN_VMEM],
         out_specs=IN_VMEM,
-        scratch_shapes=[pltpu.VMEM((4, nz, 2 * cap, width), bf16)]
+        scratch_shapes=[
+            pltpu.VMEM((4, nz, 2 * cap, width), bf16),
+            pltpu.VMEM((4, nz, seq, 2 * cap), bf16),
+        ]
         + [buf(nz, seq)] * 4
         + [buf(nz, seq // 2)] * 2
         + [buf(nz, seq)] * 2
@@ -833,7 +834,7 @@
         compiler_params=pltpu.CompilerParams(
             collective_id=collective_id, has_side_effects=True, vmem_limit_bytes=VMEM_BYTES
         ),
-    )(rows, w)
+    )(rows, slots, gates)
 
 
 def fold_kernel(parts, out, sx, sy, h0, h1, bx, by, send, recv):
@@ -1129,6 +1130,186 @@
     )(q, k, k.T, v, do, lse)
 
 
+NT = (((1,), (1,)), ((), ()))
+TN = (((0,), (0,)), ((), ()))
+
+
+def experts_kernel(
+    nz,
+    cap,
+    mine,
+    cots,
+    slots,
+    gates,
+    wg,
+    wu,
+    wd,
+    all_rows,
+    produced,
+    grad_inputs,
+    x_out,
+    dr_out,
+    a_out,
+    dg_out,
+    du_out,
+    stage_x,
+    stage_d,
+    x,
+    dr,
+    r,
+    dx,
+    a,
+    dg,
+    du,
+    send,
+    recv,
+    local,
+    load,
+    out_sem,
+    back_sem,
+):
+    p = Place()
+    greet(p, nz)
+    job = Spread(p, nz, mine, by_device(all_rows, nz), mine.shape[0] // 2, send, recv)
+    keep = pltpu.make_async_copy(mine, job.block(p.c, p.z, p.k), local)
+    keep.start()
+    seq, width = mine.shape
+    ff = a.shape[2]
+    wide = min(512, width)
+    narrow = min(256, ff)
+    lines = [(p.c, 0), (p.cx, 0), (p.c, 1), (p.cx, 1)], [(p.cy, 0), (p.cd, 0), (p.cy, 1), (p.cd, 1)]
+    turns = [(i - j, j) for i in range(1, nz + 2) for j in (1, 2) if 0 <= i - j < nz]
+    turns = [(i, j - 1) for i, j in turns]
+
+    def index(h, i, z):
+        c, other = lines[h][i]
+        return c * (2 * nz) + z * 2 + lax.rem(p.k + other, 2)
+
+    def load_x(h, i, z):
+        return pltpu.make_async_copy(all_rows.at[index(h, i, z)], stage_x.at[i], load.at[0, i])
+
+    def load_d(n, i):
+        at, h = turns[n]
+        src = cots.at[index(h, i, job.order[at])]
+        return pltpu.make_async_copy(src, stage_d.at[n % 2, i], load.at[1 + n % 2, i])
+
+    def outs(h, z):
+        whole = ((x, x_out), (dr, dr_out), (a, a_out), (dg, dg_out), (du, du_out))
+        found = [
+            pltpu.make_async_copy(src.at[h], dst.at[z, h], out_sem.at[h, n])
+            for n, (src, dst) in enumerate(whole)
+        ]
+        for n, (src, dst) in enumerate(((r, produced), (dx, grad_inputs))):
+            for i in range(4):
+                found.append(
+                    pltpu.make_async_copy(
+                        src.at[h, pl.ds(i * cap, cap)], dst.at[index(h, i, z)], back_sem.at[h, n, i]
+                    )
+                )
+        return found
+
+    def group(n):
+        at, h = turns[n]
+        z = job.order[at]
+        for i in range(4):
+            load_x(h, i, z).start()
+        if n + 1 < len(turns):
+            for i in range(4):
+                load_d(n + 1, i).start()
+        if at:
+            for copy in outs(h, job.order[at - 1]):
+                copy.wait()
+        for i in range(4):
+            names = lax.broadcasted_iota(jnp.int32, (cap, seq), 0) == slots[index(h, i, z)]
+            chosen = names.astype(f32).astype(bf16)
+            row_gate = jnp.where(names, gates[index(h, i, z)], 0.0)
+            row_gate = jnp.sum(row_gate, axis=1, keepdims=True)
+            here = pl.ds(i * cap, cap)
+            load_d(n, i).wait()
+            picked = jnp.dot(chosen, stage_d[n % 2, i], preferred_element_type=f32)
+            dr[h, here] = (row_gate * picked).astype(bf16)
+            load_x(h, i, z).wait()
+            picked = jnp.dot(chosen, stage_x[i], preferred_element_type=f32)
+            x[h, here] = picked.astype(bf16)
+
+        @pl.loop(0, ff // narrow)
+        def _(t):
+            cols = pl.ds(pl.multiple_of(t * narrow, narrow), narrow)
+            g = jnp.dot(x[h], wg[:, cols], preferred_element_type=f32)
+            u = jnp.dot(x[h], wu[:, cols], preferred_element_type=f32)
+            da = lax.dot_general(dr[h], wd[cols, :], NT, preferred_element_type=f32)
+            s = jax.nn.sigmoid(g)
+            swish = g * s
+            a[h, :, cols] = (swish * u).astype(bf16)
+            du[h, :, cols] = (da * swish).astype(bf16)
+            dg[h, :, cols] = (da * u * s * (1.0 + g * (1.0 - s))).astype(bf16)
+
+        @pl.loop(0, width // wide)
+        def _(t):
+            cols = pl.ds(pl.multiple_of(t * wide, wide), wide)
+            r[h, :, cols] = jnp.dot(a[h], wd[:, cols], preferred_element_type=f32).astype(bf16)
+            back = lax.dot_general(dg[h], wg[cols, :], NT, preferred_element_type=f32)
+            back = back + lax.dot_general(du[h], wu[cols, :], NT, preferred_element_type=f32)
+            dx[h, :, cols] = back.astype(bf16)
+
+        for copy in outs(h, z):
+            copy.start()
+
+    for i in range(4):
+        load_d(0, i).start()
+    done = 0
+    for i in range(nz + 2):
+        if i < nz:
+            job.along(i)
+        if 1 <= i <= nz:
+            z = job.order[i - 1]
+            job.beside(z)
+            for j in (5, 6):
+                job.got(j, z)
+            if i == 1:
+                keep.wait()
+            group(done)
+            done += 1
+        if i >= 2:
+            z = job.order[i - 2]
+            job.across(z)
+            for j in (7, 8, 9):
+                job.got(j, z)
+            group(done)
+            done += 1
+    for h in (0, 1):
+        for copy in outs(h, job.order[nz - 1]):
+            copy.wait()
+    job.finish(pair=False)
+
+
+def run_experts(nz, cap, mine, cots, slots, gates, wg, wu, wd):
+    seq, width = mine.shape
+    ff = wg.shape[1]
+    rows = 4 * cap
+    blocks = 8 * nz
+    shape = lambda *n: jax.ShapeDtypeStruct(n, bf16)
+    vmem = lambda *n: pltpu.VMEM(n, bf16)
+    dma = pltpu.SemaphoreType.DMA
+    return pl.pallas_call(
+        functools.partial(experts_kernel, nz, cap),
+        out_shape=[shape(blocks, seq, width)]
+        + [shape(blocks, cap, width)] * 2
+        + [shape(nz, 2, rows, width)] * 2
+        + [shape(nz, 2, rows, ff)] * 3,
+        in_specs=[ANY] * 2 + [IN_VMEM] * 5,
+        out_specs=[ANY] * 8,
+        scratch_shapes=[vmem(4, seq, width), vmem(2, 4, seq, width)]
+        + [vmem(2, rows, width)] * 4
+        + [vmem(2, rows, ff)] * 3
+        + spread_sems(nz)
+        + [dma, dma((3, 4)), dma((2, 5)), dma((2, 2, 4))],
+        compiler_params=pltpu.CompilerParams(
+            collective_id=3, has_side_effects=True, vmem_limit_bytes=VMEM_BYTES
+        ),
+    )(mine, cots, slots, gates, wg, wu, wd)[1:]
+
+
 def mm(a, b, contract, kind=f32):
     return lax.dot_general(a, b, ((contract[:1], contract[1:]), ((), ())), preferred_element_type=f32).astype(kind)
 
@@ -1171,8 +1352,8 @@
     share = norm_gains.shape[1]
     head_share = head_gains.shape[1]
     parts = [
-        routes.astype(f32).reshape(-1),
-        route_gates.reshape(-1),
+        routes.reshape(seq, topk).T.astype(f32).reshape(-1),
+        route_gates.reshape(seq, topk).T.reshape(-1),
         norm_gains.astype(f32).reshape(-1),
         head_gains.astype(f32).reshape(-1),
     ]
@@ -1191,8 +1372,8 @@
     wo = wo.reshape(-1, width)
     metas = metas.reshape(devices, -1)
     n = seq * topk
-    all_routes = metas[:, :n].reshape(devices, seq, topk)
-    all_gates = metas[:, n : 2 * n].reshape(devices, seq, topk)
+    all_routes = metas[:, :n].reshape(devices, topk, seq)
+    all_gates = metas[:, n : 2 * n].reshape(devices, topk, seq)
     at = 2 * n
     gains = metas[:, at : at + 2 * share].reshape(devices, 2, share).transpose(1, 0, 2)
     gains = gains.reshape(2, width)
@@ -1217,55 +1398,28 @@
     hidden = rows_in + fold(mm(attended, wo, (0, 0), bf16).reshape(4, seq, width), 2)
     normed_mlp = rms_scale(hidden, gains[1]).astype(bf16)
 
-    all_rows = gather_rows(nz, True, normed_mlp, 3)
-
     def picks(expert):
         named = all_routes == expert.astype(f32)
-        member = jnp.any(named, axis=2)
-        weight_of = jnp.sum(jnp.where(named, all_gates, 0.0), axis=2)
+        member = jnp.any(named, axis=1)
+        weight_of = jnp.sum(jnp.where(named, all_gates, 0.0), axis=1)
         upto = jnp.arange(seq)[:, None] <= jnp.arange(seq)[None, :]
         rank = jnp.dot(member.astype(bf16), upto.astype(bf16), preferred_element_type=f32)
         slot = jnp.where(member, rank.astype(jnp.int32) - 1, -1)
-        return slot, weight_of
+        return slot.reshape(devices, 1, seq), weight_of.reshape(devices, 1, seq)
 
     slot, weight_of = picks(me)
     slot_pair, weight_pair = picks(me + 1 - 2 * k)
-    chosen = (slot[:, None, :] == jnp.arange(cap, dtype=jnp.int32)[None, :, None])
-    row_gate = jnp.sum(jnp.where(chosen, weight_of[:, None, :], 0.0), axis=2)
-    chosen = chosen.astype(bf16)
-
-    def plane(a):
-        a = a.reshape(4, nz, 2, seq)
-        return jnp.where(k == 0, a[:, :, 0], a[:, :, 1])
-
-    slots2 = jnp.stack([plane(slot), plane(slot_pair)], axis=-1)
-    back = slots2[..., None] == jnp.arange(cap, dtype=jnp.int32)
-    gate2 = jnp.stack([plane(weight_of), plane(weight_pair)], axis=-1)
-    back_gate = jnp.where(back, gate2[..., None], 0.0).astype(bf16).reshape(4, nz, seq, 2 * cap)
-    back_one = back.astype(bf16).reshape(4, nz, seq, 2 * cap)
-
-    def pick(rows):
-        return lax.dot_general(
-            chosen, rows, (((2,), (1,)), ((0,), (0,))), preferred_element_type=f32
-        ).reshape(devices * cap, width)
-
-    gate_w, up_w, down_w = expert_gate[0], expert_up[0], expert_down[0]
-    arrived = pick(all_rows).astype(bf16)
-    grad_arrived = (row_gate.reshape(-1, 1) * pick(cots).astype(bf16).astype(f32)).astype(bf16)
-    gate_pre = mm(arrived, gate_w, (1, 0))
-    up_pre = mm(arrived, up_w, (1, 0))
-    sigmoid_gate = jax.nn.sigmoid(gate_pre)
-    swish_gate = gate_pre * sigmoid_gate
-    activated = (swish_gate * up_pre).astype(bf16)
-    produced = mm(activated, down_w, (1, 0), bf16)
-    grad_act = mm(grad_arrived, down_w, (1, 1))
-    grad_up_pre = (grad_act * swish_gate).astype(bf16)
-    grad_gate_pre = (
-        grad_act * up_pre * sigmoid_gate * (1.0 + gate_pre * (1.0 - sigmoid_gate))
-    ).astype(bf16)
-    grad_inputs = (mm(grad_gate_pre, gate_w, (1, 1)) + mm(grad_up_pre, up_w, (1, 1))).astype(bf16)
-    grad_normed_mlp = combine(nz, grad_inputs.reshape(devices, cap, width), back_one, 4)
-    mixed = hidden + combine(nz, produced.reshape(devices, cap, width), back_gate, 5)
+    slots2 = jnp.stack([slot, slot_pair])
+    gates2 = jnp.stack([weight_of, weight_pair])
+    produced, grad_inputs, arrived, grad_arrived, activated, grad_gate_pre, grad_up_pre = run_experts(
+        nz, cap, normed_mlp, cots, slot, weight_of, expert_gate[0], expert_up[0], expert_down[0]
+    )
+    grad_normed_mlp = combine(nz, grad_inputs, slots2, jnp.ones_like(gates2), 4)
+    mixed = hidden + combine(nz, produced, slots2, gates2, 5)
+    arrived, grad_arrived, activated, grad_gate_pre, grad_up_pre = (
+        a.reshape(devices * cap, -1)
+        for a in (arrived, grad_arrived, activated, grad_gate_pre, grad_up_pre)
+    )
     grad_down = mm(activated, grad_arrived, (0, 0))
     grad_gate = mm(arrived, grad_gate_pre, (0, 0))
     grad_up = mm(arrived, grad_up_pre, (0, 0))

time: 1310 us -> 1150 us (0.88)
  matrix products: 217 us -> 93.1 us
  local copies, waits for them, and re-layouts: 96.3 us -> 58.4 us
  Pallas kernels: 892 us -> 925 us
  other arithmetic: 87.3 us -> 56.1 us
    pallas_call x0 -> x1, Pallas kernels: none -> 198 us  [run_experts(): pl.pallas_call(functools.partial(experts_kernel, nz, cap), out_shape=[sha...]
    pallas_call x2 -> x1, Pallas kernels: 200 us -> 38.4 us  [gather_rows(): pl.pallas_call(functools.partial(spread_kernel, nz, everywhere), out_shap...]
    dot_general x15 -> x9, matrix products: 169 us -> 92.8 us  [mm(): lax.dot_general(a, b, ((contract[:1], contract[1:]), ((), ())), preferred...]
    dot_general x2 -> x0, matrix products: 47.1 us -> none  [pick(): lax.dot_general(chosen, rows, (((2,), (1,)), ((0,), (0,))), preferred_ele...]
    convert_element_type x4 -> x0, other arithmetic: 19.8 us -> none  [the longest x1 12.6 us: fast_body(): (row_gate.reshape(-1, 1) * pick(cots).astype(bf16).astype(f32)).astype(bf16)]
    unnamed x165 -> x148, local copies, waits for them, and re-layouts: 32.1 us -> 20.4 us
where the time goes in v2:
time: 1150 us; the launch traced here: 1130 us
  Pallas kernels  925 us (80%)
  matrix products  93.1 us (8%)
  local copies, waits for them, and re-layouts  58.4 us (5%)
  other arithmetic  56.1 us (5%)
    pallas_call x2, Pallas kernels, combine(): pl.pallas_call(functools.partial(combine_kernel, nz, cap), out_shape=jax....  293 us
    pallas_call x1, Pallas kernels, run_experts(): pl.pallas_call(functools.partial(experts_kernel, nz, cap), out_shape=[sha...  198 us
    pallas_call x1, Pallas kernels, gather_first(): pl.pallas_call(functools.partial(first_kernel, nz), out_shape=[shape((4,...  189 us
    dot_general x9, matrix products, mm(): lax.dot_general(a, b, ((contract[:1], contract[1:]), ((), ())), preferred...  92.8 us
    pallas_call x1, Pallas kernels, reduce_last(): pl.pallas_call(functools.partial(last_kernel, nz), out_shape=[shape((rows...  88.7 us
    pallas_call x2, Pallas kernels, fold(): pl.pallas_call(fold_kernel, out_shape=jax.ShapeDtypeStruct((seq, width),...  79.6 us
    pallas_call x1, Pallas kernels, gather_rows(): pl.pallas_call(functools.partial(spread_kernel, nz, everywhere), out_shap...  38.4 us
    pallas_call x1, Pallas kernels, attend_back(): pl.pallas_call(functools.partial(attend_back_kernel, scale, length // 4),...  23.4 us

profile of v2, /device:TPU:16, one launch (start us, length us, event | category | flops | bytes accessed | tf_op | source)
XLA Modules:
  0.0 1134.5 jit_solution(5930329792472304646)
XLA Ops:
  7.8 189.0 %shard_map.212 = (bf16[4,8,64,1280]{3,2,1,0:T(8,128)(2,1)}, bf16[8,128,2048]{2,1,0:T(8,128)(2,1)}, bf16[4,256,2048]{2,1,0:T(8,128)(2,1)}, bf16[32,256,2048]{2,1,0:T(8,128)(2,1)}, f32[32,48,128]{2,1,0:T(8,128)}) custom-call(bf16[4,64,1280]{2,1,0:T(8,128)(2,1)} %pad_maximum_fusion.3.pack, bf16[128,2048]{1,0:T(8,128)(2,1)} %wo.1, bf16[256,2048]{1,0:T(8,128)(2,1)} %bitcast.172, ...), custom_call_target="tpu_custom_call" | custom-call | tf_op jit(solution)/shard_map/pallas_call | solution.py:608
  196.9 1.4 copy.81
  198.5 3.2 multiply_reduce_fusion
  203.4 1.4 copy-done.57
  204.8 5.6 fusion.50
  210.4 2.3 copy-done.18
  212.8 2.7 slice.81
  215.4 5.6 copy.37
  221.0 5.3 copy.38
  226.6 2.9 multiply_reduce_fusion.3
  230.1 1.2 multiply_multiply_fusion
  231.4 1.9 multiply_cosine_fusion
  233.3 1.5 subtract_convert_fusion
  240.4 14.1 %shard_map.213 = (bf16[8,128,1024]{2,1,0:T(8,128)(2,1)S(1)}, f32[8,1,1024]{2,1,0:T(1,128)S(1)}) custom-call(bf16[8,1024,128]{2,1,0:T(8,128)(2,1)S(1)} %maximum_bitcast_fusion.q, bf16[1024,128]{1,0:T(8,128)(2,1)S(1)} %copy.43.k, bf16[128,1024]{1,0:T(8,128)(2,1)S(1)} %copy.44.vt), custom_call_target="tpu_custom_call" | custom-call | tf_op jit(solution)/shard_map/pallas_call | solution.py:1067
  254.5 19.6 %bitcast_convert_fusion = bf16[1024,2048]{1,0:T(8,128)(2,1)} fusion(bf16[8,128,1024]{2,1,0:T(8,128)(2,1)S(1)} %get-tuple-element.36, bf16[8,128,2048]{2,1,0:T(8,128)(2,1)} %get-tuple-element.37), kind=kOutput, calls=%fused_computation.3 | convolution fusion | flops 4297064448 | bytes 10485760 | tf_op jit(solution)/shard_map/dot_general | solution.py:1314
  274.1 40.8 %shard_map.214 = f32[256,2048]{1,0:T(8,128)} custom-call(bf16[4,256,2048]{2,1,0:T(8,128)(2,1)} %bitcast.179), custom_call_target="tpu_custom_call" | custom-call | tf_op jit(solution)/shard_map/pallas_call | solution.py:873
  314.9 3.8 multiply_reduce_fusion.6
  318.8 2.8 multiply_convert_fusion.1.mine
  326.1 197.9 %shard_map.215 = (bf16[32,256,2048]{2,1,0:T(8,128)(2,1)}, bf16[32,80,2048]{2,1,0:T(8,128)(2,1)}, bf16[32,80,2048]{2,1,0:T(8,128)(2,1)}, bf16[4,2,320,2048]{3,2,1...) custom-call(bf16[256,2048]{1,0:T(8,128)(2,1)} %multiply_convert_fusi, ...), custom_call_target="tpu_custom_call" | custom-call | tf_op jit(solution)/shard_map/pallas_call | solution.py:1294
  525.0 146.6 %shard_map.217 = f32[256,2048]{1,0:T(8,128)} custom-call(bf16[32,80,2048]{2,1,0:T(8,128)(2,1)} %get-tuple-element.40.rows, s32[2,32,1,256]{3,2,1,0:T(1,128)} %copy-done.28, f32[2,32,1,256]{3,2,1,0:T(1,128)} %broadcast_in_dim.25.gates), custom_call_target="tpu_custom_call" | custom-call | tf_op jit(solution)/shard_map/pallas_call | solution.py:818
  671.7 2.9 multiply_reduce_fusion.4
  674.6 1.7 fusion.47.mine
  676.4 38.4 %shard_map.218 = bf16[4,256,2048]{2,1,0:T(8,128)(2,1)} custom-call(bf16[256,2048]{1,0:T(8,128)(2,1)} %fusion.47.mine), custom_call_target="tpu_custom_call" | custom-call | tf_op jit(solution)/shard_map/pallas_call | solution.py:641
  714.8 8.4 convolution_convert_fusion.3.do
  723.3 23.4 %shard_map.219 = (f32[1024,1024]{1,0:T(8,128)S(1)}, f32[1024,128]{1,0:T(8,128)S(1)}, f32[1024,128]{1,0:T(8,128)S(1)}) custom-call(bf16[8,1024,128]{2,1,0:T(8,128)(2,1)S(1)} %maximum_bitcast_fusion.q, bf16[1024,128]{1,0:T(8,128)(2,1)S(1)} %copy.43.k, bf16[128,1024]{1,0:T(8,128)(2,1)S(1)} %get-tuple-element.84.kt, bf16[1024,128]{1,0:T(8,128)(2,1)S(1)} %slice.117.v, ...), custom_call_target="tpu_custom_call" | custom-call | tf_op jit(solution)/shard_map/pallas_call | solution.py:1112
  746.7 2.0 copy-done.2
  749.8 1.2 fusion.31
  751.0 1.8 fusion.17
  753.0 5.3 copy.50
  758.3 4.0 fusion.48
  762.3 3.8 copy.65
  766.1 2.8 copy.64
  768.9 4.8 multiply_add_fusion.1
  773.8 3.6 multiply_reduce_fusion.1
  777.4 3.9 fusion.2
  781.4 2.6 copy.55
  784.0 9.7 convolution_convert_fusion.1
  793.7 38.7 %shard_map.220 = f32[256,2048]{1,0:T(8,128)} custom-call(bf16[4,256,2048]{2,1,0:T(8,128)(2,1)} %bitcast.178), custom_call_target="tpu_custom_call" | custom-call | tf_op jit(solution)/shard_map/pallas_call | solution.py:873
  832.5 2.3 fusion.9
  835.6 146.8 %shard_map.216 = f32[256,2048]{1,0:T(8,128)} custom-call(bf16[32,80,2048]{2,1,0:T(8,128)(2,1)} %get-tuple-element.39.rows, s32[2,32,1,256]{3,2,1,0:T(1,128)} %copy-done.28, f32[2,32,1,256]{3,2,1,0:T(1,128)} %pad_maximum_fusion.5.gates), custom_call_target="tpu_custom_call" | custom-call | tf_op jit(solution)/shard_map/pallas_call | solution.py:818
  982.4 5.1 fusion.15
  989.2 7.6 convolution_convert_fusion
  996.8 6.0 convolution_convert_fusion.2
  1003.5 88.7 %shard_map.221 = (f32[64,4096]{1,0:T(8,128)}, f32[64,512]{1,0:T(8,128)}, f32[64,512]{1,0:T(8,128)}, f32[128,2048]{1,0:T(8,128)}, f32[32,48,128]{2,1,0:T(8,128)}) custom-call(bf16[4,8,64,1280]{3,2,1,0:T(8,128)(2,1)} %bitcast.175, bf16[8,128,2048]{2,1,0:T(8,128)(2,1)} %bitcast.181, f32[48,128]{1,0:T(8,128)} %pad.25.gains), custom_call_target="tpu_custom_call" | custom-call | tf_op jit(solution)/shard_map/pallas_call | solution.py:1022
  1092.2 1.2 reduce_sum.167
  1094.7 14.6 %convolution_bitcast_fusion.2 = f32[1,2048,768]{2,1,0:T(8,128)} fusion(bf16[4,2,320,2048]{3,2,1,0:T(8,128)(2,1)} %get-tuple-element.50, bf16[4,2,320,768]{3,2,1,0:T(8,128)(2,1)} %get-tuple-element.51), kind=kOutput, calls=%fused_computation.25 | convolution fusion | flops 8053063680 | bytes 20709376 | tf_op jit(solution)/shard_map/dot_general | solution.py:1314
  1109.3 10.8 convolution_bitcast_fusion.1
  1120.2 10.6 convolution_bitcast_fusion
  (211 shorter events, 29.8 us)
Async XLA Ops:
  198.2 28.1 %copy-start.24 = (f32[4,8,48,128]{3,1,2,0:T(8,128)}, f32[4,8,48,128]{3,1,2,0:T(8,128)S(1)}, u32[]{:S(2)}) copy-start(f32[4,8,48,128]{3,1,2,0:T(8,128)S(1)} %copy.81) | copy-start | bytes 2359300
  198.5 3.8 copy-start.9
  226.6 4.7 copy-start.52
  231.3 5.2 copy-start.54
  231.4 5.2 copy-start.37
  236.4 3.8 copy-start.50
  236.4 3.7 copy-start.41
  254.5 19.6 %copy-start.3 = (bf16[8,128,1024]{2,1,0:T(8,128)(2,1)}, bf16[8,128,1024]{2,1,0:T(8,128)(2,1)S(1)}, u32[]{:S(2)}) copy-start(bf16[8,128,1024]{2,1,0:T(8,128)(2,1)S(1)} %get-tuple-element.36) | copy-start | bytes 6291460
  274.0 40.9 %copy-start.13 = (bf16[1,256,2048]{2,1,0:T(8,128)(2,1)S(1)}, bf16[1,256,2048]{2,1,0:T(8,128)(2,1)}, u32[]{:S(2)}) copy-start(bf16[1,256,2048]{2,1,0:T(8,128)(2,1)} %param.13) | copy-start | bytes 3145732
  318.8 355.8 %copy-start.44 = (f32[256]{0:T(256)}, f32[256]{0:T(256)S(1)}, u32[]{:S(2)}) copy-start(f32[256]{0:T(256)S(1)} %fusion.41) | copy-start | bytes 3076
  325.5 198.6 %copy-start.31 = (f32[32,256]{1,0:T(8,128)}, f32[32,256]{1,0:T(8,128)S(1)}, u32[]{:S(2)}) copy-start(f32[32,256]{1,0:T(8,128)S(1)} %get-tuple-element.64) | copy-start | bytes 98308
  525.0 146.6 %copy-start.7 = (f32[256,2048]{1,0:T(8,128)S(1)}, f32[256,2048]{1,0:T(8,128)}, u32[]{:S(2)}) copy-start(f32[256,2048]{1,0:T(8,128)} %get-tuple-element.68) | copy-start | bytes 6291460
  674.6 40.2 %copy-start.47 = (f32[256]{0:T(256)}, f32[256]{0:T(256)S(1)}, u32[]{:S(2)}) copy-start(f32[256]{0:T(256)S(1)} %multiply_multiply_fusion.4) | copy-start | bytes 3076
  723.2 26.6 %copy-start.38 = (f32[1024]{0:T(1024)S(1)}, f32[1024]{0:T(1024)}, u32[]{:S(2)}) copy-start(f32[1024]{0:T(1024)} %copy-done.37) | copy-start | bytes 12292
  723.2 26.6 %copy-start.55 = (f32[64]{0:T(128)S(1)}, f32[64]{0:T(128)}, u32[]{:S(2)}) copy-start(f32[64]{0:T(128)} %copy-done.54) | copy-start | bytes 772
  723.2 27.8 %copy-start.40 = (f32[1024]{0:T(1024)S(1)}, f32[1024]{0:T(1024)}, u32[]{:S(2)}) copy-start(f32[1024]{0:T(1024)} %copy-done.39) | copy-start | bytes 12292
  723.3 27.8 %copy-start.51 = (f32[128]{0:T(128)S(1)}, f32[128]{0:T(128)}, u32[]{:S(2)}) copy-start(f32[128]{0:T(128)} %copy-done.50) | copy-start | bytes 1540
  723.3 29.5 %copy-start.42 = (f32[1024]{0:T(1024)S(1)}, f32[1024]{0:T(1024)}, u32[]{:S(2)}) copy-start(f32[1024]{0:T(1024)} %copy-done.41) | copy-start | bytes 12292
  748.7 4.1 copy-start.16
  768.9 4.8 copy-start.6
  768.9 4.8 copy-start.53
  793.7 38.8 %copy-start.49 = (f32[256]{0:T(256)S(1)}, f32[256]{0:T(256)}, u32[]{:S(2)}) copy-start(f32[256]{0:T(256)} %get-tuple-element.77) | copy-start | bytes 3076
  793.7 38.8 %copy-start.14 = (bf16[1,256,2048]{2,1,0:T(8,128)(2,1)S(1)}, bf16[1,256,2048]{2,1,0:T(8,128)(2,1)}, u32[]{:S(2)}) copy-start(bf16[1,256,2048]{2,1,0:T(8,128)(2,1)} %param.13) | copy-start | bytes 3145732
  793.7 41.1 %copy-start.34 = (f32[32,256]{1,0:T(8,128)S(1)}, f32[32,256]{1,0:T(8,128)}, u32[]{:S(2)}) copy-start(f32[32,256]{1,0:T(8,128)} %get-tuple-element.63) | copy-start | bytes 98308
  793.7 41.1 %copy-start.32 = (f32[32,256]{1,0:T(8,128)S(1)}, f32[32,256]{1,0:T(8,128)}, u32[]{:S(2)}) copy-start(f32[32,256]{1,0:T(8,128)} %copy-done.31) | copy-start | bytes 98308
  835.5 146.8 %copy-start.8 = (f32[256,2048]{1,0:T(8,128)S(1)}, f32[256,2048]{1,0:T(8,128)}, u32[]{:S(2)}) copy-start(f32[256,2048]{1,0:T(8,128)} %get-tuple-element.68) | copy-start | bytes 6291460
  835.5 146.8 %copy-start.12 = (f32[256,2048]{1,0:T(8,128)S(1)}, f32[256,2048]{1,0:T(8,128)}, u32[]{:S(2)}) copy-start(f32[256,2048]{1,0:T(8,128)} %shard_map.217) | copy-start | bytes 6291460
  835.6 146.9 %copy-start.45 = (f32[256]{0:T(256)S(1)}, f32[256]{0:T(256)}, u32[]{:S(2)}) copy-start(f32[256]{0:T(256)} %copy-done.44) | copy-start | bytes 3076
  835.6 146.9 %copy-start.48 = (f32[256]{0:T(256)S(1)}, f32[256]{0:T(256)}, u32[]{:S(2)}) copy-start(f32[256]{0:T(256)} %copy-done.47) | copy-start | bytes 3076
  982.4 5.1 copy-start.46
  982.4 5.1 copy-start.10
  989.2 7.6 copy-start.4
  989.2 7.6 copy-start.23
  996.8 6.0 copy-start.43
  996.8 6.0 copy-start.56
  1003.5 105.8 %slice-start.4 = ((s8[10485760]{0:T(1024)(128)(4,1)}), s8[2097152]{0:T(1024)(128)(4,1)S(1)}, s32[]{:S(2)}) async-start(s8[10485760]{0:T(1024)(128)(4,1)} %bitcast.209), calls=%async_computation.4 | async-start | bytes 4194304
  1094.7 14.6 %slice-start.5 = ((s8[10485760]{0:T(1024)(128)(4,1)}), s8[4194304]{0:T(1024)(128)(4,1)S(1)}, s32[]{:S(2)}) async-start(s8[10485760]{0:T(1024)(128)(4,1)} %bitcast.209), calls=%async_computation.5 | async-start | bytes 8388608
  1094.7 14.6 %slice-start.6 = ((s8[10485760]{0:T(1024)(128)(4,1)}), s8[4194304]{0:T(1024)(128)(4,1)S(1)}, s32[]{:S(2)}) async-start(s8[10485760]{0:T(1024)(128)(4,1)} %bitcast.209), calls=%async_computation.6 | async-start | bytes 8388608
  1094.7 14.6 %copy-start.59 = (bf16[4,2,320,768]{3,2,1,0:T(8,128)(2,1)S(1)}, bf16[4,2,320,768]{3,2,1,0:T(8,128)(2,1)}, u32[]{:S(2)}) copy-start(bf16[4,2,320,768]{3,2,1,0:T(8,128)(2,1)} %get-tuple-element.52) | copy-start | bytes 11796484
  1094.7 25.4 %slice-start.1 = ((s8[10485760]{0:T(1024)(128)(4,1)}), s8[4194304]{0:T(1024)(128)(4,1)S(1)}, s32[]{:S(2)}) async-start(s8[10485760]{0:T(1024)(128)(4,1)} %bitcast.207), calls=%async_computation.1 | async-start | bytes 8388608
  1094.7 25.4 %slice-start.2 = ((s8[10485760]{0:T(1024)(128)(4,1)}), s8[4194304]{0:T(1024)(128)(4,1)S(1)}, s32[]{:S(2)}) async-start(s8[10485760]{0:T(1024)(128)(4,1)} %bitcast.207), calls=%async_computation.2 | async-start | bytes 8388608
  1109.3 10.8 slice-start.3
  1109.3 10.8 copy-start.58
  1120.1 10.6 copy-start.27
  1120.1 11.6 %copy-start.36 = (f32[64,512]{1,0:T(8,128)S(1)}, f32[64,512]{1,0:T(8,128)}, u32[]{:S(2)}) copy-start(f32[64,512]{1,0:T(8,128)} %get-tuple-element.108) | copy-start | bytes 393220
  1120.1 12.2 %copy-start.35 = (f32[64,512]{1,0:T(8,128)S(1)}, f32[64,512]{1,0:T(8,128)}, u32[]{:S(2)}) copy-start(f32[64,512]{1,0:T(8,128)} %get-tuple-element.109) | copy-start | bytes 393220
  1120.1 12.9 %copy-start.26 = (f32[128,2048]{1,0:T(8,128)S(1)}, f32[128,2048]{1,0:T(8,128)}, u32[]{:S(2)}) copy-start(f32[128,2048]{1,0:T(8,128)} %get-tuple-element.110) | copy-start | bytes 3145732
  1120.2 13.9 %copy-start.1 = (bf16[64,512]{1,0:T(8,128)(2,1)S(1)}, bf16[64,512]{1,0:T(8,128)(2,1)}, u32[]{:S(2)}) copy-start(bf16[64,512]{1,0:T(8,128)(2,1)} %param.15) | copy-start | bytes 196612
  (19 other events, 42.4 us)

commit v3 on v2

--- a/solution.py
+++ b/solution.py
@@ -361,6 +361,8 @@
 ANY = pl.BlockSpec(memory_space=pl.ANY)
 IN_VMEM = pl.BlockSpec(memory_space=pltpu.VMEM)
 f32, bf16 = jnp.float32, jnp.bfloat16
+NT = (((1,), (1,)), ((), ()))
+TN = (((0,), (0,)), ((), ()))
 
 
 class Place:
@@ -549,76 +551,335 @@
     return [pltpu.SemaphoreType.DMA((nz, 11)), pltpu.SemaphoreType.DMA((nz, 10))]
 
 
-def first_kernel(nz, pack, wo, tok, cot, meta, packs, wos, toks, cots, metas, *sems):
-    pair_sems, (a_send, a_recv, local) = sems[:10], sems[10:]
+class Fold:
+    def __init__(self, p, parts, sx, sy, h0, h1, bx, by, send, recv):
+        half = bx.shape[0] // 2
+        self.halves = low, high = pl.ds(0, half), pl.ds(half, half)
+        self.p, self.parts, self.sx, self.sy = p, parts, sx, sy
+        self.h0, self.h1, self.bx, self.by = h0, h1, bx, by
+        copy = lambda i, src, dst, device: remote(src, dst, send.at[i], recv.at[i], device)
+        self.to_x = copy(0, parts.at[p.cd, low], h0, p.dx)
+        self.to_y = copy(1, parts.at[p.cd, high], h1, p.dy)
+        self.x_low = copy(2, parts.at[p.cx, low], bx.at[low], p.dx)
+        self.y_high = copy(3, parts.at[p.cy, high], by.at[high], p.dy)
+        self.x_high = copy(4, sx, bx.at[high], p.dx)
+        self.y_low = copy(5, sy, by.at[low], p.dy)
+
+    def begin(self):
+        for copy in (self.to_x, self.to_y, self.x_low, self.y_high):
+            copy.start()
+
+    def middle(self):
+        p, (low, high), parts = self.p, self.halves, self.parts
+        self.to_y.wait_recv()
+        total = parts[p.cx, high].astype(f32) + self.h1[...].astype(f32)
+        self.sx[...] = total.astype(self.sx.dtype)
+        self.x_high.start()
+        self.to_x.wait_recv()
+        total = parts[p.cy, low].astype(f32) + self.h0[...].astype(f32)
+        self.sy[...] = total.astype(self.sy.dtype)
+        self.y_low.start()
+
+    def end(self, store):
+        p, parts = self.p, self.parts
+        low, high = self.halves
+        for rows, waits in ((low, (self.x_low, self.y_low)), (high, (self.y_high, self.x_high))):
+            for copy in waits:
+                copy.wait_recv()
+            total = parts[p.c, rows].astype(f32) + self.bx[rows].astype(f32)
+            store(rows, total + self.by[rows].astype(f32))
+        for copy in (self.to_x, self.to_y, self.x_low, self.y_high, self.x_high, self.y_low):
+            copy.wait_send()
+
+
+def fold_scratch(seq, width):
+    buf = lambda r: pltpu.VMEM((r, width), bf16)
+    return (
+        [buf(seq // 2)] * 4 + [buf(seq)] * 2 + [pltpu.SemaphoreType.DMA((6,))] * 2
+    )
+
+
+def front_kernel(nz, scale, *refs):
+    pack, wo, tok, cot, meta, cosine, sine = refs[:7]
+    packs, wos, toks, cots, metas = refs[7:12]
+    xn, raw, q, k, v, ot, lse, hidden, hn, gain_out, head_out, slots, gates = refs[12:25]
+    tok_v, w_v, wo_v, meta_v, vt, ob, part = refs[25:32]
+    fold_refs, pair_sems = refs[32:40], refs[40:50]
+    a_send, a_recv, local, load = refs[50:]
     p = Place()
+    seq, width = tok.shape
+    length = 4 * seq
+    heads = q.shape[0]
+    me = p.c * (2 * nz) + p.e
     greet(p, nz, diagonal=True)
-    own = [
+    into = [
         pltpu.make_async_copy(src, dst, local.at[i])
         for i, (src, dst) in enumerate(
             (
-                (pack.at[p.c], packs.at[p.c, p.e]),
-                (wo, wos.at[p.e]),
-                (tok, toks.at[p.c]),
-                (cot, cots.at[p.c * (2 * nz) + p.e]),
-                (meta, metas.at[p.c * (2 * nz) + p.e]),
+                (pack.at[p.c], w_v.at[p.c, p.e]),
+                (wo, wo_v.at[p.e]),
+                (tok, tok_v.at[p.c]),
+                (cot, part.at[0]),
             )
         )
     ]
-    for copy in own:
+    own = [
+        pltpu.make_async_copy(src, dst, local.at[4 + i])
+        for i, (src, dst) in enumerate(
+            (
+                (w_v.at[p.c, p.e], packs.at[p.c, p.e]),
+                (wo_v.at[p.e], wos.at[p.e]),
+                (meta, metas.at[me]),
+                (part.at[0], cots.at[me]),
+            )
+        )
+    ]
+    loads = [
+        pltpu.make_async_copy(src, dst, load.at[i])
+        for i, (src, dst) in enumerate(
+            [(packs, w_v), (wos, wo_v), (metas, meta_v)]
+            + [(toks.at[c], tok_v.at[c]) for c in (p.cx, p.cy, p.cd)]
+        )
+    ]
+    for copy in into:
         copy.start()
+    own[2].start()
     swaps = [
         remote(pack.at[c], packs.at[p.c, p.e], a_send.at[i], a_recv.at[i], device)
         for i, (c, device) in enumerate(((p.cx, p.dx), (p.cy, p.dy), (p.cd, p.dd)))
     ]
     for copy in swaps:
         copy.start()
-    s = lambda i: (pair_sems[2 * i], pair_sems[2 * i + 1])
-    j_tok = Spread(p, nz, tok, lambda c, z, k: toks.at[c], tok.shape[0] // 2, *s(0), False, True, False)
-    j_meta = Spread(p, nz, meta, by_device(metas, nz), meta.shape[0] // 2, *s(1))
-    j_cot = Spread(p, nz, cot, by_device(cots, nz), cot.shape[0] // 2, *s(2))
-    j_wo = Spread(p, nz, wo, lambda c, z, k: wos.at[z * 2 + k], 0, *s(3), True, False, True)
+
+    def job(i, src, block, half, *ways):
+        return Spread(p, nz, src, block, half, *pair_sems[2 * i : 2 * i + 2], *ways)
+
+    j_tok = job(0, tok, lambda c, z, k: toks.at[c], seq // 2, False, True, False)
+    j_meta = job(1, meta, by_device(metas, nz), meta.shape[0] // 2)
+    j_cot = job(2, cot, by_device(cots, nz), seq // 2)
+    j_wo = job(3, wo, lambda c, z, k: wos.at[z * 2 + k], 0, True, False, True)
     own_pack = packs.at[:, p.e]
-    j_pack = Spread(
-        p, nz, own_pack, lambda c, z, k: packs.at[:, z * 2 + k], 0, *s(4), True, False, True
-    )
+    j_pack = job(4, own_pack, lambda c, z, k: packs.at[:, z * 2 + k], 0, True, False, True)
+    j_meta.step(0)
     j_tok.step(0)
-    j_meta.step(0)
+    for i in (0, 1, 3):
+        into[i].wait()
+        own[i].start()
     for i, c in enumerate((p.cx, p.cy, p.cd)):
         ref = packs.at[c, p.e]
         remote(ref, ref, a_send.at[i], a_recv.at[i], p.dx).wait_recv()
     own[0].wait()
     j_pack.step(0)
+    j_meta.step(1)
+    j_pack.step(1)
+    j_tok.step(1)
+    loads[3].start()
+    loads[4].start()
+    j_tok.step(2)
+    loads[5].start()
+    j_meta.step(2)
+    j_pack.step(2)
+    j_cot.step(0)
+    for i in range(3, nz + 2):
+        j_meta.step(i)
+        j_pack.step(i)
+    own[2].wait()
+    for z in j_meta.order:
+        j_meta.from_pair(z)
+    loads[2].start()
     j_wo.step(0)
-    j_cot.step(0)
-    for far in range(1, nz + 2):
-        for job in (j_tok, j_meta, j_pack, j_wo, j_cot):
-            job.step(far)
-    for copy in own[1:]:
+    for z in j_pack.order:
+        j_pack.from_pair(z)
+    loads[0].start()
+
+    loads[2].wait()
+    n = meta_lines(q.shape[1], width, seq)
+    per = 128 * 8 * nz // width
+
+    def gain(line):
+        found = [
+            sum(meta_v[per * j + i, pl.ds(line, 1)] for i in range(per))
+            for j in range(width // 128)
+        ]
+        return jnp.concatenate(found, axis=1)
+
+    def head_gain(line):
+        return sum(meta_v[b, pl.ds(line, 1)] for b in range(8 * nz))
+
+    gain_out[0:1] = gain(n)
+    gain_out[1:2] = gain(n + 1)
+    head_out[0:1] = head_gain(n + 2)
+    head_out[1:2] = head_gain(n + 3)
+
+    def rms(x, g):
+        return x * lax.rsqrt(jnp.mean(x * x, axis=-1, keepdims=True) + epsilon) * g
+
+    into[2].wait()
+    for copy in loads[3:]:
         copy.wait()
+
+    @pl.loop(0, 8)
+    def _(i):
+        c, h = lax.div(i, 2), lax.rem(i, 2)
+        half = seq // 2
+        rows = tok_v[c, pl.ds(pl.multiple_of(h * half, half), half)].astype(f32)
+        here = pl.ds(pl.multiple_of(i * half, half), half)
+        xn[here] = rms(rows, gain_out[0:1]).astype(bf16)
+
+    loads[0].wait()
+
+    @pl.loop(0, raw.shape[1] // 256)
+    def _(t):
+        cols = pl.ds(pl.multiple_of(t * 256, 256), 256)
+        w = w_v[:, :, :, cols].reshape(width, 256)
+        raw[:, cols] = jnp.dot(xn[...], w, preferred_element_type=f32)
+
+    j_cot.step(1)
+    j_wo.step(1)
+
+    def prep(x, g):
+        y = rms(x, g)
+        return (y * cosine[...] + pltpu.roll(y, HD // 2, 1) * sine[...]).astype(bf16)
+
+    k[...] = prep(raw[:, pl.ds(heads * HD, HD)], head_out[1:2])
+    values = raw[:, pl.ds((heads + 1) * HD, HD)]
+    v[...] = values.astype(bf16)
+    vt[...] = values.T.astype(bf16)
+
+    def attend(h):
+        cols = pl.ds(pl.multiple_of(h * HD, HD), HD)
+        q[h] = prep(raw[:, cols], head_out[0:1])
+        for i in range(length // seq):
+            keys = (i + 1) * seq
+            here = pl.ds(i * seq, seq)
+            s = lax.dot_general(k[pl.ds(0, keys)], q[h, here], NT, preferred_element_type=f32)
+            s = s * scale
+            key_pos = lax.broadcasted_iota(jnp.int32, s.shape, 0)
+            query_pos = lax.broadcasted_iota(jnp.int32, s.shape, 1) + i * seq
+            s = jnp.where(key_pos <= query_pos, s, masked_value)
+            largest = jnp.max(s, axis=0, keepdims=True)
+            weights = jnp.exp(s - largest)
+            total = jnp.sum(weights, axis=0, keepdims=True)
+            o = jnp.dot(vt[:, pl.ds(0, keys)], weights.astype(bf16), preferred_element_type=f32)
+            o = o / total
+            ot[h, :, here] = o.astype(bf16)
+            ob[here, cols] = o.T.astype(bf16)
+            lse[h, :, here] = largest + jnp.log(total)
+
+    pl.loop(0, heads // 2)(attend)
+    j_wo.step(2)
+    j_cot.step(2)
+    pl.loop(heads // 2, heads)(attend)
+    for i in range(3, nz + 2):
+        j_wo.step(i)
+    own[1].wait()
+    for z in j_wo.order:
+        j_wo.from_pair(z)
+    loads[1].start()
+    own[3].wait()
+
+    upto = lax.broadcasted_iota(jnp.int32, (seq, seq), 0) <= lax.broadcasted_iota(
+        jnp.int32, (seq, seq), 1
+    )
+    upto = upto.astype(f32).astype(bf16)
+    lines = seq // 128
+    topk = n // lines // 2
+    for j, expert in enumerate((me, me + 1 - 2 * p.k)):
+        expert = expert.astype(f32)
+        member, weight = [], []
+        for line in range(lines):
+            named = [meta_v[:, i * lines + line] == expert for i in range(topk)]
+            gate = [meta_v[:, (topk + i) * lines + line] for i in range(topk)]
+            member.append(sum(x.astype(f32) for x in named))
+            weight.append(sum(jnp.where(x, y, 0.0) for x, y in zip(named, gate)))
+        member = jnp.concatenate(member, axis=1)
+        rank = jnp.dot(member.astype(bf16), upto, preferred_element_type=f32)
+        slots[j] = jnp.where(member > 0.5, rank.astype(jnp.int32) - 1, -1)
+        gates[j] = jnp.concatenate(weight, axis=1)
+
+    loads[1].wait()
+    tile = 512
+
+    @pl.loop(0, width // tile)
+    def _(t):
+        cols = pl.ds(pl.multiple_of(t * tile, tile), tile)
+        w = wo_v[:, :, cols].reshape(heads * HD, tile)
+        out = jnp.dot(ob[...], w, preferred_element_type=f32)
+        part[:, :, cols] = out.astype(bf16).reshape(4, seq, tile)
+
+    fold = Fold(p, part, *fold_refs)
+    fold.begin()
+    j_cot.step(3)
+    fold.middle()
+
+    def store(rows, total):
+        h = tok_v[p.c, rows].astype(f32) + total
+        hidden[rows] = h
+        hn[rows] = rms(h, gain_out[1:2]).astype(bf16)
+
+    fold.end(store)
+    for i in range(4, nz + 2):
+        j_cot.step(i)
     for copy in swaps:
         copy.wait_send()
-    for job in (j_tok, j_meta, j_pack, j_wo, j_cot):
-        job.finish()
-
-
-def gather_first(nz, pack, wo, tok, cot, meta):
+    for spread in (j_tok, j_meta, j_cot, j_wo, j_pack):
+        spread.finish(pair=spread is j_cot)
+
+
+def meta_lines(length, width, seq):
+    return 2 * 8 * seq // 128
+
+
+def front(nz, scale, pack, wo, tok, cot, meta, cosine, sine):
     blocks = 8 * nz
-    shape = jax.ShapeDtypeStruct
+    seq, width = tok.shape
+    length = 4 * seq
+    wide = pack.shape[2]
+    heads = wide // HD - 2
+    hbm = lambda n, a: jax.ShapeDtypeStruct(n + a.shape, a.dtype)
+    out = lambda *n: jax.ShapeDtypeStruct(n[:-1], n[-1])
+    vmem = lambda *n: pltpu.VMEM(n, bf16)
+    dma = pltpu.SemaphoreType.DMA
     return pl.pallas_call(
-        functools.partial(first_kernel, nz),
+        functools.partial(front_kernel, nz, scale),
         out_shape=[
-            shape((4, 2 * nz) + pack.shape[1:], pack.dtype),
-            shape((2 * nz,) + wo.shape, wo.dtype),
-            shape((4,) + tok.shape, tok.dtype),
-            shape((blocks,) + cot.shape, cot.dtype),
-            shape((blocks,) + meta.shape, meta.dtype),
+            jax.ShapeDtypeStruct((4, 2 * nz) + pack.shape[1:], bf16),
+            hbm((2 * nz,), wo),
+            hbm((4,), tok),
+            hbm((blocks,), cot),
+            hbm((blocks,), meta),
+            out(length, width, bf16),
+            out(length, wide, f32),
+            out(heads, length, HD, bf16),
+            out(length, HD, bf16),
+            out(length, HD, bf16),
+            out(heads, HD, length, bf16),
+            out(heads, 1, length, f32),
+            out(seq, width, f32),
+            out(seq, width, bf16),
+            out(2, width, f32),
+            out(2, HD, f32),
+            out(2, blocks, seq, jnp.int32),
+            out(2, blocks, seq, f32),
         ],
-        in_specs=[ANY] * 5,
-        out_specs=[ANY] * 5,
-        scratch_shapes=spread_sems(nz) * 5 + [pltpu.SemaphoreType.DMA((n,)) for n in (3, 3, 5)],
-        compiler_params=pltpu.CompilerParams(collective_id=1, has_side_effects=True),
-    )(pack, wo, tok, cot, meta)
+        in_specs=[ANY] * 5 + [IN_VMEM] * 2,
+        out_specs=[ANY] * 5 + [IN_VMEM] * 13,
+        scratch_shapes=[
+            vmem(4, seq, width),
+            vmem(4, 2 * nz, pack.shape[1], wide),
+            vmem(2 * nz, wo.shape[0], width),
+            pltpu.VMEM((blocks,) + meta.shape, f32),
+            vmem(HD, length),
+            vmem(length, heads * HD),
+            vmem(4, seq, width),
+        ]
+        + fold_scratch(seq, width)
+        + spread_sems(nz) * 5
+        + [dma((n,)) for n in (3, 3, 8, 6)],
+        compiler_params=pltpu.CompilerParams(
+            collective_id=1, has_side_effects=True, vmem_limit_bytes=VMEM_BYTES
+        ),
+    )(pack, wo, tok, cot, meta, cosine, sine)
 
 
 def spread_kernel(nz, everywhere, mine, out, send, recv, local):
@@ -641,257 +902,432 @@
     return pl.pallas_call(
         functools.partial(spread_kernel, nz, everywhere),
         out_shape=jax.ShapeDtypeStruct((blocks,) + mine.shape, mine.dtype),
-        in_specs=[ANY],
+        in_specs=[IN_VMEM],
         out_specs=ANY,
         scratch_shapes=spread_sems(nz) + [pltpu.SemaphoreType.DMA],
         compiler_params=pltpu.CompilerParams(collective_id=collective_id, has_side_effects=True),
     )(mine)
 
 
-def combine_kernel(nz, cap, rows, slots, gates, out, rbuf, w, sd, sx, sy, sz, h0, h1, bx, by, bz, *sems):
-    pair_send, pair_recv, load, s_h0, s_h1, s_x, s_y, s_z, r_h0, r_h1, r_x, r_y, r_z = sems
-    p = Place()
-    order = pick_order(p, nz)
-    seq = w.shape[2]
-    half = seq // 2
-    width = rbuf.shape[3]
-    names = lax.broadcasted_iota(jnp.int32, (cap, seq), 0)
-    tile = min(512, width)
-
-    @pl.when(p.z == 0)
-    def _():
-        bz[pl.ds(0, nz)] = jnp.zeros((nz,) + bz.shape[1:], bz.dtype)
-
-    @pl.when(p.z == nz - 1)
-    def _():
-        bz[pl.ds(0, nz - 1)] = jnp.zeros((nz - 1,) + bz.shape[1:], bz.dtype)
-        bz[nz] = jnp.zeros(bz.shape[1:], bz.dtype)
-
-    greet(p, nz)
-    rel = (p.cd, p.cx, p.cy, p.c)
-
-    def pair_copy(c, z):
-        other = c * (2 * nz) + z * 2 + 1 - p.k
+class Combine:
+    def __init__(self, p, nz, cap, col, rows, slots, gates, out, *scratch):
+        self.p, self.nz, self.cap, self.rows, self.slots, self.gates = p, nz, cap, rows, slots, gates
+        self.out = out
+        self.rbuf, self.sd, self.sx, self.sy = scratch[:4]
+        self.h0, self.h1, self.bx, self.by, self.bz = scratch[4:9]
+        self.pair_send, self.pair_recv, self.load = scratch[9:12]
+        self.s_h0, self.s_h1, self.s_x, self.s_y, self.s_z = scratch[12:17]
+        self.r_h0, self.r_h1, self.r_x, self.r_y, self.r_z = scratch[17:]
+        self.order = pick_order(p, nz)
+        self.seq, self.width = self.sx.shape[1:]
+        self.half = self.seq // 2
+        self.cols = pl.ds(col, self.width)
+
+    def clear(self):
+        bz, nz = self.bz, self.nz
+
+        @pl.when(self.p.z == 0)
+        def _():
+            bz[pl.ds(0, nz)] = jnp.zeros((nz,) + bz.shape[1:], bz.dtype)
+
+        @pl.when(self.p.z == nz - 1)
+        def _():
+            bz[pl.ds(0, nz - 1)] = jnp.zeros((nz - 1,) + bz.shape[1:], bz.dtype)
+            bz[nz] = jnp.zeros(bz.shape[1:], bz.dtype)
+
+    def pair_copy(self, c, z):
+        p = self.p
         return remote(
-            rows.at[other],
-            rbuf.at[c, z, pl.ds(cap, cap)],
-            pair_send.at[c, z],
-            pair_recv.at[c, z],
+            self.rows.at[c * (2 * self.nz) + z * 2 + 1 - p.k, :, self.cols],
+            self.rbuf.at[c, z, pl.ds(self.cap, self.cap)],
+            self.pair_send.at[c, z],
+            self.pair_recv.at[c, z],
             p.pair,
         )
 
-    def load_copy(c, z):
+    def load_copy(self, c, z):
         return pltpu.make_async_copy(
-            rows.at[c * (2 * nz) + z * 2 + p.k], rbuf.at[c, z, pl.ds(0, cap)], load.at[c, z]
+            self.rows.at[c * (2 * self.nz) + z * 2 + self.p.k, :, self.cols],
+            self.rbuf.at[c, z, pl.ds(0, self.cap)],
+            self.load.at[c, z],
         )
 
-    for z in order:
-        for c in rel:
-            load_copy(c, z).start()
-            pair_copy(c, z).start()
-
-    def ready(c, z):
-        b = c * (2 * nz) + z * 2 + p.k
-        both = [jnp.where(names == slots[n, b], gates[n, b], 0.0) for n in (0, 1)]
-        w[c, z] = jnp.concatenate(both, axis=0).T.astype(bf16)
-        load_copy(c, z).wait()
-        pair_copy(c, z).wait_recv()
-
-    def fill(c, z, low, high, store):
-        for t in range(width // tile):
+    def begin(self):
+        p = self.p
+        for z in self.order:
+            for c in (p.cd, p.cx, p.cy, p.c):
+                self.load_copy(c, z).start()
+                self.pair_copy(c, z).start()
+
+    def fill(self, c, z, low, high, store):
+        half = self.half
+        b = pl.ds(c * (2 * self.nz) + z * 2 + self.p.k, 1)
+        names = lax.broadcasted_iota(jnp.int32, (self.cap, self.seq), 0)
+        both = [jnp.where(names == self.slots[n, b], self.gates[n, b], 0.0) for n in (0, 1)]
+        w = jnp.concatenate(both, axis=0).T.astype(bf16)
+        self.load_copy(c, z).wait()
+        self.pair_copy(c, z).wait_recv()
+        tile = min(512, self.width)
+        for t in range(self.width // tile):
             cols = pl.ds(t * tile, tile)
-            total = jnp.dot(w[c, z], rbuf[c, z, :, cols], preferred_element_type=f32)
+            total = jnp.dot(w, self.rbuf[c, z, :, cols], preferred_element_type=f32)
             for first, adds in ((0, low), (half, high)):
                 part = total[first : first + half]
                 for ref, start in adds:
                     part = part + ref[pl.ds(start, half), cols].astype(f32)
                 store(pl.ds(first, half), cols, part)
 
-    def into(buf, z):
+    def into(self, buf, z):
         def store(lines, cols, total):
             buf[z, lines, cols] = total.astype(buf.dtype)
 
         return store
 
-    def copy_h0(z):
-        return remote(sd.at[z, pl.ds(0, half)], h0.at[z], s_h0.at[z], r_h0.at[z], p.dx)
-
-    def copy_h1(z):
-        return remote(sd.at[z, pl.ds(half, half)], h1.at[z], s_h1.at[z], r_h1.at[z], p.dy)
-
-    def copy_x(z):
-        return remote(sx.at[z], bx.at[z], s_x.at[z], r_x.at[z], p.dx)
-
-    def copy_y(z):
-        return remote(sy.at[z], by.at[z], s_y.at[z], r_y.at[z], p.dy)
-
-    def copy_up(z):
-        return remote(sz.at[z], bz.at[z], s_z.at[z], r_z.at[z], p.up)
-
-    def copy_down(z):
-        slot = jnp.where(z == p.z - 1, nz, z)
-        return remote(sz.at[z], bz.at[slot], s_z.at[z], r_z.at[slot], p.down)
-
-    def line_recv(slot):
-        remote(bz.at[slot], bz.at[slot], s_z.at[0], r_z.at[slot], p.pair).wait_recv()
-
-    def diagonal(z):
-        ready(p.cd, z)
-        fill(p.cd, z, [], [], into(sd, z))
-        copy_h0(z).start()
-        copy_h1(z).start()
-
-    def sides(z):
-        ready(p.cx, z)
-        copy_h1(z).wait_recv()
-        fill(p.cx, z, [], [(h1.at[z], 0)], into(sx, z))
-        copy_x(z).start()
-        ready(p.cy, z)
-        copy_h0(z).wait_recv()
-        fill(p.cy, z, [(h0.at[z], 0)], [], into(sy, z))
-        copy_y(z).start()
-
-    def mine(z, last):
-        ready(p.c, z)
-        copy_x(z).wait_recv()
-        copy_y(z).wait_recv()
-        arrived = [bx.at[z], by.at[z], bz.at[z]]
+    def copy_h0(self, z):
+        src = self.sd.at[z, pl.ds(0, self.half)]
+        return remote(src, self.h0.at[z], self.s_h0.at[z], self.r_h0.at[z], self.p.dx)
+
+    def copy_h1(self, z):
+        src = self.sd.at[z, pl.ds(self.half, self.half)]
+        return remote(src, self.h1.at[z], self.s_h1.at[z], self.r_h1.at[z], self.p.dy)
+
+    def copy_x(self, z):
+        return remote(self.sx.at[z], self.bx.at[z], self.s_x.at[z], self.r_x.at[z], self.p.dx)
+
+    def copy_y(self, z):
+        return remote(self.sy.at[z], self.by.at[z], self.s_y.at[z], self.r_y.at[z], self.p.dy)
+
+    def copy_up(self, z):
+        return remote(self.sx.at[z], self.bz.at[z], self.s_z.at[z], self.r_z.at[z], self.p.up)
+
+    def copy_down(self, z):
+        slot = jnp.where(z == self.p.z - 1, self.nz, z)
+        return remote(
+            self.sx.at[z], self.bz.at[slot], self.s_z.at[z], self.r_z.at[slot], self.p.down
+        )
+
+    def line_recv(self, slot):
+        ref = self.bz.at[slot]
+        remote(ref, ref, self.s_z.at[0], self.r_z.at[slot], self.p.pair).wait_recv()
+
+    def diagonal(self, i):
+        z = self.order[i]
+        self.fill(self.p.cd, z, [], [], self.into(self.sd, z))
+        self.copy_h0(z).start()
+        self.copy_h1(z).start()
+
+    def sides(self, i):
+        z = self.order[i]
+        self.copy_h1(z).wait_recv()
+        self.fill(self.p.cx, z, [], [(self.h1.at[z], 0)], self.into(self.sx, z))
+        self.copy_x(z).start()
+        self.copy_h0(z).wait_recv()
+        self.fill(self.p.cy, z, [(self.h0.at[z], 0)], [], self.into(self.sy, z))
+        self.copy_y(z).start()
+
+    def mine(self, i):
+        p, nz, z, last = self.p, self.nz, self.order[i], i == self.nz - 1
+        self.copy_x(z).wait_recv()
+        self.copy_y(z).wait_recv()
+        self.copy_x(z).wait_send()
+        arrived = [self.bx.at[z], self.by.at[z], self.bz.at[z]]
         if last:
 
             @pl.when(p.z > 0)
             def _():
-                line_recv(z)
+                self.line_recv(z)
 
             @pl.when(p.z < nz - 1)
             def _():
-                line_recv(nz)
+                self.line_recv(nz)
 
             def store(lines, cols, total):
-                out[lines, cols] = total
-
-            arrived.append(bz.at[nz])
+                self.out[lines, cols] = total
+
+            arrived.append(self.bz.at[nz])
         else:
 
             @pl.when(((z > p.z) & (p.z > 0)) | ((z < p.z) & (p.z < nz - 1)))
             def _():
-                line_recv(z)
-
-            store = into(sz, z)
-        fill(
-            p.c, z, [(ref, 0) for ref in arrived], [(ref, half) for ref in arrived], store
-        )
+                self.line_recv(z)
+
+            store = self.into(self.sx, z)
+        lower, upper = [(ref, 0) for ref in arrived], [(ref, self.half) for ref in arrived]
+        self.fill(p.c, z, lower, upper, store)
         if not last:
 
             @pl.when(z > p.z)
             def _():
-                copy_up(z).start()
+                self.copy_up(z).start()
 
             @pl.when(z < p.z)
             def _():
-                copy_down(z).start()
-
-    diagonal(order[0])
-    if nz > 1:
-        diagonal(order[1])
-    for i in range(nz):
-        sides(order[i])
-        if i + 2 < nz:
-            diagonal(order[i + 2])
-        if i > 0:
-            mine(order[i - 1], False)
-    mine(order[nz - 1], True)
-
-    for i, z in enumerate(order):
-        for c in rel:
-            pair_copy(c, z).wait_send()
-        for copy in (copy_h0(z), copy_h1(z), copy_x(z), copy_y(z)):
-            copy.wait_send()
-        if i < nz - 1:
-            copy_up(z).wait_send()
-
-
-def combine(nz, rows, slots, gates, collective_id):
-    blocks, cap, width = rows.shape
-    seq = slots.shape[3]
+                self.copy_down(z).start()
+
+    def steps(self):
+        nz = self.nz
+        found = [(self.diagonal, 0)] + [(self.diagonal, 1)] * (nz > 1)
+        for i in range(nz):
+            found.append((self.sides, i))
+            if i + 2 < nz:
+                found.append((self.diagonal, i + 2))
+            if i > 0:
+                found.append((self.mine, i - 1))
+        found.append((self.mine, nz - 1))
+        return [functools.partial(act, i) for act, i in found]
+
+    def finish(self):
+        p = self.p
+        for i, z in enumerate(self.order):
+            for c in (p.cd, p.cx, p.cy, p.c):
+                self.pair_copy(c, z).wait_send()
+            for copy in (self.copy_h0(z), self.copy_h1(z), self.copy_y(z)):
+                copy.wait_send()
+            if i < self.nz - 1:
+                self.copy_up(z).wait_send()
+
+
+def combine_scratch(nz, cap, seq, width):
     dma = pltpu.SemaphoreType.DMA
     buf = lambda n, r: pltpu.VMEM((n, r, width), bf16)
+    return (
+        [pltpu.VMEM((4, nz, 2 * cap, width), bf16)]
+        + [buf(nz, seq)] * 3
+        + [buf(nz, seq // 2)] * 2
+        + [buf(nz, seq)] * 2
+        + [buf(nz + 1, seq)]
+        + [dma((4, nz))] * 3
+        + [dma((nz,))] * 9
+        + [dma((nz + 1,))]
+    )
+
+
+def combine_kernel(nz, cap, rows, slots, gates, out, *scratch):
+    p = Place()
+    job = Combine(p, nz, cap, 0, rows, slots, gates, out, *scratch)
+    job.clear()
+    greet(p, nz)
+    job.begin()
+    for step in job.steps():
+        step()
+    job.finish()
+
+
+def combine(nz, rows, slots, gates, collective_id):
+    _, cap, width = rows.shape
+    seq = slots.shape[2]
     return pl.pallas_call(
         functools.partial(combine_kernel, nz, cap),
         out_shape=jax.ShapeDtypeStruct((seq, width), f32),
         in_specs=[ANY, IN_VMEM, IN_VMEM],
         out_specs=IN_VMEM,
-        scratch_shapes=[
-            pltpu.VMEM((4, nz, 2 * cap, width), bf16),
-            pltpu.VMEM((4, nz, seq, 2 * cap), bf16),
-        ]
-        + [buf(nz, seq)] * 4
-        + [buf(nz, seq // 2)] * 2
-        + [buf(nz, seq)] * 2
-        + [buf(nz + 1, seq)]
-        + [dma((4, nz))] * 3
-        + [dma((nz,))] * 9
-        + [dma((nz + 1,))],
+        scratch_shapes=combine_scratch(nz, cap, seq, width),
         compiler_params=pltpu.CompilerParams(
             collective_id=collective_id, has_side_effects=True, vmem_limit_bytes=VMEM_BYTES
         ),
     )(rows, slots, gates)
 
 
-def fold_kernel(parts, out, sx, sy, h0, h1, bx, by, send, recv):
+def rms_back(x, gain, grad):
+    r = lax.rsqrt(jnp.mean(x * x, axis=-1, keepdims=True) + epsilon)
+    scaled = gain * grad
+    mean = jnp.mean(x * scaled, axis=-1, keepdims=True)
+    by_gain = jnp.sum(x * r * grad, axis=0, keepdims=True)
+    return r * scaled - x * (r * r * r * mean), by_gain
+
+
+def back_kernel(nz, cap, scale, *refs):
+    branch, wos, packs, xn, raw, q, ot, rows = refs[:8]
+    k, v, lse, cosine, sine, head_gain, slots, gates = refs[8:16]
+    gwo, gw, part, head_grad, mixed = refs[16:21]
+    rows_v, wo_v, w_v, raw_v, q_v, ot_v, do, kt, low, dq, dk, dv, wo_stage, w_stage = refs[21:35]
+    load, wo_sem, w_sem = refs[35:38]
     p = Place()
-    greet(p, 1, line=False, pair=False)
-    half = out.shape[0] // 2
-    low, high = pl.ds(0, half), pl.ds(half, half)
-    to_x = remote(parts.at[p.cd, low], h0, send.at[0], recv.at[0], p.dx)
-    to_y = remote(parts.at[p.cd, high], h1, send.at[1], recv.at[1], p.dy)
-    x_low = remote(parts.at[p.cx, low], bx.at[low], send.at[2], recv.at[2], p.dx)
-    y_high = remote(parts.at[p.cy, high], by.at[high], send.at[3], recv.at[3], p.dy)
-    x_high = remote(sx, bx.at[high], send.at[4], recv.at[4], p.dx)
-    y_low = remote(sy, by.at[low], send.at[5], recv.at[5], p.dy)
-    copies = (to_x, to_y, x_low, y_high, x_high, y_low)
-    for copy in copies[:4]:
+    combine = Combine(p, nz, cap, 0, rows, slots, gates, mixed, *refs[38:])
+    length, wide = raw.shape
+    heads = q.shape[0]
+    seq = length // 4
+    width = part.shape[2]
+    loads = [
+        pltpu.make_async_copy(src, dst, load.at[i])
+        for i, (src, dst) in enumerate(
+            ((branch, rows_v), (wos, wo_v), (q, q_v), (ot, ot_v), (packs, w_v))
+        )
+    ]
+    load_xn = pltpu.make_async_copy(xn, rows_v, load.at[5])
+
+    def load_raw(cols):
+        return pltpu.make_async_copy(raw.at[:, cols], raw_v, load.at[6])
+
+    for copy in loads:
         copy.start()
-    to_y.wait_recv()
-    sx[...] = (parts[p.cx, high].astype(f32) + h1[...].astype(f32)).astype(sx.dtype)
-    x_high.start()
-    to_x.wait_recv()
-    sy[...] = (parts[p.cy, low].astype(f32) + h0[...].astype(f32)).astype(sy.dtype)
-    y_low.start()
-    x_low.wait_recv()
-    y_low.wait_recv()
-    out[low] = parts[p.c, low].astype(f32) + bx[low].astype(f32) + by[low].astype(f32)
-    y_high.wait_recv()
-    x_high.wait_recv()
-    out[high] = parts[p.c, high].astype(f32) + bx[high].astype(f32) + by[high].astype(f32)
-    for copy in copies:
-        copy.wait_send()
-
-
-def fold(parts, collective_id):
-    _, seq, width = parts.shape
-    buf = lambda r: pltpu.VMEM((r, width), parts.dtype)
+    combine.clear()
+    greet(p, nz)
+    combine.begin()
+    steps = combine.steps()
+    run = lambda n: [steps.pop(0)() for _ in range(min(n, len(steps)))]
+    kt[...] = k[...].astype(f32).T.astype(bf16)
+    run(2)
+    loads[0].wait()
+    loads[1].wait()
+
+    @pl.loop(0, heads * HD // 256)
+    def _(t):
+        cols = pl.ds(pl.multiple_of(t * 256, 256), 256)
+        w = wo_v[pl.ds(t * (256 // wo_v.shape[1]), 256 // wo_v.shape[1])].reshape(256, width)
+        out = lax.dot_general(rows_v[...].reshape(length, width), w, NT, preferred_element_type=f32)
+        do[:, cols] = out.astype(bf16)
+
+    run(1)
+    loads[2].wait()
+    loads[3].wait()
+    dk[...] = jnp.zeros(dk.shape, f32)
+    dv[...] = jnp.zeros(dv.shape, f32)
+    head_grad[...] = jnp.zeros(head_grad.shape, f32)
+
+    def unprep(x, gain, grad):
+        grad = grad * cosine[...] + pltpu.roll(grad * sine[...], HD // 2, 1)
+        return rms_back(x, gain, grad)
+
+    def attend(h):
+        cols = pl.ds(pl.multiple_of(h * HD, HD), HD)
+        load_raw(cols).start()
+        for i in range(length // seq):
+            keys = pl.ds(0, (i + 1) * seq)
+            here = pl.ds(i * seq, seq)
+            s = lax.dot_general(k[keys], q_v[h, here], NT, preferred_element_type=f32) * scale
+            key_pos = lax.broadcasted_iota(jnp.int32, s.shape, 0)
+            query_pos = lax.broadcasted_iota(jnp.int32, s.shape, 1) + i * seq
+            probs = jnp.where(key_pos <= query_pos, jnp.exp(s - lse[h, :, here]), 0.0)
+            dp = lax.dot_general(v[keys], do[here, cols], NT, preferred_element_type=f32)
+            delta = jnp.sum(probs * dp, axis=0, keepdims=True)
+            ds = (probs * (dp - delta)).astype(bf16)
+            dk[keys] += jnp.dot(ds, q_v[h, here], preferred_element_type=f32) * scale
+            dv[keys] += jnp.dot(probs.astype(bf16), do[here, cols], preferred_element_type=f32)
+            dq[here] = (jnp.dot(kt[:, keys], ds, preferred_element_type=f32) * scale).T
+        load_raw(cols).wait()
+        by_x, by_gain = unprep(raw_v[...], head_gain[0:1], dq[...])
+        low[:, cols] = by_x.astype(bf16)
+        head_grad[0:1] += by_gain
+
+    for first in range(0, heads, 2):
+        pl.loop(first, first + 2)(attend)
+        run(1)
+    load_raw(pl.ds(heads * HD, HD)).start()
+    load_raw(pl.ds(heads * HD, HD)).wait()
+    by_x, by_gain = unprep(raw_v[...], head_gain[1:2], dk[...])
+    low[:, pl.ds(heads * HD, HD)] = by_x.astype(bf16)
+    head_grad[1:2] = by_gain
+    low[:, pl.ds((heads + 1) * HD, HD)] = dv[...].astype(bf16)
+
+    tile = wo_stage.shape[3]
+    wo_out = lambda t: pltpu.make_async_copy(
+        wo_stage.at[t % 2], gwo.at[:, :, pl.ds(t * tile, tile)], wo_sem.at[t % 2]
+    )
+    for t in range(width // tile):
+        if t >= 2:
+            wo_out(t - 2).wait()
+        out = jnp.dot(
+            ot_v[...].reshape(heads * HD, length),
+            rows_v[:, :, pl.ds(t * tile, tile)].reshape(length, tile),
+            preferred_element_type=f32,
+        )
+        wo_stage[t % 2] = out.astype(bf16).reshape(wo_stage.shape[1:])
+        wo_out(t).start()
+        if t % 2:
+            run(1)
+    load_xn.start()
+    loads[4].wait()
+    for c in range(4):
+        w = w_v[c].reshape(width // 4, wide)
+        out = lax.dot_general(low[...], w, NT, preferred_element_type=f32)
+        part[:, :, pl.ds(c * (width // 4), width // 4)] = out.astype(bf16).reshape(
+            4, seq, width // 4
+        )
+        if c % 2:
+            run(1)
+    load_xn.wait()
+    lines = w_stage.shape[1] * w_stage.shape[2]
+
+    def w_out(t):
+        first = t * w_stage.shape[1]
+        c, e = first // (2 * nz), first % (2 * nz)
+        return pltpu.make_async_copy(
+            w_stage.at[t % 2], gw.at[c, pl.ds(e, w_stage.shape[1])], w_sem.at[t % 2]
+        )
+
+    for t in range(width // lines):
+        if t >= 2:
+            w_out(t - 2).wait()
+        x = rows_v[:, :, pl.ds(t * lines, lines)].reshape(length, lines)
+        out = lax.dot_general(x, low[...], TN, preferred_element_type=f32)
+        w_stage[t % 2] = out.astype(bf16).reshape(w_stage.shape[1:])
+        w_out(t).start()
+        if t % 3 == 2:
+            run(1)
+    run(len(steps))
+    for t in range(2):
+        wo_out(width // tile - 2 + t).wait()
+        w_out(width // lines - 2 + t).wait()
+    combine.finish()
+
+
+def back(nz, scale, columns, branch, wos, packs, xn, raw, q, ot, rows, k, v, lse, cosine, sine, head_gain, slots, gates):
+    length, wide = raw.shape
+    heads = q.shape[0]
+    seq = length // 4
+    width = xn.shape[1]
+    cap = rows.shape[1]
+    shape = jax.ShapeDtypeStruct
+    vmem = lambda *n: pltpu.VMEM(n, bf16)
+    wide_f = lambda *n: pltpu.VMEM(n, f32)
+    dma = pltpu.SemaphoreType.DMA
     return pl.pallas_call(
-        fold_kernel,
-        out_shape=jax.ShapeDtypeStruct((seq, width), f32),
-        in_specs=[IN_VMEM],
-        out_specs=IN_VMEM,
-        scratch_shapes=[buf(seq // 2)] * 4
-        + [buf(seq)] * 2
-        + [pltpu.SemaphoreType.DMA((6,))] * 2,
+        functools.partial(back_kernel, nz, cap, scale),
+        out_shape=[
+            shape(wos.shape, bf16),
+            shape(packs.shape, bf16),
+            shape((4, seq, width), bf16),
+            shape((2, HD), f32),
+            shape((seq, columns), f32),
+        ],
+        in_specs=[ANY] * 8 + [IN_VMEM] * 8,
+        out_specs=[ANY] * 2 + [IN_VMEM] * 3,
+        scratch_shapes=[
+            vmem(4, seq, width),
+            vmem(*wos.shape),
+            vmem(*packs.shape),
+            wide_f(length, HD),
+            vmem(*q.shape),
+            vmem(*ot.shape),
+            vmem(length, heads * HD),
+            vmem(HD, length),
+            vmem(length, wide),
+            wide_f(length, HD),
+            wide_f(length, HD),
+            wide_f(length, HD),
+            vmem(2, wos.shape[0], wos.shape[1], 256),
+            vmem(2, 4, packs.shape[2], wide),
+            dma((7,)),
+            dma((2,)),
+            dma((2,)),
+        ]
+        + combine_scratch(nz, cap, seq, columns),
         compiler_params=pltpu.CompilerParams(
-            collective_id=collective_id, has_side_effects=True, vmem_limit_bytes=VMEM_BYTES
+            collective_id=5, has_side_effects=True, vmem_limit_bytes=VMEM_BYTES
         ),
-    )(parts)
-
-
-def last_kernel(nz, gq, go, gains, oq, ok, ov, oo, all_gains, *scratch):
-    own_q, own_o, sib_q, sib_o, s_q, s_o, b_q, b_o, swap_s, swap_r, scratch = (
-        *scratch[:10],
-        scratch[10:],
-    )
-    load, pair_s, pair_r, line_s, line_r, a_send, a_recv, g_send, g_recv, local = scratch
+    )(branch, wos, packs, xn.reshape(4, seq, width), raw, q, ot, rows, k, v, lse, cosine, sine, head_gain, slots, gates)
+
+
+def last_kernel(nz, cap, col, *refs):
+    gq, go, rows, part, tok, dh, gains, mlp_grad, head_grad, slots, gates = refs[:11]
+    oq, ok, ov, oo, all_gains, grad_tokens, mixed = refs[11:18]
+    own_q, own_o, sib_q, sib_o, b_q, b_o, swap_s, swap_r, gain_v = refs[18:27]
+    load, pair_s, pair_r, line_s, line_r, a_send, a_recv, g_send, g_recv, local = refs[27:37]
     p = Place()
     order = pick_order(p, nz)
+    fold = Fold(p, part, *refs[37:45])
+    combine = Combine(p, nz, cap, col, rows, slots, gates, mixed, *refs[45:])
 
     @pl.when(p.z == 0)
     def _():
@@ -904,92 +1340,127 @@
             ref[pl.ds(0, nz - 1)] = jnp.zeros((nz - 1,) + ref.shape[1:], ref.dtype)
             ref[nz] = jnp.zeros(ref.shape[1:], ref.dtype)
 
+    combine.clear()
     greet(p, nz, diagonal=True)
-    keep = pltpu.make_async_copy(gains, all_gains.at[p.c * (2 * nz) + p.e], local)
-    keep.start()
-    job = Spread(p, nz, gains, by_device(all_gains, nz), gains.shape[0] // 2, g_send, g_recv)
     arrays = (
-        (0, lambda z, k: gq.at[:, z * 2 + k], own_q, sib_q, s_q, b_q),
-        (1, lambda z, k: go.at[z * 2 + k], own_o, sib_o, s_o, b_o),
+        (0, lambda z, k: gq.at[:, z * 2 + k], own_q, sib_q, b_q),
+        (1, lambda z, k: go.at[z * 2 + k], own_o, sib_o, b_o),
     )
 
     def load_copy(i, z):
-        _, part, own, _, _, _ = arrays[i]
+        _, part, own, _, _ = arrays[i]
         return pltpu.make_async_copy(part(z, p.k), own.at[z], load.at[i, z])
 
     def pair_copy(i, z):
-        _, part, _, sib, _, _ = arrays[i]
+        _, part, _, sib, _ = arrays[i]
         return remote(part(z, 1 - p.k), sib.at[z], pair_s.at[i, z], pair_r.at[i, z], p.pair)
 
     def copy_up(i, z):
-        _, _, _, _, s, b = arrays[i]
+        _, _, s, _, b = arrays[i]
         return remote(s.at[z], b.at[z], line_s.at[i, z], line_r.at[i, z], p.up)
 
     def copy_down(i, z):
-        _, _, _, _, s, b = arrays[i]
+        _, _, s, _, b = arrays[i]
         slot = jnp.where(z == p.z - 1, nz, z)
         return remote(s.at[z], b.at[slot], line_s.at[i, z], line_r.at[i, slot], p.down)
 
     def line_recv(i, slot):
-        b = arrays[i][5]
+        b = arrays[i][4]
         remote(b.at[slot], b.at[slot], line_s.at[i, 0], line_r.at[i, slot], p.pair).wait_recv()
 
+    def swaps():
+        return [
+            remote(swap_s.at[c], swap_r.at[p.c], a_send.at[n], a_recv.at[n], device)
+            for n, (c, device) in enumerate(((p.cx, p.dx), (p.cy, p.dy), (p.cd, p.dd)))
+        ]
+
+    def reduce(i, n):
+        z, last = order[n], n == nz - 1
+        _, _, own, sib, b = arrays[i]
+        load_copy(i, z).wait()
+        pair_copy(i, z).wait_recv()
+        if last:
+
+            @pl.when(p.z > 0)
+            def _():
+                line_recv(i, z)
+
+            @pl.when(p.z < nz - 1)
+            def _():
+                line_recv(i, nz)
+
+            total = own[z].astype(f32) + sib[z].astype(f32) + b[z].astype(f32)
+            total = total + b[nz].astype(f32)
+            if i:
+                oo[...] = total
+            else:
+                swap_s[...] = total.astype(swap_s.dtype)
+                for copy in swaps():
+                    copy.start()
+                swap_r[p.c] = swap_s[p.c]
+            return
+
+        @pl.when(((z > p.z) & (p.z > 0)) | ((z < p.z) & (p.z < nz - 1)))
+        def _():
+            line_recv(i, z)
+
+        total = own[z].astype(f32) + sib[z].astype(f32) + b[z].astype(f32)
+        own[z] = total.astype(own.dtype)
+
+        @pl.when(z > p.z)
+        def _():
+            copy_up(i, z).start()
+
+        @pl.when(z < p.z)
+        def _():
+            copy_down(i, z).start()
+
+    fold.begin()
     for z in order:
-        for i in (0, 1):
+        for i in (1, 0):
             pair_copy(i, z).start()
             load_copy(i, z).start()
-    for far in range(nz + 2):
-        job.step(far)
-        if far >= nz:
-            continue
-        z, last = order[far], far == nz - 1
-        for i in (0, 1):
-            _, _, own, sib, s, b = arrays[i]
-            load_copy(i, z).wait()
-            pair_copy(i, z).wait_recv()
-            if last:
-
-                @pl.when(p.z > 0)
-                def _():
-                    line_recv(i, z)
-
-                @pl.when(p.z < nz - 1)
-                def _():
-                    line_recv(i, nz)
-
-                total = own[z].astype(f32) + sib[z].astype(f32) + b[z].astype(f32)
-                total = total + b[nz].astype(f32)
-                if i:
-                    oo[...] = total
-                else:
-                    swap_s[...] = total.astype(swap_s.dtype)
-            else:
-
-                @pl.when(((z > p.z) & (p.z > 0)) | ((z < p.z) & (p.z < nz - 1)))
-                def _():
-                    line_recv(i, z)
-
-                total = own[z].astype(f32) + sib[z].astype(f32) + b[z].astype(f32)
-                s[z] = total.astype(s.dtype)
-
-                @pl.when(z > p.z)
-                def _():
-                    copy_up(i, z).start()
-
-                @pl.when(z < p.z)
-                def _():
-                    copy_down(i, z).start()
-
-            if last and i == 0:
-                swaps = [
-                    remote(
-                        swap_s.at[c], swap_r.at[p.c], a_send.at[n], a_recv.at[n], device
-                    )
-                    for n, (c, device) in enumerate(((p.cx, p.dx), (p.cy, p.dy), (p.cd, p.dd)))
-                ]
-                for copy in swaps:
-                    copy.start()
-                swap_r[p.c] = swap_s[p.c]
+    combine.begin()
+    steps = combine.steps()
+    run = lambda n: [steps.pop(0)() for _ in range(min(n, len(steps)))]
+    reduce(1, 0)
+    reduce(0, 0)
+    run(1)
+    fold.middle()
+    run(1)
+    reduce(1, 1)
+    reduce(0, 1)
+    run(1)
+
+    half = tok.shape[0] // 2
+    gain_v[...] = jnp.zeros(gain_v.shape, f32)
+    width = tok.shape[1]
+
+    def store(lines, total):
+        by_x, by_gain = rms_back(tok[lines].astype(f32), gains[0:1], total)
+        grad_tokens[lines] = (dh[lines] + by_x).astype(bf16)
+        for j in range(width // 128):
+            gain_v[pl.ds(j, 1)] += by_gain[:, j * 128 : (j + 1) * 128]
+
+    fold.end(store)
+    for j in range(width // 128):
+        gain_v[pl.ds(width // 128 + j, 1)] = mlp_grad[:, pl.ds(j * 128, 128)]
+    gain_v[pl.ds(2 * width // 128, 2)] = head_grad[...]
+    block = by_device(all_gains, nz)
+    keep = pltpu.make_async_copy(gain_v, block(p.c, p.z, p.k), local)
+    keep.start()
+    job = Spread(p, nz, gain_v, block, gain_v.shape[0] // 2, g_send, g_recv)
+    job.step(0)
+    run(1)
+    job.step(1)
+    for n in range(2, nz):
+        reduce(1, n)
+        reduce(0, n)
+        run(2)
+        job.step(n)
+    for i in range(nz, nz + 2):
+        job.step(i)
+        run(1)
     for n, c in enumerate((p.cx, p.cy, p.cd)):
         ref = swap_r.at[c]
         remote(ref, ref, a_send.at[n], a_recv.at[n], p.dx).wait_recv()
@@ -999,7 +1470,8 @@
         oq[:, pl.ds(c * heads, heads)] = swap_r[c, :, pl.ds(0, heads)].astype(f32)
         ok[:, pl.ds(c * kv, kv)] = swap_r[c, :, pl.ds(heads, kv)].astype(f32)
         ov[:, pl.ds(c * kv, kv)] = swap_r[c, :, pl.ds(heads + kv, kv)].astype(f32)
-    for copy in swaps:
+    run(len(steps))
+    for copy in swaps():
         copy.wait_send()
     for n, z in enumerate(order):
         for i in (0, 1):
@@ -1008,130 +1480,47 @@
                 copy_up(i, z).wait_send()
     keep.wait()
     job.finish()
-
-
-def reduce_last(nz, gq, go, gains):
+    combine.finish()
+
+
+def reduce_last(nz, col, gq, go, rows, part, tok, dh, gains, mlp_grad, head_grad, slots, gates):
     _, _, rows_q, wide = gq.shape
     _, rows_o, width = go.shape
+    cap = rows.shape[1]
+    seq = tok.shape[0]
     kv = HD
     heads = wide - 2 * kv
+    lines = -(-(2 * width // 128 + 2) // 16) * 16
     dma = pltpu.SemaphoreType.DMA
     shape = jax.ShapeDtypeStruct
     q = lambda *n: pltpu.VMEM(n + (4, rows_q, wide), bf16)
     o = lambda *n: pltpu.VMEM(n + (rows_o, width), bf16)
     return pl.pallas_call(
-        functools.partial(last_kernel, nz),
+        functools.partial(last_kernel, nz, cap, col),
         out_shape=[
             shape((rows_q, 4 * heads), f32),
             shape((rows_q, 4 * kv), f32),
             shape((rows_q, 4 * kv), f32),
             shape((rows_o, width), f32),
-            shape((8 * nz,) + gains.shape, f32),
+            shape((8 * nz, lines, 128), f32),
+            shape((seq, width), bf16),
+            shape((seq, width - col), f32),
         ],
-        in_specs=[ANY] * 3,
-        out_specs=[IN_VMEM] * 4 + [ANY],
-        scratch_shapes=[q(nz), o(nz), q(nz), o(nz), q(nz), o(nz), q(nz + 1), o(nz + 1), q(), q()]
+        in_specs=[ANY] * 3 + [IN_VMEM] * 8,
+        out_specs=[IN_VMEM] * 4 + [ANY] + [IN_VMEM] * 2,
+        scratch_shapes=[q(nz), o(nz), q(nz), o(nz), q(nz + 1), o(nz + 1), q(), q()]
+        + [pltpu.VMEM((lines, 128), f32)]
         + [dma((2, nz))] * 4
         + [dma((2, nz + 1))]
         + [dma((3,))] * 2
         + spread_sems(nz)
-        + [dma],
+        + [dma]
+        + fold_scratch(seq, width)
+        + combine_scratch(nz, cap, seq, width - col),
         compiler_params=pltpu.CompilerParams(
             collective_id=9, has_side_effects=True, vmem_limit_bytes=VMEM_BYTES
         ),
-    )(gq, go, gains)
-
-
-def attend_kernel(scale, span, q, k, vt, ot, lse):
-    for i in range(q.shape[1] // span):
-        keys = (i + 1) * span
-        here = pl.ds(i * span, span)
-        s = lax.dot_general(
-            k[pl.ds(0, keys)], q[0, here], (((1,), (1,)), ((), ())), preferred_element_type=f32
-        )
-        s = s * scale
-        key_pos = lax.broadcasted_iota(jnp.int32, s.shape, 0)
-        query_pos = lax.broadcasted_iota(jnp.int32, s.shape, 1) + i * span
-        s = jnp.where(key_pos <= query_pos, s, masked_value)
-        largest = jnp.max(s, axis=0, keepdims=True)
-        weights = jnp.exp(s - largest)
-        total = jnp.sum(weights, axis=0, keepdims=True)
-        o = jnp.dot(vt[:, pl.ds(0, keys)], weights.astype(bf16), preferred_element_type=f32)
-        ot[0, :, here] = (o / total).astype(bf16)
-        lse[0, :, here] = largest + jnp.log(total)
-
-
-def attend(q, k, vt, scale):
-    heads, length, hd = q.shape
-    shape = jax.ShapeDtypeStruct
-    return pl.pallas_call(
-        functools.partial(attend_kernel, scale, length // 4),
-        grid=(heads,),
-        out_shape=[shape((heads, hd, length), bf16), shape((heads, 1, length), f32)],
-        in_specs=[
-            pl.BlockSpec((1, length, hd), lambda h: (h, 0, 0)),
-            pl.BlockSpec((length, hd), lambda h: (0, 0)),
-            pl.BlockSpec((hd, length), lambda h: (0, 0)),
-        ],
-        out_specs=[
-            pl.BlockSpec((1, hd, length), lambda h: (h, 0, 0)),
-            pl.BlockSpec((1, 1, length), lambda h: (h, 0, 0)),
-        ],
-        compiler_params=pltpu.CompilerParams(vmem_limit_bytes=32 * 2**20),
-    )(q, k, vt)
-
-
-def attend_back_kernel(scale, span, q, k, kt, v, do, lse, dq, dk, dv):
-    @pl.when(pl.program_id(0) == 0)
-    def _():
-        dk[...] = jnp.zeros(dk.shape, f32)
-        dv[...] = jnp.zeros(dv.shape, f32)
-
-    for i in range(q.shape[1] // span):
-        keys = pl.ds(0, (i + 1) * span)
-        here = pl.ds(i * span, span)
-        nt = (((1,), (1,)), ((), ()))
-        s = lax.dot_general(k[keys], q[0, here], nt, preferred_element_type=f32) * scale
-        key_pos = lax.broadcasted_iota(jnp.int32, s.shape, 0)
-        query_pos = lax.broadcasted_iota(jnp.int32, s.shape, 1) + i * span
-        probs = jnp.where(key_pos <= query_pos, jnp.exp(s - lse[0, :, here]), 0.0)
-        dp = lax.dot_general(v[keys], do[here], nt, preferred_element_type=f32)
-        delta = jnp.sum(probs * dp, axis=0, keepdims=True)
-        ds = (probs * (dp - delta)).astype(bf16)
-        dk[keys] += jnp.dot(ds, q[0, here], preferred_element_type=f32) * scale
-        dv[keys] += jnp.dot(probs.astype(bf16), do[here], preferred_element_type=f32)
-        part = jnp.dot(kt[:, keys], ds, preferred_element_type=f32) * scale
-        dq[here] = part.T
-
-
-def attend_back(q, k, v, do, lse, scale):
-    heads, length, hd = q.shape
-    shape = jax.ShapeDtypeStruct
-    whole = pl.BlockSpec((length, hd), lambda h: (0, 0))
-    column = pl.BlockSpec((length, hd), lambda h: (0, h))
-    return pl.pallas_call(
-        functools.partial(attend_back_kernel, scale, length // 4),
-        grid=(heads,),
-        out_shape=[
-            shape((length, heads * hd), f32),
-            shape((length, hd), f32),
-            shape((length, hd), f32),
-        ],
-        in_specs=[
-            pl.BlockSpec((1, length, hd), lambda h: (h, 0, 0)),
-            whole,
-            pl.BlockSpec((hd, length), lambda h: (0, 0)),
-            whole,
-            column,
-            pl.BlockSpec((1, 1, length), lambda h: (h, 0, 0)),
-        ],
-        out_specs=[column, whole, whole],
-        compiler_params=pltpu.CompilerParams(vmem_limit_bytes=32 * 2**20),
-    )(q, k, k.T, v, do, lse)
-
-
-NT = (((1,), (1,)), ((), ()))
-TN = (((0,), (0,)), ((), ()))
+    )(gq, go, rows, part, tok, dh, gains, mlp_grad, head_grad, slots, gates)
 
 
 def experts_kernel(
@@ -1163,7 +1552,6 @@
     du,
     send,
     recv,
-    local,
     load,
     out_sem,
     back_sem,
@@ -1171,8 +1559,6 @@
     p = Place()
     greet(p, nz)
     job = Spread(p, nz, mine, by_device(all_rows, nz), mine.shape[0] // 2, send, recv)
-    keep = pltpu.make_async_copy(mine, job.block(p.c, p.z, p.k), local)
-    keep.start()
     seq, width = mine.shape
     ff = a.shape[2]
     wide = min(512, width)
@@ -1185,8 +1571,10 @@
         c, other = lines[h][i]
         return c * (2 * nz) + z * 2 + lax.rem(p.k + other, 2)
 
-    def load_x(h, i, z):
-        return pltpu.make_async_copy(all_rows.at[index(h, i, z)], stage_x.at[i], load.at[0, i])
+    def load_x(n, i):
+        at, h = turns[n]
+        src = mine if n == i == 0 else all_rows.at[index(h, i, job.order[at])]
+        return pltpu.make_async_copy(src, stage_x.at[i], load.at[0, i])
 
     def load_d(n, i):
         at, h = turns[n]
@@ -1212,7 +1600,7 @@
         at, h = turns[n]
         z = job.order[at]
         for i in range(4):
-            load_x(h, i, z).start()
+            load_x(n, i).start()
         if n + 1 < len(turns):
             for i in range(4):
                 load_d(n + 1, i).start()
@@ -1220,15 +1608,16 @@
             for copy in outs(h, job.order[at - 1]):
                 copy.wait()
         for i in range(4):
-            names = lax.broadcasted_iota(jnp.int32, (cap, seq), 0) == slots[index(h, i, z)]
+            at_b = pl.ds(index(h, i, z), 1)
+            names = lax.broadcasted_iota(jnp.int32, (cap, seq), 0) == slots[0, at_b]
             chosen = names.astype(f32).astype(bf16)
-            row_gate = jnp.where(names, gates[index(h, i, z)], 0.0)
+            row_gate = jnp.where(names, gates[0, at_b], 0.0)
             row_gate = jnp.sum(row_gate, axis=1, keepdims=True)
             here = pl.ds(i * cap, cap)
             load_d(n, i).wait()
             picked = jnp.dot(chosen, stage_d[n % 2, i], preferred_element_type=f32)
             dr[h, here] = (row_gate * picked).astype(bf16)
-            load_x(h, i, z).wait()
+            load_x(n, i).wait()
             picked = jnp.dot(chosen, stage_x[i], preferred_element_type=f32)
             x[h, here] = picked.astype(bf16)
 
@@ -1266,8 +1655,6 @@
             job.beside(z)
             for j in (5, 6):
                 job.got(j, z)
-            if i == 1:
-                keep.wait()
             group(done)
             done += 1
         if i >= 2:
@@ -1303,7 +1690,7 @@
         + [vmem(2, rows, width)] * 4
         + [vmem(2, rows, ff)] * 3
         + spread_sems(nz)
-        + [dma, dma((3, 4)), dma((2, 5)), dma((2, 2, 4))],
+        + [dma((3, 4)), dma((2, 5)), dma((2, 2, 4))],
         compiler_params=pltpu.CompilerParams(
             collective_id=3, has_side_effects=True, vmem_limit_bytes=VMEM_BYTES
         ),
@@ -1342,7 +1729,6 @@
     e = lax.axis_index("expert")
     k = lax.rem(e, 2)
     me = c * (2 * nz) + e
-    rows_in = tokens.reshape(seq, width).astype(f32)
     rows_q = query_weight.shape[0]
 
     def cols(weight):
@@ -1351,71 +1737,46 @@
     pack = jnp.concatenate([cols(query_weight), cols(key_weight), cols(value_weight)], axis=2)
     share = norm_gains.shape[1]
     head_share = head_gains.shape[1]
-    parts = [
-        routes.reshape(seq, topk).T.astype(f32).reshape(-1),
-        route_gates.reshape(seq, topk).T.reshape(-1),
-        norm_gains.astype(f32).reshape(-1),
-        head_gains.astype(f32).reshape(-1),
-    ]
-    flat = jnp.concatenate(parts)
-    lines = -(-flat.shape[0] // (128 * 16)) * 16
-    meta = jnp.pad(flat, (0, lines * 128 - flat.shape[0])).reshape(lines, 128)
-    weight, wo, toks, cots, metas = gather_first(
+    lane = jnp.arange(128)
+
+    def placed(part, size):
+        spread = jnp.tile(part.astype(f32), (1, 128 // size))
+        return jnp.where(lane[None, :] // size == lax.rem(me, 128 // size), spread, 0.0)
+
+    meta = jnp.concatenate(
+        [
+            routes.reshape(seq, topk).T.astype(f32).reshape(-1, 128),
+            route_gates.reshape(seq, topk).T.reshape(-1, 128),
+            placed(norm_gains, share),
+            placed(head_gains, head_share),
+        ]
+    )
+    meta = jnp.pad(meta, ((0, -meta.shape[0] % 16), (0, 0)))
+    half = HD // 2
+    angles = jnp.arange(length, dtype=jnp.int32).astype(f32)[:, None] * (
+        rope_base ** (-jnp.arange(half, dtype=f32) / half)
+    )
+    cosine, sine = jnp.cos(angles), jnp.sin(angles)
+    tables = (
+        jnp.concatenate([cosine, cosine], axis=1),
+        jnp.concatenate([-sine, sine], axis=1),
+    )
+    found = front(
         nz,
+        scale,
         pack,
         output_weight,
         tokens.reshape(seq, width),
         cotangent.reshape(seq, width),
         meta,
-    )
-    weight = weight.reshape(width, -1)
-    wo = wo.reshape(-1, width)
-    metas = metas.reshape(devices, -1)
-    n = seq * topk
-    all_routes = metas[:, :n].reshape(devices, topk, seq)
-    all_gates = metas[:, n : 2 * n].reshape(devices, topk, seq)
-    at = 2 * n
-    gains = metas[:, at : at + 2 * share].reshape(devices, 2, share).transpose(1, 0, 2)
-    gains = gains.reshape(2, width)
-    at += 2 * share
-    head_gain = metas[:, at : at + 2 * head_share].reshape(devices, 2, head_share)
-    head_gain = head_gain.transpose(1, 0, 2).reshape(2, HD)
-
-    positions = jnp.arange(length, dtype=jnp.int32)
-    normed = rms_scale(toks.reshape(length, width).astype(f32), gains[0]).astype(bf16)
-    raw = mm(normed, weight, (1, 0))
-    query_raw = raw[:, :wq].reshape(length, heads, HD)
-    key_raw = raw[:, wq : wq + HD].reshape(length, 1, HD)
-    values = raw[:, wq + HD :].astype(bf16)
-
-    def head_prep(raw_heads, gain_vec):
-        return rotate(rms_scale(raw_heads, gain_vec), positions)
-
-    queries = head_prep(query_raw, head_gain[0]).astype(bf16).transpose(1, 0, 2)
-    keys = head_prep(key_raw, head_gain[1]).astype(bf16).reshape(length, HD)
-    attended, lse = attend(queries, keys, values.T, scale)
-    attended = attended.reshape(wq, length)
-    hidden = rows_in + fold(mm(attended, wo, (0, 0), bf16).reshape(4, seq, width), 2)
-    normed_mlp = rms_scale(hidden, gains[1]).astype(bf16)
-
-    def picks(expert):
-        named = all_routes == expert.astype(f32)
-        member = jnp.any(named, axis=1)
-        weight_of = jnp.sum(jnp.where(named, all_gates, 0.0), axis=1)
-        upto = jnp.arange(seq)[:, None] <= jnp.arange(seq)[None, :]
-        rank = jnp.dot(member.astype(bf16), upto.astype(bf16), preferred_element_type=f32)
-        slot = jnp.where(member, rank.astype(jnp.int32) - 1, -1)
-        return slot.reshape(devices, 1, seq), weight_of.reshape(devices, 1, seq)
-
-    slot, weight_of = picks(me)
-    slot_pair, weight_pair = picks(me + 1 - 2 * k)
-    slots2 = jnp.stack([slot, slot_pair])
-    gates2 = jnp.stack([weight_of, weight_pair])
+        *tables,
+    )
+    weight, wo, _, cots, _, normed, raw, queries, keys, values, attended, lse = found[:12]
+    hidden, normed_mlp, gains, head_gain, slots2, gates2 = found[12:]
     produced, grad_inputs, arrived, grad_arrived, activated, grad_gate_pre, grad_up_pre = run_experts(
-        nz, cap, normed_mlp, cots, slot, weight_of, expert_gate[0], expert_up[0], expert_down[0]
+        nz, cap, normed_mlp, cots, slots2, gates2, expert_gate[0], expert_up[0], expert_down[0]
     )
     grad_normed_mlp = combine(nz, grad_inputs, slots2, jnp.ones_like(gates2), 4)
-    mixed = hidden + combine(nz, produced, slots2, gates2, 5)
     arrived, grad_arrived, activated, grad_gate_pre, grad_up_pre = (
         a.reshape(devices * cap, -1)
         for a in (arrived, grad_arrived, activated, grad_gate_pre, grad_up_pre)
@@ -1428,46 +1789,50 @@
     _, norm_pull = jax.vjp(rms_scale, hidden, gains[1])
     grad_hidden_norm, grad_gain_mlp = norm_pull(grad_normed_mlp)
     grad_hidden = grad_out + grad_hidden_norm
-    branch = gather_rows(nz, False, grad_hidden.astype(bf16), 6).reshape(length, width)
-    grad_wo = mm(attended, branch, (1, 0), bf16)
-    grad_attended = mm(branch, wo, (1, 1), bf16)
-    grad_query, grad_key, grad_value = attend_back(
-        queries, keys, values, grad_attended, lse, scale
-    )
-    _, pull_query = jax.vjp(head_prep, query_raw, head_gain[0])
-    grad_query_raw, grad_query_gain = pull_query(grad_query.reshape(length, heads, HD))
-    _, pull_key = jax.vjp(head_prep, key_raw, head_gain[1])
-    grad_key_raw, grad_key_gain = pull_key(grad_key.reshape(length, 1, HD))
-    low = jnp.concatenate(
-        [
-            grad_query_raw.reshape(length, wq).astype(bf16),
-            grad_key_raw.reshape(length, HD).astype(bf16),
-            grad_value.astype(bf16),
-        ],
-        axis=1,
-    )
-    grad_weight = mm(normed, low, (0, 0), bf16)
-    grad_normed = fold(mm(low, weight, (1, 1), bf16).reshape(4, seq, width), 7)
-    _, pull_attn = jax.vjp(rms_scale, rows_in, gains[0])
-    grad_rows_norm, grad_gain_attn = pull_attn(grad_normed)
-    grad_input = grad_hidden + grad_rows_norm
-    gain_parts = jnp.concatenate(
-        [grad_gain_attn, grad_gain_mlp, grad_query_gain, grad_key_gain]
-    ).reshape(-1, 128)
-    extra = -gain_parts.shape[0] % 16
-    gain_parts = jnp.pad(gain_parts, ((0, extra), (0, 0)))
-    sum_q, sum_k, sum_v, sum_o, all_gain_parts = reduce_last(
+    branch = gather_rows(nz, False, grad_hidden.astype(bf16), 6)
+    columns = width // 2
+    grad_wo, grad_weight, part, grad_head, mixed_low = back(
         nz,
-        grad_weight.reshape(4, 2 * nz, rows_q, -1),
-        grad_wo.reshape(2 * nz, -1, width),
-        gain_parts,
-    )
+        scale,
+        columns,
+        branch,
+        wo,
+        weight,
+        normed,
+        raw,
+        queries,
+        attended,
+        produced,
+        keys,
+        values,
+        lse,
+        *tables,
+        head_gain,
+        slots2,
+        gates2,
+    )
+    sum_q, sum_k, sum_v, sum_o, all_gain_parts, grad_input, mixed_high = reduce_last(
+        nz,
+        columns,
+        grad_weight,
+        grad_wo,
+        produced,
+        part,
+        tokens.reshape(seq, width),
+        grad_hidden,
+        gains,
+        grad_gain_mlp.reshape(1, width),
+        grad_head,
+        slots2,
+        gates2,
+    )
+    mixed = hidden + jnp.concatenate([mixed_low, mixed_high], axis=1)
     gain_sums = jnp.sum(all_gain_parts, axis=0).reshape(-1)
     norm_sums = gain_sums[: 2 * width].reshape(2, width)
     head_sums = gain_sums[2 * width : 2 * width + 2 * HD].reshape(2, HD)
     return (
         mixed.astype(bf16).reshape(tokens.shape),
-        grad_input.astype(bf16).reshape(tokens.shape),
+        grad_input.reshape(tokens.shape),
         sum_q,
         sum_k,
         sum_v,
@@ -1481,7 +1846,7 @@
 
 
 def solution(mesh):
-    small = mesh.shape["ctx"] == HK and mesh.shape["expert"] % 2 == 0 and mesh.size <= 32
+    small = mesh.shape["ctx"] == HK and mesh.size == 32
     return jax.shard_map(
         fast_body if small else body,
         mesh=mesh,

time: 1150 us -> 947 us (0.82)
  matrix products: 93.1 us -> 36 us
  local copies, waits for them, and re-layouts: 58.4 us -> 9.9 us
  Pallas kernels: 925 us -> 880 us
  other arithmetic: 56.1 us -> 14.7 us
    pallas_call x2 -> x1, Pallas kernels: 293 us -> 146 us  [combine(): pl.pallas_call(functools.partial(combine_kernel, nz, cap), out_shape=jax....]
    pallas_call x6 -> x3, Pallas kernels: 395 us -> 502 us  [the longest x1 246 us: front(): pl.pallas_call(functools.partial(front_kernel, nz, scale), out_shape=[jax...]
    dot_general x9 -> x3, matrix products: 92.8 us -> 36 us  [mm(): lax.dot_general(a, b, ((contract[:1], contract[1:]), ((), ())), preferred...]
    unnamed x148 -> x37, local copies, waits for them, and re-layouts: 20.4 us -> 5.63 us
where the time goes in v3:
time: 947 us; the launch traced here: 942 us
  Pallas kernels  880 us (93%)
  matrix products  36 us (4%)
  other arithmetic  14.7 us (2%)
  local copies, waits for them, and re-layouts  9.9 us (1%)
    pallas_call x1, Pallas kernels, front(): pl.pallas_call(functools.partial(front_kernel, nz, scale), out_shape=[jax...  246 us
    pallas_call x1, Pallas kernels, run_experts(): pl.pallas_call(functools.partial(experts_kernel, nz, cap), out_shape=[sha...  191 us
    pallas_call x1, Pallas kernels, reduce_last(): pl.pallas_call(functools.partial(last_kernel, nz, cap, col), out_shape=[s...  151 us
    pallas_call x1, Pallas kernels, combine(): pl.pallas_call(functools.partial(combine_kernel, nz, cap), out_shape=jax....  146 us
    pallas_call x1, Pallas kernels, back(): pl.pallas_call(functools.partial(back_kernel, nz, cap, scale), out_shape=...  105 us
    pallas_call x1, Pallas kernels, gather_rows(): pl.pallas_call(functools.partial(spread_kernel, nz, everywhere), out_shap...  40.5 us
    dot_general x3, matrix products, mm(): lax.dot_general(a, b, ((contract[:1], contract[1:]), ((), ())), preferred...  36 us

profile of v3, /device:TPU:16, one launch (start us, length us, event | category | flops | bytes accessed | tf_op | source)
XLA Modules:
  0.0 941.5 jit_solution(15146540394859485545)
XLA Ops:
  0.6 0.0 copy-start
  0.7 0.0 copy-start.11
  0.7 0.0 copy-start.8
  0.7 0.7 tile.20
  1.4 0.1 tile.21
  1.5 0.7 tile.8
  2.2 0.1 tile.9
  2.3 0.7 convert_bitcast_fusion
  3.0 0.7 reshape.194
  3.7 0.6 select_maximum_fusion.refs_4_
  4.3 1.9 fusion.3
  6.2 1.3 pad_maximum_fusion.1
  7.6 0.0 copy-done
  7.6 0.0 copy-done.11
  7.6 0.0 copy-done.8
  7.6 0.9 pad_maximum_fusion.refs_0_
  8.5 246.4 %shard_map.212 = (bf16[4,8,64,1280]{3,2,1,0:T(8,128)(2,1)}, bf16[8,128,2048]{2,1,0:T(8,128)(2,1)}, bf16[4,256,2048]{2,1,0:T(8,128)(2,1)}, bf16[32,256,2048]{2,1,...) custom-call(bf16[4,64,1280]{2,1,0:T(8,128)(2,1)} %pad_maximum_fusion, ...), custom_call_target="tpu_custom_call" | custom-call | tf_op jit(solution)/shard_map/pallas_call | solution.py:843
  254.9 191.3 %shard_map.213 = (bf16[32,256,2048]{2,1,0:T(8,128)(2,1)}, bf16[32,80,2048]{2,1,0:T(8,128)(2,1)}, bf16[32,80,2048]{2,1,0:T(8,128)(2,1)}, bf16[4,2,320,2048]{3,2,1...) custom-call(bf16[256,2048]{1,0:T(8,128)(2,1)} %get-tuple-element.47., ...), custom_call_target="tpu_custom_call" | custom-call | tf_op jit(solution)/shard_map/pallas_call | solution.py:1681
  446.3 0.0 copy-start.13
  446.3 0.0 copy-start.15
  446.3 14.1 %convolution_bitcast_fusion = f32[1,768,2048]{2,1,0:T(8,128)} fusion(bf16[4,2,320,768]{3,2,1,0:T(8,128)(2,1)} %get-tuple-element.79, bf16[4,2,320,2048]{3,2,1,0:T(8,128)(2,1)} %get-tuple-element.80), kind=kOutput, calls=%fused_computation | convolution fusion | flops 8053063680 | bytes 20709376 | tf_op jit(solution)/shard_map/dot_general | solution.py:1701
  460.4 0.0 copy-done.13
  460.4 0.0 copy-done.15
  460.4 11.0 %convolution_bitcast_fusion.1 = f32[1,2048,768]{2,1,0:T(8,128)} fusion(bf16[4,2,320,2048]{3,2,1,0:T(8,128)(2,1)S(1)} %copy-done.13, bf16[4,2,320,768]{3,2,1,0:T(8,128)(2,1)S(1)} %copy-done.15), kind=kOutput, calls=%fused_computation.1 | convolution fusion | flops 8053063680 | bytes 20709376 | tf_op jit(solution)/shard_map/dot_general | solution.py:1701
  471.4 0.0 copy-done.14
  471.4 11.0 %convolution_bitcast_fusion.2 = f32[1,2048,768]{2,1,0:T(8,128)} fusion(bf16[4,2,320,2048]{3,2,1,0:T(8,128)(2,1)S(1)} %copy-done.13, bf16[4,2,320,768]{3,2,1,0:T(8,128)(2,1)S(1)} %copy-done.14), kind=kOutput, calls=%fused_computation.2 | convolution fusion | flops 8053063680 | bytes 20709376 | tf_op jit(solution)/shard_map/dot_general | solution.py:1701
  482.3 0.6 broadcast_in_dim.41.gates
  483.0 145.8 %shard_map.214 = f32[256,2048]{1,0:T(8,128)} custom-call(bf16[32,80,2048]{2,1,0:T(8,128)(2,1)} %get-tuple-element.51.rows, s32[2,32,256]{2,1,0:T(8,128)} %get-tuple-element.49.slots.refs_14_.refs_9_, f32[2,32,256]{2,1,0:T(8,128)} %broadcast_in_dim.41.gates), custom_call_target="tpu_custom_call" | custom-call | tf_op jit(solution)/shard_map/pallas_call | solution.py:1119
  628.8 0.0 copy-start.3
  628.8 0.0 copy-start.4
  628.8 0.0 copy-done.12
  628.9 0.2 multiply_reduce_fusion.2
  629.1 2.9 multiply_reduce_fusion
  632.0 2.4 fusion.7
  634.3 40.5 %shard_map.215.refs_0_ = bf16[4,256,2048]{2,1,0:T(8,128)(2,1)} custom-call(bf16[256,2048]{1,0:T(8,128)(2,1)} %get-tuple-element.83.mine), custom_call_target="tpu_custom_call" | custom-call | tf_op jit(solution)/shard_map/pallas_call | solution.py:902
  674.8 104.8 %shard_map.216 = (bf16[8,128,2048]{2,1,0:T(8,128)(2,1)}, bf16[4,8,64,1280]{3,2,1,0:T(8,128)(2,1)}, bf16[4,256,2048]{2,1,0:T(8,128)(2,1)}, f32[2,128]{1,0:T(2,128)}, f32[256,1024]{1,0:T(8,128)}) custom-call(bf16[4,256,2048]{2,1,0:T(8,128)(2,1)} %shard_map.215.refs_0_, bf16[8,128,2048]{2,1,0:T(8,128)(2,1)} %get-tuple-element.53.refs_1_, ...), custom_call_target="tpu_custom_call" | custom-call | tf_op jit(solution)/shard_map/pallas_call | solution.py:1285
  779.6 0.0 copy-start.5
  779.6 151.0 %shard_map.217 = (f32[64,4096]{1,0:T(8,128)}, f32[64,512]{1,0:T(8,128)}, f32[64,512]{1,0:T(8,128)}, f32[128,2048]{1,0:T(8,128)}, f32[32,48,128]{2,1,0:T(8,128)},...) custom-call(bf16[4,8,64,1280]{3,2,1,0:T(8,128)(2,1)} %get-tuple-element.65.refs_0_, ...), custom_call_target="tpu_custom_call" | custom-call | tf_op jit(solution)/shard_map/pallas_call | solution.py:1498
  930.6 0.0 copy-start.1
  930.6 2.5 fusion.2
  933.2 1.3 reduce_sum.41
  934.5 0.6 constant_dynamic-slice_fusion.1
  935.1 0.6 constant_dynamic-slice_fusion
  935.8 2.3 copy.42
  938.1 1.0 copy.43
  939.1 0.7 copy.44
  939.7 0.7 copy.45
  940.4 1.0 copy.46
  (30 shorter events, 0.2 us)
Async XLA Ops:
  0.6 6.9 copy-start
  0.7 6.9 copy-start.11
  0.7 6.9 copy-start.8
  446.3 14.1 %copy-start.13 = (bf16[4,2,320,2048]{3,2,1,0:T(8,128)(2,1)S(1)}, bf16[4,2,320,2048]{3,2,1,0:T(8,128)(2,1)}, u32[]{:S(2)}) copy-start(bf16[4,2,320,2048]{3,2,1,0:T(8,128)(2,1)} %get-tuple-element.76) | copy-start | bytes 31457284
  446.3 14.1 %copy-start.15 = (bf16[4,2,320,768]{3,2,1,0:T(8,128)(2,1)S(1)}, bf16[4,2,320,768]{3,2,1,0:T(8,128)(2,1)}, u32[]{:S(2)}) copy-start(bf16[4,2,320,768]{3,2,1,0:T(8,128)(2,1)} %get-tuple-element.78) | copy-start | bytes 11796484
  460.4 11.0 %copy-start.14 = (bf16[4,2,320,768]{3,2,1,0:T(8,128)(2,1)S(1)}, bf16[4,2,320,768]{3,2,1,0:T(8,128)(2,1)}, u32[]{:S(2)}) copy-start(bf16[4,2,320,768]{3,2,1,0:T(8,128)(2,1)} %get-tuple-element.77) | copy-start | bytes 11796484
  483.0 145.8 %copy-start.12 = (f32[2,2048]{1,0:T(2,128)S(1)}, f32[2,2048]{1,0:T(2,128)}, u32[]{:S(2)}) copy-start(f32[2,2048]{1,0:T(2,128)} %get-tuple-element.52.refs_6_) | copy-start | bytes 49156
  483.0 145.9 %copy-start.2 = (f32[256,2048]{1,0:T(8,128)S(1)}, f32[256,2048]{1,0:T(8,128)}, u32[]{:S(2)}) copy-start(f32[256,2048]{1,0:T(8,128)} %get-tuple-element.46) | copy-start | bytes 6291460
  628.8 3.2 copy-start.3
  628.8 3.1 copy-start.4
  779.6 151.0 %copy-start.5 = (f32[256,1024]{1,0:T(8,128)S(1)}, f32[256,1024]{1,0:T(8,128)}, u32[]{:S(2)}) copy-start(f32[256,1024]{1,0:T(8,128)} %get-tuple-element.64) | copy-start | bytes 3145732
  930.6 7.5 copy-start.7
  930.6 8.4 copy-start.10
  930.6 10.7 %copy-start.1 = (bf16[64,512]{1,0:T(8,128)(2,1)S(1)}, bf16[64,512]{1,0:T(8,128)(2,1)}, u32[]{:S(2)}) copy-start(bf16[64,512]{1,0:T(8,128)(2,1)} %param.15) | copy-start | bytes 196612
  933.2 6.5 copy-start.9
  933.2 7.2 copy-start.6

commit v4 on v3

--- a/solution.py
+++ b/solution.py
@@ -358,6 +358,8 @@
 
 MESH = pl.DeviceIdType.MESH
 VMEM_BYTES = 58 * 2**20
+LAST_DEEP = 0
+DEEP = 32
 ANY = pl.BlockSpec(memory_space=pl.ANY)
 IN_VMEM = pl.BlockSpec(memory_space=pltpu.VMEM)
 f32, bf16 = jnp.float32, jnp.bfloat16
@@ -543,6 +545,113 @@
             self.each(far, act)
 
 
+class SpreadDeep:
+    def __init__(self, p, nz, mine, block, send, recv, send_in, recv_in):
+        self.p, self.nz, self.mine, self.block = p, nz, mine, block
+        self.send, self.recv, self.send_in, self.recv_in = send, recv, send_in, recv_in
+        self.places = (p.c, p.cx, p.cy, p.cd)
+        self.half = mine.shape[0] // 2
+
+    def ref(self, r, z, h=None, k=None):
+        whole = self.block(self.places[r], z, self.p.k if k is None else k)
+        return whole if h is None else whole.at[pl.ds(h * self.half, self.half)]
+
+    def near(self, i):
+        p, own = self.p, self.ref(0, self.p.z)
+        src, dst, device = (
+            lambda: (self.mine, own, p.dx),
+            lambda: (self.mine, own, p.dy),
+            lambda: (self.ref(1, p.z, 0), self.ref(1, p.z, 0), p.dy),
+            lambda: (self.ref(2, p.z, 1), self.ref(2, p.z, 1), p.dx),
+        )[i]()
+        return remote(src, dst, self.send_in.at[i], self.recv_in.at[i], device)
+
+    def hop(self, r, z, i, own=False):
+        dst = self.ref(r, z)
+        device = (self.p.up, self.p.down, self.p.pair)[i]
+        src = self.mine if own else dst
+        return remote(src, dst, self.send.at[z, r, i], self.recv.at[z, r, i // 2], device)
+
+    def forward(self, r, z, way, act):
+        p, own = self.p, r == 0 and way == 0
+        if way <= 0:
+
+            @pl.when(p.z < self.nz - 1)
+            def _():
+                act(self.hop(r, z, 0, own))
+
+        if way >= 0:
+
+            @pl.when(p.z > 0)
+            def _():
+                act(self.hop(r, z, 1, own))
+
+        act(self.hop(r, z, 2, own))
+
+    def each(self, far, act):
+        for way in (-1, 1):
+            z = self.p.z + way * far
+
+            @pl.when((z >= 0) & (z < self.nz))
+            def _():
+                act(z, way)
+
+    def step(self, i):
+        start = lambda copy: copy.start()
+        z = self.p.z
+        if i == 0:
+            self.near(0).start()
+            self.near(1).start()
+            self.forward(0, z, 0, start)
+        elif i == 1:
+            for n in (0, 1):
+                ref = self.ref(1 + n, z)
+                remote(ref, ref, self.send_in.at[n], self.recv_in.at[n], self.p.pair).wait_recv()
+                self.near(2 + n).start()
+                self.forward(1 + n, z, 0, start)
+        elif i == 2:
+            for n in (0, 1):
+                ref = self.ref(3, z, n)
+                remote(
+                    ref, ref, self.send_in.at[n], self.recv_in.at[2 + n], self.p.pair
+                ).wait_recv()
+            self.forward(3, z, 0, start)
+        elif i < self.nz + 2:
+
+            def act(z, way):
+                for r in range(4):
+                    self.got(r, z, 0)
+                    self.forward(r, z, way, start)
+
+            self.each(i - 2, act)
+
+    def got(self, r, z, i):
+        ref = self.ref(r, z, None, self.p.k if i == 0 else 1 - self.p.k)
+        remote(ref, ref, self.send.at[z, r, 0], self.recv.at[z, r, i], self.p.pair).wait_recv()
+
+    def finish(self, pair=True):
+        def act(z, way):
+            for r in range(4):
+                if pair:
+                    self.got(r, z, 1)
+                self.forward(r, z, way, lambda copy: copy.wait_send())
+
+        for i in range(4):
+            self.near(i).wait_send()
+        act(self.p.z, 0)
+        for far in range(1, self.nz):
+            self.each(far, act)
+
+
+def deep_sems(nz):
+    dma = pltpu.SemaphoreType.DMA
+    return [dma((nz, 4, 3)), dma((nz, 4, 2)), dma((4,)), dma((4,))]
+
+
+def lines_of(ref, nz, first, count):
+    return lambda c, z, k: ref.at[c * (2 * nz) + z * 2 + k, pl.ds(first, count)]
+
+
 def by_device(ref, nz):
     return lambda c, z, k: ref.at[c * (2 * nz) + z * 2 + k]
 
@@ -552,16 +661,17 @@
 
 
 class Fold:
-    def __init__(self, p, parts, sx, sy, h0, h1, bx, by, send, recv):
+    def __init__(self, p, parts, sx, sy, h0, h1, bx, by, send, recv, far=None):
+        far = parts if far is None else far
         half = bx.shape[0] // 2
         self.halves = low, high = pl.ds(0, half), pl.ds(half, half)
         self.p, self.parts, self.sx, self.sy = p, parts, sx, sy
         self.h0, self.h1, self.bx, self.by = h0, h1, bx, by
         copy = lambda i, src, dst, device: remote(src, dst, send.at[i], recv.at[i], device)
-        self.to_x = copy(0, parts.at[p.cd, low], h0, p.dx)
-        self.to_y = copy(1, parts.at[p.cd, high], h1, p.dy)
-        self.x_low = copy(2, parts.at[p.cx, low], bx.at[low], p.dx)
-        self.y_high = copy(3, parts.at[p.cy, high], by.at[high], p.dy)
+        self.to_x = copy(0, far.at[p.cd, low], h0, p.dx)
+        self.to_y = copy(1, far.at[p.cd, high], h1, p.dy)
+        self.x_low = copy(2, far.at[p.cx, low], bx.at[low], p.dx)
+        self.y_high = copy(3, far.at[p.cy, high], by.at[high], p.dy)
         self.x_high = copy(4, sx, bx.at[high], p.dx)
         self.y_low = copy(5, sy, by.at[low], p.dy)
 
@@ -602,10 +712,16 @@
 def front_kernel(nz, scale, *refs):
     pack, wo, tok, cot, meta, cosine, sine = refs[:7]
     packs, wos, toks, cots, metas = refs[7:12]
-    xn, raw, q, k, v, ot, lse, hidden, hn, gain_out, head_out, slots, gates = refs[12:25]
-    tok_v, w_v, wo_v, meta_v, vt, ob, part = refs[25:32]
-    fold_refs, pair_sems = refs[32:40], refs[40:50]
-    a_send, a_recv, local, load = refs[50:]
+    results, held = refs[12:25], refs[25:38]
+    xn, raw, q, k, v, ot, lse, hidden, hn, gain_out, head_out, slots, gates = held
+    tok_v, w_v, wo_v, meta_v, vt, ob, part = refs[38:45]
+    fold_refs, pair_sems = refs[45:53], refs[53:63]
+    a_send, a_recv, local, load, out_sem = refs[63:68]
+
+    def copy_out(*which):
+        for i in which:
+            pltpu.make_async_copy(held[i], results[i], out_sem.at[i]).start()
+
     p = Place()
     seq, width = tok.shape
     length = 4 * seq
@@ -656,7 +772,11 @@
 
     j_tok = job(0, tok, lambda c, z, k: toks.at[c], seq // 2, False, True, False)
     j_meta = job(1, meta, by_device(metas, nz), meta.shape[0] // 2)
-    j_cot = job(2, cot, by_device(cots, nz), seq // 2)
+    most = seq - DEEP
+    j_cot = job(2, cot.at[pl.ds(0, most)], lines_of(cots, nz, 0, most), most // 2)
+    j_deep = SpreadDeep(
+        p, nz, cot.at[pl.ds(most, DEEP)], lines_of(cots, nz, most, DEEP), *refs[68:]
+    )
     j_wo = job(3, wo, lambda c, z, k: wos.at[z * 2 + k], 0, True, False, True)
     own_pack = packs.at[:, p.e]
     j_pack = job(4, own_pack, lambda c, z, k: packs.at[:, z * 2 + k], 0, True, False, True)
@@ -680,6 +800,7 @@
     j_meta.step(2)
     j_pack.step(2)
     j_cot.step(0)
+    j_deep.step(0)
     for i in range(3, nz + 2):
         j_meta.step(i)
         j_pack.step(i)
@@ -734,7 +855,9 @@
         w = w_v[:, :, :, cols].reshape(width, 256)
         raw[:, cols] = jnp.dot(xn[...], w, preferred_element_type=f32)
 
+    copy_out(0, 1, 9, 10)
     j_cot.step(1)
+    j_deep.step(1)
     j_wo.step(1)
 
     def prep(x, g):
@@ -745,6 +868,7 @@
     values = raw[:, pl.ds((heads + 1) * HD, HD)]
     v[...] = values.astype(bf16)
     vt[...] = values.T.astype(bf16)
+    copy_out(3, 4)
 
     def attend(h):
         cols = pl.ds(pl.multiple_of(h * HD, HD), HD)
@@ -769,7 +893,9 @@
     pl.loop(0, heads // 2)(attend)
     j_wo.step(2)
     j_cot.step(2)
+    j_deep.step(2)
     pl.loop(heads // 2, heads)(attend)
+    copy_out(2, 5, 6)
     for i in range(3, nz + 2):
         j_wo.step(i)
     own[1].wait()
@@ -797,6 +923,7 @@
         slots[j] = jnp.where(member > 0.5, rank.astype(jnp.int32) - 1, -1)
         gates[j] = jnp.concatenate(weight, axis=1)
 
+    copy_out(11, 12)
     loads[1].wait()
     tile = 512
 
@@ -810,6 +937,7 @@
     fold = Fold(p, part, *fold_refs)
     fold.begin()
     j_cot.step(3)
+    j_deep.step(3)
     fold.middle()
 
     def store(rows, total):
@@ -818,12 +946,17 @@
         hn[rows] = rms(h, gain_out[1:2]).astype(bf16)
 
     fold.end(store)
+    copy_out(7, 8)
     for i in range(4, nz + 2):
         j_cot.step(i)
+        j_deep.step(i)
     for copy in swaps:
         copy.wait_send()
     for spread in (j_tok, j_meta, j_cot, j_wo, j_pack):
         spread.finish(pair=spread is j_cot)
+    j_deep.finish()
+    for i in range(len(held)):
+        pltpu.make_async_copy(held[i], results[i], out_sem.at[i]).wait()
 
 
 def meta_lines(length, width, seq):
@@ -840,6 +973,21 @@
     out = lambda *n: jax.ShapeDtypeStruct(n[:-1], n[-1])
     vmem = lambda *n: pltpu.VMEM(n, bf16)
     dma = pltpu.SemaphoreType.DMA
+    held = [
+        out(length, width, bf16),
+        out(length, wide, f32),
+        out(heads, length, HD, bf16),
+        out(length, HD, bf16),
+        out(length, HD, bf16),
+        out(heads, HD, length, bf16),
+        out(heads, 1, length, f32),
+        out(seq, width, f32),
+        out(seq, width, bf16),
+        out(2, width, f32),
+        out(2, HD, f32),
+        out(2, blocks, seq, jnp.int32),
+        out(2, blocks, seq, f32),
+    ]
     return pl.pallas_call(
         functools.partial(front_kernel, nz, scale),
         out_shape=[
@@ -848,23 +996,12 @@
             hbm((4,), tok),
             hbm((blocks,), cot),
             hbm((blocks,), meta),
-            out(length, width, bf16),
-            out(length, wide, f32),
-            out(heads, length, HD, bf16),
-            out(length, HD, bf16),
-            out(length, HD, bf16),
-            out(heads, HD, length, bf16),
-            out(heads, 1, length, f32),
-            out(seq, width, f32),
-            out(seq, width, bf16),
-            out(2, width, f32),
-            out(2, HD, f32),
-            out(2, blocks, seq, jnp.int32),
-            out(2, blocks, seq, f32),
-        ],
+        ]
+        + held,
         in_specs=[ANY] * 5 + [IN_VMEM] * 2,
-        out_specs=[ANY] * 5 + [IN_VMEM] * 13,
-        scratch_shapes=[
+        out_specs=[ANY] * 18,
+        scratch_shapes=[pltpu.VMEM(a.shape, a.dtype) for a in held]
+        + [
             vmem(4, seq, width),
             vmem(4, 2 * nz, pack.shape[1], wide),
             vmem(2 * nz, wo.shape[0], width),
@@ -875,7 +1012,8 @@
         ]
         + fold_scratch(seq, width)
         + spread_sems(nz) * 5
-        + [dma((n,)) for n in (3, 3, 8, 6)],
+        + [dma((n,)) for n in (3, 3, 8, 6, len(held))]
+        + deep_sems(nz),
         compiler_params=pltpu.CompilerParams(
             collective_id=1, has_side_effects=True, vmem_limit_bytes=VMEM_BYTES
         ),
@@ -910,30 +1048,38 @@
 
 
 class Combine:
-    def __init__(self, p, nz, cap, col, rows, slots, gates, out, *scratch):
+    def __init__(self, p, nz, cap, col, deep, rows, slots, gates, out, *scratch):
         self.p, self.nz, self.cap, self.rows, self.slots, self.gates = p, nz, cap, rows, slots, gates
         self.out = out
         self.rbuf, self.sd, self.sx, self.sy = scratch[:4]
         self.h0, self.h1, self.bx, self.by, self.bz = scratch[4:9]
         self.pair_send, self.pair_recv, self.load = scratch[9:12]
         self.s_h0, self.s_h1, self.s_x, self.s_y, self.s_z = scratch[12:17]
-        self.r_h0, self.r_h1, self.r_x, self.r_y, self.r_z = scratch[17:]
+        self.r_h0, self.r_h1, self.r_x, self.r_y, self.r_z = scratch[17:22]
         self.order = pick_order(p, nz)
-        self.seq, self.width = self.sx.shape[1:]
-        self.half = self.seq // 2
+        self.most, self.width = self.sx.shape[1:]
+        self.seq = self.most + deep
+        self.half = self.most // 2
         self.cols = pl.ds(col, self.width)
+        self.deep = deep
+        self.tile = max(t for t in range(128, 1025, 128) if self.width % t == 0)
+        if deep:
+            self.s_d, self.b_d, self.send_d, self.recv_d = scratch[22:26]
+            self.fold = Fold(p, self.s_d.at[p.z], *scratch[26:])
 
     def clear(self):
         bz, nz = self.bz, self.nz
 
         @pl.when(self.p.z == 0)
         def _():
-            bz[pl.ds(0, nz)] = jnp.zeros((nz,) + bz.shape[1:], bz.dtype)
+            for ref in [bz] + ([self.b_d] if self.deep else []):
+                ref[pl.ds(0, nz)] = jnp.zeros((nz,) + ref.shape[1:], ref.dtype)
 
         @pl.when(self.p.z == nz - 1)
         def _():
-            bz[pl.ds(0, nz - 1)] = jnp.zeros((nz - 1,) + bz.shape[1:], bz.dtype)
-            bz[nz] = jnp.zeros(bz.shape[1:], bz.dtype)
+            for ref in [bz] + ([self.b_d] if self.deep else []):
+                ref[pl.ds(0, nz - 1)] = jnp.zeros((nz - 1,) + ref.shape[1:], ref.dtype)
+                ref[nz] = jnp.zeros(ref.shape[1:], ref.dtype)
 
     def pair_copy(self, c, z):
         p = self.p
@@ -959,15 +1105,100 @@
                 self.load_copy(c, z).start()
                 self.pair_copy(c, z).start()
 
-    def fill(self, c, z, low, high, store):
-        half = self.half
+    def places(self, c, z):
         b = pl.ds(c * (2 * self.nz) + z * 2 + self.p.k, 1)
         names = lax.broadcasted_iota(jnp.int32, (self.cap, self.seq), 0)
         both = [jnp.where(names == self.slots[n, b], self.gates[n, b], 0.0) for n in (0, 1)]
-        w = jnp.concatenate(both, axis=0).T.astype(bf16)
+        return jnp.concatenate(both, axis=0).T.astype(bf16)
+
+    def arrived(self, c, z):
         self.load_copy(c, z).wait()
         self.pair_copy(c, z).wait_recv()
-        tile = min(512, self.width)
+
+    def copy_deep(self, z, up):
+        p = self.p
+        slot = z if up else jnp.where(z == p.z - 1, self.nz, z)
+        return remote(
+            self.s_d.at[z],
+            self.b_d.at[slot],
+            self.send_d.at[z],
+            self.recv_d.at[slot],
+            p.up if up else p.down,
+        )
+
+    def deep_send(self, z):
+        @pl.when(z > self.p.z)
+        def _():
+            self.copy_deep(z, True).start()
+
+        @pl.when(z < self.p.z)
+        def _():
+            self.copy_deep(z, False).start()
+
+    def deep_recv(self, slot):
+        ref = self.b_d.at[slot]
+        remote(ref, ref, self.send_d.at[0], self.recv_d.at[slot], self.p.pair).wait_recv()
+
+    def deep_first(self, i):
+        p, nz, z = self.p, self.nz, self.order[i]
+        for c in range(4):
+            self.arrived(c, z)
+            w = self.places(c, z)[self.most :]
+            for t in range(self.width // self.tile):
+                cols = pl.ds(t * self.tile, self.tile)
+                total = jnp.dot(w, self.rbuf[c, z, :, cols], preferred_element_type=f32)
+                self.s_d[z, c, :, cols] = total.astype(bf16)
+        if i < nz - 1:
+
+            @pl.when((p.z == 0) | (p.z == nz - 1))
+            def _():
+                self.deep_send(z)
+
+    def deep_add(self, z, *slots):
+        for c in range(4):
+            total = self.s_d[z, c].astype(f32)
+            for slot in slots:
+                total = total + self.b_d[slot, c].astype(f32)
+            self.s_d[z, c] = total.astype(bf16)
+
+    def deep_next(self, i):
+        p, nz, z = self.p, self.nz, self.order[i]
+        if i < nz - 1:
+
+            @pl.when((p.z > 0) & (p.z < nz - 1))
+            def _():
+                self.deep_recv(z)
+                self.deep_add(z, z)
+                self.deep_send(z)
+
+            return
+
+        @pl.when(p.z > 0)
+        def _():
+            self.deep_recv(z)
+
+        @pl.when(p.z < nz - 1)
+        def _():
+            self.deep_recv(nz)
+
+        self.deep_add(z, z, nz)
+        self.fold.begin()
+
+    def deep_end(self, i):
+        if i == 0:
+            self.fold.middle()
+            return
+
+        def store(lines, total):
+            self.out[pl.ds(self.most + lines.start, lines.size)] = total
+
+        self.fold.end(store)
+
+    def fill(self, c, z, low, high, store):
+        half, tile = self.half, self.tile
+        w = self.places(c, z)[: self.most]
+        if not self.deep:
+            self.arrived(c, z)
         for t in range(self.width // tile):
             cols = pl.ds(t * tile, tile)
             total = jnp.dot(w, self.rbuf[c, z, :, cols], preferred_element_type=f32)
@@ -1074,6 +1305,19 @@
             if i > 0:
                 found.append((self.mine, i - 1))
         found.append((self.mine, nz - 1))
+        if self.deep:
+            first = [(self.deep_first, i) for i in range(nz)]
+            late = [(self.deep_next, i) for i in range(nz)]
+            plan = first[:1]
+            for act in found:
+                if act[0] == self.diagonal and act[1] > 0:
+                    plan.append(first[act[1]])
+                if act == (self.mine, nz - 1):
+                    plan.append(late[nz - 1])
+                plan.append(act)
+                if act[0] == self.sides and 1 <= act[1] < nz:
+                    plan.append(late[act[1] - 1])
+            found = plan + [(self.deep_end, 0), (self.deep_end, 1)]
         return [functools.partial(act, i) for act, i in found]
 
     def finish(self):
@@ -1085,11 +1329,18 @@
                 copy.wait_send()
             if i < self.nz - 1:
                 self.copy_up(z).wait_send()
-
-
-def combine_scratch(nz, cap, seq, width):
+                if self.deep:
+                    self.copy_deep(z, True).wait_send()
+
+
+def combine_scratch(nz, cap, seq, width, deep):
     dma = pltpu.SemaphoreType.DMA
     buf = lambda n, r: pltpu.VMEM((n, r, width), bf16)
+    seq = seq - deep
+    last = []
+    if deep:
+        last = [pltpu.VMEM((n, 4, deep, width), bf16) for n in (nz, nz + 1)]
+        last += [dma((nz,)), dma((nz + 1,))] + fold_scratch(deep, width)
     return (
         [pltpu.VMEM((4, nz, 2 * cap, width), bf16)]
         + [buf(nz, seq)] * 3
@@ -1099,12 +1350,13 @@
         + [dma((4, nz))] * 3
         + [dma((nz,))] * 9
         + [dma((nz + 1,))]
-    )
-
-
-def combine_kernel(nz, cap, rows, slots, gates, out, *scratch):
+        + last
+    )
+
+
+def combine_kernel(nz, cap, deep, rows, slots, gates, out, *scratch):
     p = Place()
-    job = Combine(p, nz, cap, 0, rows, slots, gates, out, *scratch)
+    job = Combine(p, nz, cap, 0, deep, rows, slots, gates, out, *scratch)
     job.clear()
     greet(p, nz)
     job.begin()
@@ -1113,19 +1365,104 @@
     job.finish()
 
 
-def combine(nz, rows, slots, gates, collective_id):
+def combine(nz, deep, rows, slots, gates, collective_id):
     _, cap, width = rows.shape
     seq = slots.shape[2]
     return pl.pallas_call(
-        functools.partial(combine_kernel, nz, cap),
+        functools.partial(combine_kernel, nz, cap, deep),
         out_shape=jax.ShapeDtypeStruct((seq, width), f32),
         in_specs=[ANY, IN_VMEM, IN_VMEM],
         out_specs=IN_VMEM,
-        scratch_shapes=combine_scratch(nz, cap, seq, width),
+        scratch_shapes=combine_scratch(nz, cap, seq, width, deep),
         compiler_params=pltpu.CompilerParams(
             collective_id=collective_id, has_side_effects=True, vmem_limit_bytes=VMEM_BYTES
         ),
     )(rows, slots, gates)
+
+
+class LineSum:
+    def __init__(self, p, nz, part, own, sib, b, pair_s, pair_r, line_s, line_r):
+        self.p, self.nz, self.part, self.own, self.sib, self.b = p, nz, part, own, sib, b
+        self.pair_s, self.pair_r, self.line_s, self.line_r = pair_s, pair_r, line_s, line_r
+        self.order = pick_order(p, nz)
+
+    def clear(self):
+        b, nz = self.b, self.nz
+
+        @pl.when(self.p.z == 0)
+        def _():
+            b[pl.ds(0, nz)] = jnp.zeros((nz,) + b.shape[1:], b.dtype)
+
+        @pl.when(self.p.z == nz - 1)
+        def _():
+            b[pl.ds(0, nz - 1)] = jnp.zeros((nz - 1,) + b.shape[1:], b.dtype)
+            b[nz] = jnp.zeros(b.shape[1:], b.dtype)
+
+    def pair_copy(self, z):
+        p = self.p
+        src = self.part(z, 1 - p.k)
+        return remote(src, self.sib.at[z], self.pair_s.at[z], self.pair_r.at[z], p.pair)
+
+    def begin(self):
+        for z in self.order:
+            self.pair_copy(z).start()
+
+    def copy_up(self, z):
+        p = self.p
+        return remote(self.own(z), self.b.at[z], self.line_s.at[z], self.line_r.at[z], p.up)
+
+    def copy_down(self, z):
+        p = self.p
+        slot = jnp.where(z == p.z - 1, self.nz, z)
+        return remote(self.own(z), self.b.at[slot], self.line_s.at[z], self.line_r.at[slot], p.down)
+
+    def line_recv(self, slot):
+        ref = self.b.at[slot]
+        remote(ref, ref, self.line_s.at[0], self.line_r.at[slot], self.p.pair).wait_recv()
+
+    def reduce(self, n, store=None):
+        p, nz, z = self.p, self.nz, self.order[n]
+        own, b = self.own(z), self.b
+        self.pair_copy(z).wait_recv()
+        if n == nz - 1:
+
+            @pl.when(p.z > 0)
+            def _():
+                self.line_recv(z)
+
+            @pl.when(p.z < nz - 1)
+            def _():
+                self.line_recv(nz)
+
+            total = own[...].astype(f32) + self.sib[z].astype(f32) + b[z].astype(f32)
+            store(total + b[nz].astype(f32))
+            return
+
+        @pl.when(((z > p.z) & (p.z > 0)) | ((z < p.z) & (p.z < nz - 1)))
+        def _():
+            self.line_recv(z)
+
+        total = own[...].astype(f32) + self.sib[z].astype(f32) + b[z].astype(f32)
+        own[...] = total.astype(own.dtype)
+
+        @pl.when(z > p.z)
+        def _():
+            self.copy_up(z).start()
+
+        @pl.when(z < p.z)
+        def _():
+            self.copy_down(z).start()
+
+    def finish(self):
+        for n, z in enumerate(self.order):
+            self.pair_copy(z).wait_send()
+            if n < self.nz - 1:
+                self.copy_up(z).wait_send()
+
+
+def line_sems(nz):
+    dma = pltpu.SemaphoreType.DMA
+    return [dma((nz,))] * 3 + [dma((nz + 1,))]
 
 
 def rms_back(x, gain, grad):
@@ -1139,29 +1476,43 @@
 def back_kernel(nz, cap, scale, *refs):
     branch, wos, packs, xn, raw, q, ot, rows = refs[:8]
     k, v, lse, cosine, sine, head_gain, slots, gates = refs[8:16]
-    gwo, gw, part, head_grad, mixed = refs[16:21]
-    rows_v, wo_v, w_v, raw_v, q_v, ot_v, do, kt, low, dq, dk, dv, wo_stage, w_stage = refs[21:35]
-    load, wo_sem, w_sem = refs[35:38]
+    sum_o, gw, part, head_grad, mixed = refs[16:21]
+    rows_v, wo_v, w_v, raw_v, q_v, ot_v, do, kt, low, dq, dk, dv, w_stage, sib, line_b = refs[21:36]
+    load, w_sem, ot_sem = refs[36:39]
     p = Place()
-    combine = Combine(p, nz, cap, 0, rows, slots, gates, mixed, *refs[38:])
+    line = LineSum(
+        p,
+        nz,
+        lambda z, k: wo_v.at[z * 2 + k],
+        lambda z: wo_v.at[z * 2 + p.k],
+        sib,
+        line_b,
+        *refs[39:43],
+    )
+    combine = Combine(p, nz, cap, 0, 0, rows, slots, gates, mixed, *refs[43:])
     length, wide = raw.shape
     heads = q.shape[0]
     seq = length // 4
-    width = part.shape[2]
+    width = xn.shape[2]
     loads = [
         pltpu.make_async_copy(src, dst, load.at[i])
         for i, (src, dst) in enumerate(
-            ((branch, rows_v), (wos, wo_v), (q, q_v), (ot, ot_v), (packs, w_v))
+            ((branch, rows_v), (wos, wo_v), (q, q_v), (packs, w_v))
         )
     ]
+    load_ot = [
+        pltpu.make_async_copy(ot.at[pl.ds(2 * t, 2)], ot_v.at[t % 2], ot_sem.at[t % 2])
+        for t in range(heads // 2)
+    ]
     load_xn = pltpu.make_async_copy(xn, rows_v, load.at[5])
 
     def load_raw(cols):
         return pltpu.make_async_copy(raw.at[:, cols], raw_v, load.at[6])
 
-    for copy in loads:
+    for copy in loads + load_ot[:2]:
         copy.start()
     combine.clear()
+    line.clear()
     greet(p, nz)
     combine.begin()
     steps = combine.steps()
@@ -1179,15 +1530,44 @@
         do[:, cols] = out.astype(bf16)
 
     run(1)
+
+    for t in range(heads // 2):
+        load_ot[t].wait()
+        here = 2 * HD // wo_v.shape[1]
+
+        @pl.loop(0, width // 512)
+        def _(i):
+            cols = pl.ds(pl.multiple_of(i * 512, 512), 512)
+            out = jnp.dot(
+                ot_v[t % 2].reshape(2 * HD, length),
+                rows_v[:, :, cols].reshape(length, 512),
+                preferred_element_type=f32,
+            )
+            wo_v[pl.ds(t * here, here), :, cols] = out.astype(bf16).reshape(
+                here, wo_v.shape[1], 512
+            )
+
+        if t + 2 < heads // 2:
+            load_ot[t + 2].start()
+
+    line.begin()
+    load_xn.start()
+    run(1)
     loads[2].wait()
-    loads[3].wait()
     dk[...] = jnp.zeros(dk.shape, f32)
     dv[...] = jnp.zeros(dv.shape, f32)
     head_grad[...] = jnp.zeros(head_grad.shape, f32)
 
-    def unprep(x, gain, grad):
-        grad = grad * cosine[...] + pltpu.roll(grad * sine[...], HD // 2, 1)
-        return rms_back(x, gain, grad)
+    def unprep(gain, grad, cols):
+        by_gain = jnp.zeros((1, HD), f32)
+        for i in range(length // seq):
+            here = pl.ds(i * seq, seq)
+            g = grad[here]
+            g = g * cosine[here] + pltpu.roll(g * sine[here], HD // 2, 1)
+            by_x, more = rms_back(raw_v[here], gain, g)
+            low[here, cols] = by_x.astype(bf16)
+            by_gain = by_gain + more
+        return by_gain
 
     def attend(h):
         cols = pl.ds(pl.multiple_of(h * HD, HD), HD)
@@ -1206,46 +1586,21 @@
             dv[keys] += jnp.dot(probs.astype(bf16), do[here, cols], preferred_element_type=f32)
             dq[here] = (jnp.dot(kt[:, keys], ds, preferred_element_type=f32) * scale).T
         load_raw(cols).wait()
-        by_x, by_gain = unprep(raw_v[...], head_gain[0:1], dq[...])
-        low[:, cols] = by_x.astype(bf16)
-        head_grad[0:1] += by_gain
-
-    for first in range(0, heads, 2):
+        head_grad[0:1] += unprep(head_gain[0:1], dq, cols)
+
+    def store(total):
+        sum_o[...] = total
+
+    for n, first in enumerate(range(0, heads, 2)):
         pl.loop(first, first + 2)(attend)
         run(1)
+        if n < nz - 1:
+            line.reduce(n)
     load_raw(pl.ds(heads * HD, HD)).start()
     load_raw(pl.ds(heads * HD, HD)).wait()
-    by_x, by_gain = unprep(raw_v[...], head_gain[1:2], dk[...])
-    low[:, pl.ds(heads * HD, HD)] = by_x.astype(bf16)
-    head_grad[1:2] = by_gain
+    head_grad[1:2] = unprep(head_gain[1:2], dk, pl.ds(heads * HD, HD))
     low[:, pl.ds((heads + 1) * HD, HD)] = dv[...].astype(bf16)
 
-    tile = wo_stage.shape[3]
-    wo_out = lambda t: pltpu.make_async_copy(
-        wo_stage.at[t % 2], gwo.at[:, :, pl.ds(t * tile, tile)], wo_sem.at[t % 2]
-    )
-    for t in range(width // tile):
-        if t >= 2:
-            wo_out(t - 2).wait()
-        out = jnp.dot(
-            ot_v[...].reshape(heads * HD, length),
-            rows_v[:, :, pl.ds(t * tile, tile)].reshape(length, tile),
-            preferred_element_type=f32,
-        )
-        wo_stage[t % 2] = out.astype(bf16).reshape(wo_stage.shape[1:])
-        wo_out(t).start()
-        if t % 2:
-            run(1)
-    load_xn.start()
-    loads[4].wait()
-    for c in range(4):
-        w = w_v[c].reshape(width // 4, wide)
-        out = lax.dot_general(low[...], w, NT, preferred_element_type=f32)
-        part[:, :, pl.ds(c * (width // 4), width // 4)] = out.astype(bf16).reshape(
-            4, seq, width // 4
-        )
-        if c % 2:
-            run(1)
     load_xn.wait()
     lines = w_stage.shape[1] * w_stage.shape[2]
 
@@ -1265,11 +1620,28 @@
         w_out(t).start()
         if t % 3 == 2:
             run(1)
+    loads[3].wait()
+    for c in range(4):
+
+        @pl.loop(0, 2)
+        def _(i):
+            here = nz * w_v.shape[2]
+            w = w_v[c, pl.ds(i * nz, nz)].reshape(here, wide)
+            out = lax.dot_general(low[...], w, NT, preferred_element_type=f32)
+            cols = pl.ds(pl.multiple_of((2 * c + i) * here, here), here)
+            rows_v[:, :, cols] = out.astype(bf16).reshape(4, seq, here)
+
+        if c % 2:
+            run(1)
+    part_out = pltpu.make_async_copy(rows_v, part, load.at[4])
+    part_out.start()
+    line.reduce(nz - 1, store)
     run(len(steps))
+    part_out.wait()
     for t in range(2):
-        wo_out(width // tile - 2 + t).wait()
         w_out(width // lines - 2 + t).wait()
     combine.finish()
+    line.finish()
 
 
 def back(nz, scale, columns, branch, wos, packs, xn, raw, q, ot, rows, k, v, lse, cosine, sine, head_gain, slots, gates):
@@ -1285,34 +1657,36 @@
     return pl.pallas_call(
         functools.partial(back_kernel, nz, cap, scale),
         out_shape=[
-            shape(wos.shape, bf16),
+            shape(wos.shape[1:], f32),
             shape(packs.shape, bf16),
             shape((4, seq, width), bf16),
             shape((2, HD), f32),
             shape((seq, columns), f32),
         ],
         in_specs=[ANY] * 8 + [IN_VMEM] * 8,
-        out_specs=[ANY] * 2 + [IN_VMEM] * 3,
+        out_specs=[IN_VMEM, ANY, ANY] + [IN_VMEM] * 2,
         scratch_shapes=[
             vmem(4, seq, width),
             vmem(*wos.shape),
             vmem(*packs.shape),
             wide_f(length, HD),
             vmem(*q.shape),
-            vmem(*ot.shape),
+            vmem(2, 2, HD, length),
             vmem(length, heads * HD),
             vmem(HD, length),
             vmem(length, wide),
             wide_f(length, HD),
             wide_f(length, HD),
             wide_f(length, HD),
-            vmem(2, wos.shape[0], wos.shape[1], 256),
             vmem(2, 4, packs.shape[2], wide),
+            vmem(nz, *wos.shape[1:]),
+            vmem(nz + 1, *wos.shape[1:]),
             dma((7,)),
             dma((2,)),
             dma((2,)),
         ]
-        + combine_scratch(nz, cap, seq, columns),
+        + line_sems(nz)
+        + combine_scratch(nz, cap, seq, columns, 0),
         compiler_params=pltpu.CompilerParams(
             collective_id=5, has_side_effects=True, vmem_limit_bytes=VMEM_BYTES
         ),
@@ -1320,53 +1694,28 @@
 
 
 def last_kernel(nz, cap, col, *refs):
-    gq, go, rows, part, tok, dh, gains, mlp_grad, head_grad, slots, gates = refs[:11]
-    oq, ok, ov, oo, all_gains, grad_tokens, mixed = refs[11:18]
-    own_q, own_o, sib_q, sib_o, b_q, b_o, swap_s, swap_r, gain_v = refs[18:27]
-    load, pair_s, pair_r, line_s, line_r, a_send, a_recv, g_send, g_recv, local = refs[27:37]
+    gq, rows, part, tok_in, dh_in, gains, mlp_grad, head_grad, slots, gates = refs[:10]
+    oq, ok, ov, all_gains, grad_tokens, mixed = refs[10:16]
+    own, sib, line_b, swap_s, swap_r, gain_v, part_v, tok, dh = refs[16:25]
+    load, a_send, a_recv, g_send, g_recv, local, in_sem = refs[25:32]
     p = Place()
-    order = pick_order(p, nz)
-    fold = Fold(p, part, *refs[37:45])
-    combine = Combine(p, nz, cap, col, rows, slots, gates, mixed, *refs[45:])
-
-    @pl.when(p.z == 0)
-    def _():
-        for ref in (b_q, b_o):
-            ref[pl.ds(0, nz)] = jnp.zeros((nz,) + ref.shape[1:], ref.dtype)
-
-    @pl.when(p.z == nz - 1)
-    def _():
-        for ref in (b_q, b_o):
-            ref[pl.ds(0, nz - 1)] = jnp.zeros((nz - 1,) + ref.shape[1:], ref.dtype)
-            ref[nz] = jnp.zeros(ref.shape[1:], ref.dtype)
-
+    fold = Fold(p, part_v, *refs[32:40], far=part)
+    line = LineSum(
+        p, nz, lambda z, k: gq.at[:, z * 2 + k], lambda z: own.at[z], sib, line_b, *refs[40:44]
+    )
+    combine = Combine(p, nz, cap, col, LAST_DEEP, rows, slots, gates, mixed, *refs[44:])
     combine.clear()
+    line.clear()
+    inputs = [
+        pltpu.make_async_copy(src, dst, in_sem.at[i])
+        for i, (src, dst) in enumerate(((part, part_v), (tok_in, tok), (dh_in, dh)))
+    ]
+    for copy in inputs:
+        copy.start()
     greet(p, nz, diagonal=True)
-    arrays = (
-        (0, lambda z, k: gq.at[:, z * 2 + k], own_q, sib_q, b_q),
-        (1, lambda z, k: go.at[z * 2 + k], own_o, sib_o, b_o),
-    )
-
-    def load_copy(i, z):
-        _, part, own, _, _ = arrays[i]
-        return pltpu.make_async_copy(part(z, p.k), own.at[z], load.at[i, z])
-
-    def pair_copy(i, z):
-        _, part, _, sib, _ = arrays[i]
-        return remote(part(z, 1 - p.k), sib.at[z], pair_s.at[i, z], pair_r.at[i, z], p.pair)
-
-    def copy_up(i, z):
-        _, _, s, _, b = arrays[i]
-        return remote(s.at[z], b.at[z], line_s.at[i, z], line_r.at[i, z], p.up)
-
-    def copy_down(i, z):
-        _, _, s, _, b = arrays[i]
-        slot = jnp.where(z == p.z - 1, nz, z)
-        return remote(s.at[z], b.at[slot], line_s.at[i, z], line_r.at[i, slot], p.down)
-
-    def line_recv(i, slot):
-        b = arrays[i][4]
-        remote(b.at[slot], b.at[slot], line_s.at[i, 0], line_r.at[i, slot], p.pair).wait_recv()
+
+    def load_copy(z):
+        return pltpu.make_async_copy(gq.at[:, z * 2 + p.k], own.at[z], load.at[z])
 
     def swaps():
         return [
@@ -1374,67 +1723,35 @@
             for n, (c, device) in enumerate(((p.cx, p.dx), (p.cy, p.dy), (p.cd, p.dd)))
         ]
 
-    def reduce(i, n):
-        z, last = order[n], n == nz - 1
-        _, _, own, sib, b = arrays[i]
-        load_copy(i, z).wait()
-        pair_copy(i, z).wait_recv()
-        if last:
-
-            @pl.when(p.z > 0)
-            def _():
-                line_recv(i, z)
-
-            @pl.when(p.z < nz - 1)
-            def _():
-                line_recv(i, nz)
-
-            total = own[z].astype(f32) + sib[z].astype(f32) + b[z].astype(f32)
-            total = total + b[nz].astype(f32)
-            if i:
-                oo[...] = total
-            else:
-                swap_s[...] = total.astype(swap_s.dtype)
-                for copy in swaps():
-                    copy.start()
-                swap_r[p.c] = swap_s[p.c]
-            return
-
-        @pl.when(((z > p.z) & (p.z > 0)) | ((z < p.z) & (p.z < nz - 1)))
-        def _():
-            line_recv(i, z)
-
-        total = own[z].astype(f32) + sib[z].astype(f32) + b[z].astype(f32)
-        own[z] = total.astype(own.dtype)
-
-        @pl.when(z > p.z)
-        def _():
-            copy_up(i, z).start()
-
-        @pl.when(z < p.z)
-        def _():
-            copy_down(i, z).start()
+    def swap(total):
+        swap_s[...] = total.astype(swap_s.dtype)
+        for copy in swaps():
+            copy.start()
+        swap_r[p.c] = swap_s[p.c]
 
     fold.begin()
-    for z in order:
-        for i in (1, 0):
-            pair_copy(i, z).start()
-            load_copy(i, z).start()
+    line.begin()
+    for z in line.order:
+        load_copy(z).start()
     combine.begin()
     steps = combine.steps()
     run = lambda n: [steps.pop(0)() for _ in range(min(n, len(steps)))]
-    reduce(1, 0)
-    reduce(0, 0)
+
+    def reduce(n):
+        load_copy(line.order[n]).wait()
+        line.reduce(n, swap)
+
+    reduce(0)
     run(1)
+    inputs[0].wait()
     fold.middle()
-    run(1)
-    reduce(1, 1)
-    reduce(0, 1)
-    run(1)
-
-    half = tok.shape[0] // 2
+    reduce(1)
+    run(2)
+
     gain_v[...] = jnp.zeros(gain_v.shape, f32)
     width = tok.shape[1]
+    for copy in inputs[1:]:
+        copy.wait()
 
     def store(lines, total):
         by_x, by_gain = rms_back(tok[lines].astype(f32), gains[0:1], total)
@@ -1454,8 +1771,7 @@
     run(1)
     job.step(1)
     for n in range(2, nz):
-        reduce(1, n)
-        reduce(0, n)
+        reduce(n)
         run(2)
         job.step(n)
     for i in range(nz, nz + 2):
@@ -1473,54 +1789,49 @@
     run(len(steps))
     for copy in swaps():
         copy.wait_send()
-    for n, z in enumerate(order):
-        for i in (0, 1):
-            pair_copy(i, z).wait_send()
-            if n < nz - 1:
-                copy_up(i, z).wait_send()
     keep.wait()
     job.finish()
     combine.finish()
-
-
-def reduce_last(nz, col, gq, go, rows, part, tok, dh, gains, mlp_grad, head_grad, slots, gates):
+    line.finish()
+
+
+def reduce_last(nz, col, gq, rows, part, tok, dh, gains, mlp_grad, head_grad, slots, gates):
     _, _, rows_q, wide = gq.shape
-    _, rows_o, width = go.shape
+    seq, width = tok.shape
     cap = rows.shape[1]
-    seq = tok.shape[0]
     kv = HD
     heads = wide - 2 * kv
     lines = -(-(2 * width // 128 + 2) // 16) * 16
     dma = pltpu.SemaphoreType.DMA
     shape = jax.ShapeDtypeStruct
     q = lambda *n: pltpu.VMEM(n + (4, rows_q, wide), bf16)
-    o = lambda *n: pltpu.VMEM(n + (rows_o, width), bf16)
     return pl.pallas_call(
         functools.partial(last_kernel, nz, cap, col),
         out_shape=[
             shape((rows_q, 4 * heads), f32),
             shape((rows_q, 4 * kv), f32),
             shape((rows_q, 4 * kv), f32),
-            shape((rows_o, width), f32),
             shape((8 * nz, lines, 128), f32),
             shape((seq, width), bf16),
             shape((seq, width - col), f32),
         ],
-        in_specs=[ANY] * 3 + [IN_VMEM] * 8,
-        out_specs=[IN_VMEM] * 4 + [ANY] + [IN_VMEM] * 2,
-        scratch_shapes=[q(nz), o(nz), q(nz), o(nz), q(nz + 1), o(nz + 1), q(), q()]
+        in_specs=[ANY] * 5 + [IN_VMEM] * 5,
+        out_specs=[IN_VMEM] * 3 + [ANY] + [IN_VMEM] * 2,
+        scratch_shapes=[q(nz), q(nz), q(nz + 1), q(), q()]
         + [pltpu.VMEM((lines, 128), f32)]
-        + [dma((2, nz))] * 4
-        + [dma((2, nz + 1))]
+        + [pltpu.VMEM((4, seq, width), bf16), pltpu.VMEM((seq, width), bf16)]
+        + [pltpu.VMEM((seq, width), f32)]
+        + [dma((nz,))]
         + [dma((3,))] * 2
         + spread_sems(nz)
-        + [dma]
+        + [dma, dma((3,))]
         + fold_scratch(seq, width)
-        + combine_scratch(nz, cap, seq, width - col),
+        + line_sems(nz)
+        + combine_scratch(nz, cap, seq, width - col, LAST_DEEP),
         compiler_params=pltpu.CompilerParams(
             collective_id=9, has_side_effects=True, vmem_limit_bytes=VMEM_BYTES
         ),
-    )(gq, go, rows, part, tok, dh, gains, mlp_grad, head_grad, slots, gates)
+    )(gq, rows, part, tok, dh, gains, mlp_grad, head_grad, slots, gates)
 
 
 def experts_kernel(
@@ -1530,9 +1841,9 @@
     cots,
     slots,
     gates,
-    wg,
-    wu,
-    wd,
+    wg_hbm,
+    wu_hbm,
+    wd_hbm,
     all_rows,
     produced,
     grad_inputs,
@@ -1555,8 +1866,18 @@
     load,
     out_sem,
     back_sem,
+    wg,
+    wu,
+    wd,
+    w_sem,
 ):
     p = Place()
+    weights = [
+        pltpu.make_async_copy(src, dst, w_sem.at[i])
+        for i, (src, dst) in enumerate(((wg_hbm, wg), (wu_hbm, wu), (wd_hbm, wd)))
+    ]
+    for copy in weights:
+        copy.start()
     greet(p, nz)
     job = Spread(p, nz, mine, by_device(all_rows, nz), mine.shape[0] // 2, send, recv)
     seq, width = mine.shape
@@ -1621,6 +1942,10 @@
             picked = jnp.dot(chosen, stage_x[i], preferred_element_type=f32)
             x[h, here] = picked.astype(bf16)
 
+        if n == 0:
+            for copy in weights:
+                copy.wait()
+
         @pl.loop(0, ff // narrow)
         def _(t):
             cols = pl.ds(pl.multiple_of(t * narrow, narrow), narrow)
@@ -1684,13 +2009,14 @@
         + [shape(blocks, cap, width)] * 2
         + [shape(nz, 2, rows, width)] * 2
         + [shape(nz, 2, rows, ff)] * 3,
-        in_specs=[ANY] * 2 + [IN_VMEM] * 5,
+        in_specs=[ANY] * 2 + [IN_VMEM] * 2 + [ANY] * 3,
         out_specs=[ANY] * 8,
         scratch_shapes=[vmem(4, seq, width), vmem(2, 4, seq, width)]
         + [vmem(2, rows, width)] * 4
         + [vmem(2, rows, ff)] * 3
         + spread_sems(nz)
-        + [dma((3, 4)), dma((2, 5)), dma((2, 2, 4))],
+        + [dma((3, 4)), dma((2, 5)), dma((2, 2, 4))]
+        + [vmem(*wg.shape), vmem(*wu.shape), vmem(*wd.shape), dma((3,))],
         compiler_params=pltpu.CompilerParams(
             collective_id=3, has_side_effects=True, vmem_limit_bytes=VMEM_BYTES
         ),
@@ -1776,7 +2102,7 @@
     produced, grad_inputs, arrived, grad_arrived, activated, grad_gate_pre, grad_up_pre = run_experts(
         nz, cap, normed_mlp, cots, slots2, gates2, expert_gate[0], expert_up[0], expert_down[0]
     )
-    grad_normed_mlp = combine(nz, grad_inputs, slots2, jnp.ones_like(gates2), 4)
+    grad_normed_mlp = combine(nz, 32, grad_inputs, slots2, jnp.ones_like(gates2), 4)
     arrived, grad_arrived, activated, grad_gate_pre, grad_up_pre = (
         a.reshape(devices * cap, -1)
         for a in (arrived, grad_arrived, activated, grad_gate_pre, grad_up_pre)
@@ -1791,7 +2117,7 @@
     grad_hidden = grad_out + grad_hidden_norm
     branch = gather_rows(nz, False, grad_hidden.astype(bf16), 6)
     columns = width // 2
-    grad_wo, grad_weight, part, grad_head, mixed_low = back(
+    sum_o, grad_weight, part, grad_head, mixed_low = back(
         nz,
         scale,
         columns,
@@ -1811,11 +2137,10 @@
         slots2,
         gates2,
     )
-    sum_q, sum_k, sum_v, sum_o, all_gain_parts, grad_input, mixed_high = reduce_last(
+    sum_q, sum_k, sum_v, all_gain_parts, grad_input, mixed_high = reduce_last(
         nz,
         columns,
         grad_weight,
-        grad_wo,
         produced,
         part,
         tokens.reshape(seq, width),

time: 947 us -> 915 us (0.966)
  Pallas kernels: 880 us -> 844 us
    pallas_call x1, Pallas kernels: 246 us -> 229 us  [front(): pl.pallas_call(functools.partial(front_kernel, nz, scale), out_shape=[jax...]
    pallas_call x1, Pallas kernels: 151 us -> 136 us  [reduce_last(): pl.pallas_call(functools.partial(last_kernel, nz, cap, col), out_shape=[s...]
    pallas_call x1, Pallas kernels: 146 us -> 136 us  [combine(): pl.pallas_call(functools.partial(combine_kernel, nz, cap, deep), out_shap...]
where the time goes in v4:
time: 915 us; the launch traced here: 906 us
  Pallas kernels  844 us (92%)
  matrix products  36.4 us (4%)
  other arithmetic  14.7 us (2%)
  local copies, waits for them, and re-layouts  9.9 us (1%)
    pallas_call x1, Pallas kernels, front(): pl.pallas_call(functools.partial(front_kernel, nz, scale), out_shape=[jax...  229 us
    pallas_call x1, Pallas kernels, run_experts(): pl.pallas_call(functools.partial(experts_kernel, nz, cap), out_shape=[sha...  191 us
    pallas_call x1, Pallas kernels, reduce_last(): pl.pallas_call(functools.partial(last_kernel, nz, cap, col), out_shape=[s...  136 us
    pallas_call x1, Pallas kernels, combine(): pl.pallas_call(functools.partial(combine_kernel, nz, cap, deep), out_shap...  136 us
    pallas_call x1, Pallas kernels, back(): pl.pallas_call(functools.partial(back_kernel, nz, cap, scale), out_shape=...  113 us
    pallas_call x1, Pallas kernels, gather_rows(): pl.pallas_call(functools.partial(spread_kernel, nz, everywhere), out_shap...  39.2 us
    dot_general x3, matrix products, mm(): lax.dot_general(a, b, ((contract[:1], contract[1:]), ((), ())), preferred...  36.4 us

profile of v4, /device:TPU:16, one launch (start us, length us, event | category | flops | bytes accessed | tf_op | source)
XLA Modules:
  0.0 906.4 jit_solution(12074580409003644995)
XLA Ops:
  0.6 0.0 copy-start
  0.7 0.0 copy-start.11
  0.7 0.0 copy-start.8
  0.7 0.7 tile.20
  1.4 0.1 tile.21
  1.5 0.7 tile.8
  2.2 0.1 tile.9
  2.3 0.7 convert_bitcast_fusion
  3.0 0.7 reshape.194
  3.7 0.6 select_maximum_fusion.refs_4_
  4.3 1.9 fusion.3
  6.2 1.3 pad_maximum_fusion.1
  7.6 0.0 copy-done
  7.6 0.0 copy-done.11
  7.6 0.0 copy-done.8
  7.6 0.9 pad_maximum_fusion.refs_0_
  8.5 228.6 %shard_map.212 = (bf16[4,8,64,1280]{3,2,1,0:T(8,128)(2,1)}, bf16[8,128,2048]{2,1,0:T(8,128)(2,1)}, bf16[4,256,2048]{2,1,0:T(8,128)(2,1)}, bf16[32,256,2048]{2,1,...) custom-call(bf16[4,64,1280]{2,1,0:T(8,128)(2,1)} %pad_maximum_fusion, ...), custom_call_target="tpu_custom_call" | custom-call | tf_op jit(solution)/shard_map/pallas_call | solution.py:991
  237.1 191.5 %shard_map.213 = (bf16[32,256,2048]{2,1,0:T(8,128)(2,1)}, bf16[32,80,2048]{2,1,0:T(8,128)(2,1)}, bf16[32,80,2048]{2,1,0:T(8,128)(2,1)}, bf16[4,2,320,2048]{3,2,1...) custom-call(bf16[256,2048]{1,0:T(8,128)(2,1)} %get-tuple-element.46., ...), custom_call_target="tpu_custom_call" | custom-call | tf_op jit(solution)/shard_map/pallas_call | solution.py:2006
  428.6 0.0 copy-start.13
  428.6 0.0 copy-start.15
  428.6 14.1 %convolution_bitcast_fusion = f32[1,768,2048]{2,1,0:T(8,128)} fusion(bf16[4,2,320,768]{3,2,1,0:T(8,128)(2,1)} %get-tuple-element.77, bf16[4,2,320,2048]{3,2,1,0:T(8,128)(2,1)} %get-tuple-element.78), kind=kOutput, calls=%fused_computation | convolution fusion | flops 8053063680 | bytes 20709376 | tf_op jit(solution)/shard_map/dot_general | solution.py:2027
  442.7 0.0 copy-done.13
  442.7 0.0 copy-done.15
  442.7 11.0 %convolution_bitcast_fusion.1 = f32[1,2048,768]{2,1,0:T(8,128)} fusion(bf16[4,2,320,2048]{3,2,1,0:T(8,128)(2,1)S(1)} %copy-done.13, bf16[4,2,320,768]{3,2,1,0:T(8,128)(2,1)S(1)} %copy-done.15), kind=kOutput, calls=%fused_computation.1 | convolution fusion | flops 8053063680 | bytes 20709376 | tf_op jit(solution)/shard_map/dot_general | solution.py:2027
  453.7 0.0 copy-done.14
  453.7 11.4 %convolution_bitcast_fusion.2 = f32[1,2048,768]{2,1,0:T(8,128)} fusion(bf16[4,2,320,2048]{3,2,1,0:T(8,128)(2,1)S(1)} %copy-done.13, bf16[4,2,320,768]{3,2,1,0:T(8,128)(2,1)S(1)} %copy-done.14), kind=kOutput, calls=%fused_computation.2 | convolution fusion | flops 8053063680 | bytes 20709376 | tf_op jit(solution)/shard_map/dot_general | solution.py:2027
  465.0 0.6 broadcast_in_dim.41.gates
  465.7 135.9 %shard_map.214 = f32[256,2048]{1,0:T(8,128)} custom-call(bf16[32,80,2048]{2,1,0:T(8,128)(2,1)} %get-tuple-element.50.rows, s32[2,32,256]{2,1,0:T(8,128)} %get-tuple-element.48.slots.refs_14_.refs_8_, f32[2,32,256]{2,1,0:T(8,128)} %broadcast_in_dim.41.gates), custom_call_target="tpu_custom_call" | custom-call | tf_op jit(solution)/shard_map/pallas_call | solution.py:1371
  601.6 0.0 copy-start.3
  601.6 0.0 copy-start.4
  601.6 0.0 copy-done.12
  601.7 0.2 multiply_reduce_fusion.2
  601.9 2.9 multiply_reduce_fusion
  604.8 0.0 copy-done.4
  604.8 2.4 fusion.7
  607.1 39.2 %shard_map.215.refs_0_ = bf16[4,256,2048]{2,1,0:T(8,128)(2,1)} custom-call(bf16[256,2048]{1,0:T(8,128)(2,1)} %get-tuple-element.81.mine), custom_call_target="tpu_custom_call" | custom-call | tf_op jit(solution)/shard_map/pallas_call | solution.py:1040
  646.4 113.1 %shard_map.216 = (f32[128,2048]{1,0:T(8,128)}, bf16[4,8,64,1280]{3,2,1,0:T(8,128)(2,1)}, bf16[4,256,2048]{2,1,0:T(8,128)(2,1)}, f32[2,128]{1,0:T(2,128)}, f32[256,1024]{1,0:T(8,128)}) custom-call(bf16[4,256,2048]{2,1,0:T(8,128)(2,1)} %shard_map.215.refs_0_, bf16[8,128,2048]{2,1,0:T(8,128)(2,1)} %get-tuple-element.52.refs_1_, ...), custom_call_target="tpu_custom_call" | custom-call | tf_op jit(solution)/shard_map/pallas_call | solution.py:1657
  759.5 136.0 %shard_map.217 = (f32[64,4096]{1,0:T(8,128)}, f32[64,512]{1,0:T(8,128)}, f32[64,512]{1,0:T(8,128)}, f32[32,48,128]{2,1,0:T(8,128)}, bf16[256,2048]{1,0:T(8,128)(2,1)}, /*index=5*/f32[256,1024]{1,0:T(8,128)}) custom-call(bf16[4,8,64,1280]{3,2,1,0:T(8,128)(2,1)} %get-tuple-element.64.refs_0_, bf16[32,80,2048]{2,1,0:T(8,128)(2,1)} %get-tuple-element.58.refs_7_.refs_1_, ...), custom_call_target="tpu_custom_call" | custom-call | tf_op jit(solution)/shard_map/pallas_call | solution.py:1808
  895.5 0.0 copy-start.1
  895.6 2.5 fusion.2
  898.1 1.3 reduce_sum.41
  899.4 0.6 constant_dynamic-slice_fusion.1
  900.1 0.6 constant_dynamic-slice_fusion
  900.7 2.3 copy.42
  903.0 1.0 copy.43
  904.0 0.7 copy.44
  904.6 0.7 copy.45
  905.3 1.0 copy.46
  (30 shorter events, 0.2 us)
Async XLA Ops:
  0.6 6.9 copy-start
  0.7 6.9 copy-start.11
  0.7 6.9 copy-start.8
  428.6 14.1 %copy-start.13 = (bf16[4,2,320,2048]{3,2,1,0:T(8,128)(2,1)S(1)}, bf16[4,2,320,2048]{3,2,1,0:T(8,128)(2,1)}, u32[]{:S(2)}) copy-start(bf16[4,2,320,2048]{3,2,1,0:T(8,128)(2,1)} %get-tuple-element.74) | copy-start | bytes 31457284
  428.6 14.1 %copy-start.15 = (bf16[4,2,320,768]{3,2,1,0:T(8,128)(2,1)S(1)}, bf16[4,2,320,768]{3,2,1,0:T(8,128)(2,1)}, u32[]{:S(2)}) copy-start(bf16[4,2,320,768]{3,2,1,0:T(8,128)(2,1)} %get-tuple-element.76) | copy-start | bytes 11796484
  442.7 11.0 %copy-start.14 = (bf16[4,2,320,768]{3,2,1,0:T(8,128)(2,1)S(1)}, bf16[4,2,320,768]{3,2,1,0:T(8,128)(2,1)}, u32[]{:S(2)}) copy-start(bf16[4,2,320,768]{3,2,1,0:T(8,128)(2,1)} %get-tuple-element.75) | copy-start | bytes 11796484
  465.7 136.0 %copy-start.12 = (f32[2,2048]{1,0:T(2,128)S(1)}, f32[2,2048]{1,0:T(2,128)}, u32[]{:S(2)}) copy-start(f32[2,2048]{1,0:T(2,128)} %get-tuple-element.51.refs_5_) | copy-start | bytes 49156
  465.7 136.0 %copy-start.2 = (f32[256,2048]{1,0:T(8,128)S(1)}, f32[256,2048]{1,0:T(8,128)}, u32[]{:S(2)}) copy-start(f32[256,2048]{1,0:T(8,128)} %get-tuple-element.45) | copy-start | bytes 6291460
  601.6 3.2 copy-start.3
  601.6 3.1 copy-start.4
  759.5 136.0 %copy-start.5 = (f32[256,1024]{1,0:T(8,128)S(1)}, f32[256,1024]{1,0:T(8,128)}, u32[]{:S(2)}) copy-start(f32[256,1024]{1,0:T(8,128)} %get-tuple-element.63) | copy-start | bytes 3145732
  895.5 7.5 copy-start.7
  895.5 8.4 copy-start.10
  895.5 10.7 %copy-start.1 = (bf16[64,512]{1,0:T(8,128)(2,1)S(1)}, bf16[64,512]{1,0:T(8,128)(2,1)}, u32[]{:S(2)}) copy-start(bf16[64,512]{1,0:T(8,128)(2,1)} %param.15) | copy-start | bytes 196612
  898.1 6.5 copy-start.9
  898.1 7.2 copy-start.6

commit v5 on v4

--- a/solution.py
+++ b/solution.py
@@ -847,6 +847,7 @@
         here = pl.ds(pl.multiple_of(i * half, half), half)
         xn[here] = rms(rows, gain_out[0:1]).astype(bf16)
 
+    j_cot.step(1)
     loads[0].wait()
 
     @pl.loop(0, raw.shape[1] // 256)
@@ -856,9 +857,9 @@
         raw[:, cols] = jnp.dot(xn[...], w, preferred_element_type=f32)
 
     copy_out(0, 1, 9, 10)
-    j_cot.step(1)
+    j_wo.step(1)
+    j_cot.step(2)
     j_deep.step(1)
-    j_wo.step(1)
 
     def prep(x, g):
         y = rms(x, g)
@@ -891,13 +892,14 @@
             lse[h, :, here] = largest + jnp.log(total)
 
     pl.loop(0, heads // 2)(attend)
+    j_cot.step(3)
     j_wo.step(2)
-    j_cot.step(2)
     j_deep.step(2)
     pl.loop(heads // 2, heads)(attend)
     copy_out(2, 5, 6)
-    for i in range(3, nz + 2):
-        j_wo.step(i)
+    j_wo.step(3)
+    j_cot.step(4)
+    j_deep.step(3)
     own[1].wait()
     for z in j_wo.order:
         j_wo.from_pair(z)
@@ -936,8 +938,8 @@
 
     fold = Fold(p, part, *fold_refs)
     fold.begin()
-    j_cot.step(3)
-    j_deep.step(3)
+    j_cot.step(5)
+    j_deep.step(4)
     fold.middle()
 
     def store(rows, total):
@@ -947,9 +949,7 @@
 
     fold.end(store)
     copy_out(7, 8)
-    for i in range(4, nz + 2):
-        j_cot.step(i)
-        j_deep.step(i)
+    j_deep.step(5)
     for copy in swaps:
         copy.wait_send()
     for spread in (j_tok, j_meta, j_cot, j_wo, j_pack):
@@ -1020,33 +1020,6 @@
     )(pack, wo, tok, cot, meta, cosine, sine)
 
 
-def spread_kernel(nz, everywhere, mine, out, send, recv, local):
-    p = Place()
-    greet(p, nz, line=everywhere, pair=everywhere)
-    block = by_device(out, nz) if everywhere else (lambda c, z, k: out.at[c])
-    keep = pltpu.make_async_copy(mine, block(p.c, p.z, p.k), local)
-    keep.start()
-    job = Spread(
-        p, nz, mine, block, mine.shape[0] // 2, send, recv, everywhere, True, everywhere
-    )
-    for far in range(nz + 2 if everywhere else 3):
-        job.step(far)
-    keep.wait()
-    job.finish()
-
-
-def gather_rows(nz, everywhere, mine, collective_id):
-    blocks = 8 * nz if everywhere else 4
-    return pl.pallas_call(
-        functools.partial(spread_kernel, nz, everywhere),
-        out_shape=jax.ShapeDtypeStruct((blocks,) + mine.shape, mine.dtype),
-        in_specs=[IN_VMEM],
-        out_specs=ANY,
-        scratch_shapes=spread_sems(nz) + [pltpu.SemaphoreType.DMA],
-        compiler_params=pltpu.CompilerParams(collective_id=collective_id, has_side_effects=True),
-    )(mine)
-
-
 class Combine:
     def __init__(self, p, nz, cap, col, deep, rows, slots, gates, out, *scratch):
         self.p, self.nz, self.cap, self.rows, self.slots, self.gates = p, nz, cap, rows, slots, gates
@@ -1354,30 +1327,138 @@
     )
 
 
-def combine_kernel(nz, cap, deep, rows, slots, gates, out, *scratch):
+class WeightGrads:
+    def __init__(self, pairs, outs, held, tiles, stage, stage_t, load, load_held, out_sem):
+        self.pairs, self.outs, self.held, self.tiles = pairs, outs, held, tiles
+        self.stage, self.stage_t = stage, stage_t
+        self.load, self.load_held, self.out_sem = load, load_held, out_sem
+        self.wide = tiles.shape[2]
+        self.per = pairs[0][0].shape[1] // self.wide
+        self.count = self.per * len(pairs)
+        self.next = 0
+
+    def columns(self, u):
+        return pl.ds(u % self.per * self.wide, self.wide)
+
+    def tile_copy(self, u):
+        src = self.pairs[u // self.per][0].at[:, self.columns(u)]
+        return pltpu.make_async_copy(src, self.tiles.at[u % 2], self.load.at[u % 2])
+
+    def held_copy(self, n):
+        return pltpu.make_async_copy(self.pairs[n][1], self.held, self.load_held)
+
+    def out_copy(self, u):
+        n = u // self.per
+        if n < 2:
+            return pltpu.make_async_copy(self.stage, self.outs[n].at[self.columns(u)], self.out_sem)
+        out = self.outs[n].at[:, self.columns(u)]
+        return pltpu.make_async_copy(self.stage_t, out, self.out_sem)
+
+    def begin(self):
+        self.held_copy(0).start()
+        self.tile_copy(0).start()
+        self.tile_copy(1).start()
+
+    def unit(self):
+        u = self.next
+        if u == self.count:
+            return
+        self.next = u + 1
+        n = u // self.per
+        if u % self.per == 0:
+            self.held_copy(n).wait()
+        self.tile_copy(u).wait()
+        total = lax.dot_general(
+            self.tiles[u % 2], self.held[...], TN, preferred_element_type=f32
+        )
+        if u:
+            self.out_copy(u - 1).wait()
+        if n < 2:
+            self.stage[...] = total
+        else:
+            self.stage_t[...] = total.T
+        self.out_copy(u).start()
+        if u + 2 < self.count:
+            self.tile_copy(u + 2).start()
+        if u + 1 < self.count and (u + 1) % self.per == 0:
+            self.held_copy(n + 1).start()
+
+    def finish(self):
+        while self.next < self.count:
+            self.unit()
+        self.out_copy(self.count - 1).wait()
+
+
+def middle_kernel(nz, cap, deep, *refs):
+    rows, x, dr, a, dg, du, slots, gates, hidden, cot, gains = refs[:11]
+    grad_hidden, mlp_grad, branch, out_gate, out_up, out_down = refs[11:17]
+    low, local, send, recv = refs[17:21]
     p = Place()
-    job = Combine(p, nz, cap, 0, deep, rows, slots, gates, out, *scratch)
+    work = WeightGrads(((x, dg), (x, du), (dr, a)), (out_gate, out_up, out_down), *refs[21:28])
+    job = Combine(p, nz, cap, 0, deep, rows, slots, gates, grad_hidden, *refs[28:])
     job.clear()
     greet(p, nz)
     job.begin()
-    for step in job.steps():
+    work.begin()
+    for i, step in enumerate(job.steps()):
         step()
+        if i >= 4 and i % 2:
+            work.unit()
+    seq = cot.shape[0]
+    mlp_grad[...] = jnp.zeros(mlp_grad.shape, f32)
+    for first in range(0, seq, seq // 4):
+        lines = pl.ds(first, seq // 4)
+        by_x, by_gain = rms_back(hidden[lines], gains[1:2], grad_hidden[lines])
+        total = cot[lines].astype(f32) + by_x
+        grad_hidden[lines] = total
+        low[lines] = total.astype(bf16)
+        mlp_grad[...] += by_gain
+    keep = pltpu.make_async_copy(low, branch.at[p.c], local)
+    keep.start()
+    gather = Spread(
+        p, nz, low, lambda c, z, k: branch.at[c], seq // 2, send, recv, False, True, False
+    )
+    gather.step(0)
+    for i in range(8):
+        work.unit()
+    gather.step(1)
+    work.finish()
+    gather.step(2)
+    keep.wait()
+    gather.finish()
     job.finish()
 
 
-def combine(nz, deep, rows, slots, gates, collective_id):
+def middle(nz, deep, rows, x, dr, a, dg, du, slots, gates, hidden, cot, gains):
     _, cap, width = rows.shape
     seq = slots.shape[2]
+    ff = a.shape[1]
+    shape = jax.ShapeDtypeStruct
+    dma = pltpu.SemaphoreType.DMA
+    vmem = lambda *n: pltpu.VMEM(n, bf16)
+    tile = min(256, ff)
     return pl.pallas_call(
-        functools.partial(combine_kernel, nz, cap, deep),
-        out_shape=jax.ShapeDtypeStruct((seq, width), f32),
-        in_specs=[ANY, IN_VMEM, IN_VMEM],
-        out_specs=IN_VMEM,
-        scratch_shapes=combine_scratch(nz, cap, seq, width, deep),
+        functools.partial(middle_kernel, nz, cap, deep),
+        out_shape=[
+            shape((seq, width), f32),
+            shape((1, width), f32),
+            shape((4, seq, width), bf16),
+            shape((width, ff), f32),
+            shape((width, ff), f32),
+            shape((ff, width), f32),
+        ],
+        in_specs=[ANY] * 6 + [IN_VMEM] * 5,
+        out_specs=[IN_VMEM] * 2 + [ANY] * 4,
+        scratch_shapes=[vmem(seq, width), dma]
+        + spread_sems(nz)
+        + [vmem(*a.shape), vmem(2, x.shape[0], tile)]
+        + [pltpu.VMEM((tile, ff), f32), pltpu.VMEM((ff, tile), f32)]
+        + [dma((2,)), dma, dma]
+        + combine_scratch(nz, cap, seq, width, deep),
         compiler_params=pltpu.CompilerParams(
-            collective_id=collective_id, has_side_effects=True, vmem_limit_bytes=VMEM_BYTES
+            collective_id=4, has_side_effects=True, vmem_limit_bytes=VMEM_BYTES
         ),
-    )(rows, slots, gates)
+    )(rows, x, dr, a, dg, du, slots, gates, hidden, cot, gains)
 
 
 class LineSum:
@@ -1767,15 +1848,15 @@
     keep = pltpu.make_async_copy(gain_v, block(p.c, p.z, p.k), local)
     keep.start()
     job = Spread(p, nz, gain_v, block, gain_v.shape[0] // 2, g_send, g_recv)
+    run(2)
+    reduce(2)
     job.step(0)
+    run(2)
+    job.step(1)
+    reduce(3)
     run(1)
-    job.step(1)
-    for n in range(2, nz):
-        reduce(n)
-        run(2)
+    for n in range(2, nz + 2):
         job.step(n)
-    for i in range(nz, nz + 2):
-        job.step(i)
         run(1)
     for n, c in enumerate((p.cx, p.cy, p.cd)):
         ref = swap_r.at[c]
@@ -2102,20 +2183,20 @@
     produced, grad_inputs, arrived, grad_arrived, activated, grad_gate_pre, grad_up_pre = run_experts(
         nz, cap, normed_mlp, cots, slots2, gates2, expert_gate[0], expert_up[0], expert_down[0]
     )
-    grad_normed_mlp = combine(nz, 32, grad_inputs, slots2, jnp.ones_like(gates2), 4)
-    arrived, grad_arrived, activated, grad_gate_pre, grad_up_pre = (
-        a.reshape(devices * cap, -1)
-        for a in (arrived, grad_arrived, activated, grad_gate_pre, grad_up_pre)
-    )
-    grad_down = mm(activated, grad_arrived, (0, 0))
-    grad_gate = mm(arrived, grad_gate_pre, (0, 0))
-    grad_up = mm(arrived, grad_up_pre, (0, 0))
-
-    grad_out = cotangent.reshape(seq, width).astype(f32)
-    _, norm_pull = jax.vjp(rms_scale, hidden, gains[1])
-    grad_hidden_norm, grad_gain_mlp = norm_pull(grad_normed_mlp)
-    grad_hidden = grad_out + grad_hidden_norm
-    branch = gather_rows(nz, False, grad_hidden.astype(bf16), 6)
+    grad_hidden, grad_gain_mlp, branch, grad_gate, grad_up, grad_down = middle(
+        nz,
+        DEEP,
+        grad_inputs,
+        *(
+            a.reshape(devices * cap, -1)
+            for a in (arrived, grad_arrived, activated, grad_gate_pre, grad_up_pre)
+        ),
+        slots2,
+        jnp.ones_like(gates2),
+        hidden,
+        cotangent.reshape(seq, width),
+        gains,
+    )
     columns = width // 2
     sum_o, grad_weight, part, grad_head, mixed_low = back(
         nz,
@@ -2146,7 +2227,7 @@
         tokens.reshape(seq, width),
         grad_hidden,
         gains,
-        grad_gain_mlp.reshape(1, width),
+        grad_gain_mlp,
         grad_head,
         slots2,
         gates2,

time: 915 us -> 867 us (0.948)
  matrix products: 36.4 us -> 0 us
  Pallas kernels: 844 us -> 826 us
  local copies, waits for them, and re-layouts: 9.9 us -> 21.7 us
    dot_general x3 -> x0, matrix products: 36.4 us -> none  [mm(): lax.dot_general(a, b, ((contract[:1], contract[1:]), ((), ())), preferred...]
    unnamed x37 -> x36, local copies, waits for them, and re-layouts: 5.63 us -> 17.4 us
    pallas_call x1, Pallas kernels: 136 us -> 125 us  [reduce_last(): pl.pallas_call(functools.partial(last_kernel, nz, cap, col), out_shape=[s...]
    pallas_call x2 -> x1, Pallas kernels: 175 us -> 180 us  [middle(): pl.pallas_call(functools.partial(middle_kernel, nz, cap, deep), out_shape...]
where the time goes in v5:
time: 867 us; the launch traced here: 858 us
  Pallas kernels  826 us (95%)
  local copies, waits for them, and re-layouts  21.7 us (3%)
  other arithmetic  9.25 us (1%)
    pallas_call x1, Pallas kernels, front(): pl.pallas_call(functools.partial(front_kernel, nz, scale), out_shape=[jax...  220 us
    pallas_call x1, Pallas kernels, run_experts(): pl.pallas_call(functools.partial(experts_kernel, nz, cap), out_shape=[sha...  184 us
    pallas_call x1, Pallas kernels, middle(): pl.pallas_call(functools.partial(middle_kernel, nz, cap, deep), out_shape...  180 us
    pallas_call x1, Pallas kernels, reduce_last(): pl.pallas_call(functools.partial(last_kernel, nz, cap, col), out_shape=[s...  125 us
    pallas_call x1, Pallas kernels, back(): pl.pallas_call(functools.partial(back_kernel, nz, cap, scale), out_shape=...  117 us
    unnamed x36, local copies, waits for them, and re-layouts  17.4 us

profile of v5, /device:TPU:16, one launch (start us, length us, event | category | flops | bytes accessed | tf_op | source)
XLA Modules:
  0.0 858.0 jit_solution(5803079831978576690)
XLA Ops:
  0.6 0.0 copy-start
  0.7 0.0 copy-start.9
  0.7 0.0 copy-start.6
  0.7 0.7 tile.20
  1.4 0.1 tile.21
  1.5 0.7 tile.8
  2.2 0.1 tile.9
  2.3 0.7 convert_bitcast_fusion
  3.0 0.7 reshape.182
  3.7 0.6 select_maximum_fusion.refs_4_
  4.3 1.9 fusion.2
  6.2 1.3 pad_maximum_fusion.1
  7.6 0.0 copy-done
  7.6 0.0 copy-done.9
  7.6 0.0 copy-done.6
  7.6 0.9 pad_maximum_fusion.refs_0_
  8.5 219.5 %shard_map.212 = (bf16[4,8,64,1280]{3,2,1,0:T(8,128)(2,1)}, bf16[8,128,2048]{2,1,0:T(8,128)(2,1)}, bf16[4,256,2048]{2,1,0:T(8,128)(2,1)}, bf16[32,256,2048]{2,1,...) custom-call(bf16[4,64,1280]{2,1,0:T(8,128)(2,1)} %pad_maximum_fusion, ...), custom_call_target="tpu_custom_call" | custom-call | tf_op jit(solution)/shard_map/pallas_call | solution.py:991
  228.1 183.8 %shard_map.213 = (bf16[32,256,2048]{2,1,0:T(8,128)(2,1)}, bf16[32,80,2048]{2,1,0:T(8,128)(2,1)}, bf16[32,80,2048]{2,1,0:T(8,128)(2,1)}, bf16[4,2,320,2048]{3,2,1...) custom-call(bf16[256,2048]{1,0:T(8,128)(2,1)} %get-tuple-element.52., ...), custom_call_target="tpu_custom_call" | custom-call | tf_op jit(solution)/shard_map/pallas_call | solution.py:2087
  411.9 0.6 broadcast_in_dim.37.refs_7_
  412.5 180.3 %shard_map.214 = (f32[256,2048]{1,0:T(8,128)}, f32[1,2048]{1,0:T(1,128)}, bf16[4,256,2048]{2,1,0:T(8,128)(2,1)}, f32[2048,768]{1,0:T(8,128)}, f32[2048,768]{1,0:T(8,128)}, /*index=5*/f32[768,2048]{1,0:T(8,128)}) custom-call(bf16[32,80,2048]{2,1,0:T(8,128)(2,1)} %get-tuple-element.56.refs_0_, bf16[2560,2048]{1,0:T(8,128)(2,1)} %bitcast.45, ...), custom_call_target="tpu_custom_call" | custom-call | tf_op jit(solution)/shard_map/pallas_call | solution.py:1440
  592.8 117.2 %shard_map.215 = (f32[128,2048]{1,0:T(8,128)}, bf16[4,8,64,1280]{3,2,1,0:T(8,128)(2,1)}, bf16[4,256,2048]{2,1,0:T(8,128)(2,1)}, f32[2,128]{1,0:T(2,128)}, f32[256,1024]{1,0:T(8,128)}) custom-call(bf16[4,256,2048]{2,1,0:T(8,128)(2,1)} %get-tuple-element.63.refs_0_, bf16[8,128,2048]{2,1,0:T(8,128)(2,1)} %get-tuple-element.64.refs_1_, ...), custom_call_target="tpu_custom_call" | custom-call | tf_op jit(solution)/shard_map/pallas_call | solution.py:1738
  709.9 0.0 copy-start.2
  709.9 0.0 copy-start.3
  710.0 125.2 %shard_map.216 = (f32[64,4096]{1,0:T(8,128)}, f32[64,512]{1,0:T(8,128)}, f32[64,512]{1,0:T(8,128)}, f32[32,48,128]{2,1,0:T(8,128)}, bf16[256,2048]{1,0:T(8,128)(2,1)}, /*index=5*/f32[256,1024]{1,0:T(8,128)}) custom-call(bf16[4,8,64,1280]{3,2,1,0:T(8,128)(2,1)} %get-tuple-element.76.refs_0_, bf16[32,80,2048]{2,1,0:T(8,128)(2,1)} %get-tuple-element.70.refs_7_.refs_1_, ...), custom_call_target="tpu_custom_call" | custom-call | tf_op jit(solution)/shard_map/pallas_call | solution.py:1889
  835.2 0.0 copy-start.5
  835.2 0.0 copy-done.2
  835.2 0.0 copy-done.3
  835.2 0.0 copy-start.8
  835.2 0.0 copy-start.7
  835.2 0.0 copy-start.4
  835.2 2.6 fusion.1
  837.8 1.2 reduce_sum.9
  839.1 0.6 constant_dynamic-slice_fusion.1
  839.7 0.6 constant_dynamic-slice_fusion
  840.3 2.3 copy.42
  842.6 0.0 copy-done.5
  842.7 1.0 copy.43
  843.6 0.0 copy-done.8
  843.6 0.7 copy.44
  844.3 0.0 copy-done.7
  844.3 0.7 copy.45
  844.9 0.0 copy-done.4
  844.9 1.0 copy.46
  845.9 6.1 copy.47
  852.0 0.0 copy-start.1
  852.0 2.8 copy.48
  854.8 0.2 slice-done.1
  855.1 2.7 copy.49
  (21 shorter events, 0.1 us)
Async XLA Ops:
  0.6 6.9 copy-start
  0.7 6.9 copy-start.9
  0.7 6.9 copy-start.6
  709.9 125.3 %copy-start.2 = (f32[256,2048]{1,0:T(8,128)S(1)}, f32[256,2048]{1,0:T(8,128)}, u32[]{:S(2)}) copy-start(f32[256,2048]{1,0:T(8,128)} %get-tuple-element.51.refs_8_) | copy-start | bytes 6291460
  709.9 125.3 %copy-start.3 = (f32[256,1024]{1,0:T(8,128)S(1)}, f32[256,1024]{1,0:T(8,128)}, u32[]{:S(2)}) copy-start(f32[256,1024]{1,0:T(8,128)} %get-tuple-element.75) | copy-start | bytes 3145732
  835.2 7.5 copy-start.5
  835.2 8.4 copy-start.8
  835.2 9.1 %copy-start.7 = (f32[64,512]{1,0:T(8,128)S(1)}, f32[64,512]{1,0:T(8,128)}, u32[]{:S(2)}) copy-start(f32[64,512]{1,0:T(8,128)} %get-tuple-element.115) | copy-start | bytes 393220
  835.2 9.7 %copy-start.4 = (f32[128,2048]{1,0:T(8,128)S(1)}, f32[128,2048]{1,0:T(8,128)}, u32[]{:S(2)}) copy-start(f32[128,2048]{1,0:T(8,128)} %get-tuple-element.116) | copy-start | bytes 3145732
  842.7 9.3 %slice-start.2 = ((s8[6291456]{0:T(1024)(128)(4,1)}), s8[4194304]{0:T(1024)(128)(4,1)S(1)}, s32[]{:S(2)}) async-start(s8[6291456]{0:T(1024)(128)(4,1)} %bitcast.50), calls=%async_computation.2 | async-start | bytes 8388608
  845.9 6.1 slice-start.3
  845.9 8.9 %slice-start = ((s8[6291456]{0:T(1024)(128)(4,1)}), s8[4194304]{0:T(1024)(128)(4,1)S(1)}, s32[]{:S(2)}) async-start(s8[6291456]{0:T(1024)(128)(4,1)} %bitcast.47), calls=%async_computation | async-start | bytes 8388608
  852.0 3.1 slice-start.1
  852.0 5.8 copy-start.1

commit v6 on v5

--- a/solution.py
+++ b/solution.py
@@ -1402,7 +1402,9 @@
     work.begin()
     for i, step in enumerate(job.steps()):
         step()
-        if i >= 4 and i % 2:
+        if 1 <= i < 10:
+            work.unit()
+        if 1 <= i < 5:
             work.unit()
     seq = cot.shape[0]
     mlp_grad[...] = jnp.zeros(mlp_grad.shape, f32)

time: 867 us -> 858 us (0.990)
  Pallas kernels: 826 us -> 817 us
where the time goes in v6:
time: 858 us; the launch traced here: 849 us
  Pallas kernels  817 us (95%)
  local copies, waits for them, and re-layouts  21.7 us (3%)
  other arithmetic  9.25 us (1%)
    pallas_call x1, Pallas kernels, front(): pl.pallas_call(functools.partial(front_kernel, nz, scale), out_shape=[jax...  220 us
    pallas_call x1, Pallas kernels, run_experts(): pl.pallas_call(functools.partial(experts_kernel, nz, cap), out_shape=[sha...  184 us
    pallas_call x1, Pallas kernels, middle(): pl.pallas_call(functools.partial(middle_kernel, nz, cap, deep), out_shape...  175 us
    pallas_call x1, Pallas kernels, reduce_last(): pl.pallas_call(functools.partial(last_kernel, nz, cap, col), out_shape=[s...  125 us
    pallas_call x1, Pallas kernels, back(): pl.pallas_call(functools.partial(back_kernel, nz, cap, scale), out_shape=...  114 us
    unnamed x36, local copies, waits for them, and re-layouts  17.4 us

profile of v6, /device:TPU:16, one launch (start us, length us, event | category | flops | bytes accessed | tf_op | source)
XLA Modules:
  0.0 849.0 jit_solution(12744995430816563811)
XLA Ops:
  0.6 0.0 copy-start
  0.7 0.0 copy-start.9
  0.7 0.0 copy-start.6
  0.7 0.7 tile.20
  1.4 0.1 tile.21
  1.5 0.7 tile.8
  2.2 0.1 tile.9
  2.3 0.7 convert_bitcast_fusion
  3.0 0.7 reshape.182
  3.7 0.6 select_maximum_fusion.refs_4_
  4.3 1.9 fusion.2
  6.2 1.3 pad_maximum_fusion.1
  7.6 0.0 copy-done
  7.6 0.0 copy-done.9
  7.6 0.0 copy-done.6
  7.6 0.9 pad_maximum_fusion.refs_0_
  8.5 219.5 %shard_map.212 = (bf16[4,8,64,1280]{3,2,1,0:T(8,128)(2,1)}, bf16[8,128,2048]{2,1,0:T(8,128)(2,1)}, bf16[4,256,2048]{2,1,0:T(8,128)(2,1)}, bf16[32,256,2048]{2,1,...) custom-call(bf16[4,64,1280]{2,1,0:T(8,128)(2,1)} %pad_maximum_fusion, ...), custom_call_target="tpu_custom_call" | custom-call | tf_op jit(solution)/shard_map/pallas_call | solution.py:991
  228.1 183.6 %shard_map.213 = (bf16[32,256,2048]{2,1,0:T(8,128)(2,1)}, bf16[32,80,2048]{2,1,0:T(8,128)(2,1)}, bf16[32,80,2048]{2,1,0:T(8,128)(2,1)}, bf16[4,2,320,2048]{3,2,1...) custom-call(bf16[256,2048]{1,0:T(8,128)(2,1)} %get-tuple-element.52., ...), custom_call_target="tpu_custom_call" | custom-call | tf_op jit(solution)/shard_map/pallas_call | solution.py:2089
  411.7 0.6 broadcast_in_dim.37.refs_7_
  412.3 174.9 %shard_map.214 = (f32[256,2048]{1,0:T(8,128)}, f32[1,2048]{1,0:T(1,128)}, bf16[4,256,2048]{2,1,0:T(8,128)(2,1)}, f32[2048,768]{1,0:T(8,128)}, f32[2048,768]{1,0:T(8,128)}, /*index=5*/f32[768,2048]{1,0:T(8,128)}) custom-call(bf16[32,80,2048]{2,1,0:T(8,128)(2,1)} %get-tuple-element.56.refs_0_, bf16[2560,2048]{1,0:T(8,128)(2,1)} %bitcast.45, ...), custom_call_target="tpu_custom_call" | custom-call | tf_op jit(solution)/shard_map/pallas_call | solution.py:1442
  587.2 113.8 %shard_map.215 = (f32[128,2048]{1,0:T(8,128)}, bf16[4,8,64,1280]{3,2,1,0:T(8,128)(2,1)}, bf16[4,256,2048]{2,1,0:T(8,128)(2,1)}, f32[2,128]{1,0:T(2,128)}, f32[256,1024]{1,0:T(8,128)}) custom-call(bf16[4,256,2048]{2,1,0:T(8,128)(2,1)} %get-tuple-element.63.refs_0_, bf16[8,128,2048]{2,1,0:T(8,128)(2,1)} %get-tuple-element.64.refs_1_, ...), custom_call_target="tpu_custom_call" | custom-call | tf_op jit(solution)/shard_map/pallas_call | solution.py:1740
  701.1 0.0 copy-start.2
  701.1 0.0 copy-start.3
  701.1 125.2 %shard_map.216 = (f32[64,4096]{1,0:T(8,128)}, f32[64,512]{1,0:T(8,128)}, f32[64,512]{1,0:T(8,128)}, f32[32,48,128]{2,1,0:T(8,128)}, bf16[256,2048]{1,0:T(8,128)(2,1)}, /*index=5*/f32[256,1024]{1,0:T(8,128)}) custom-call(bf16[4,8,64,1280]{3,2,1,0:T(8,128)(2,1)} %get-tuple-element.76.refs_0_, bf16[32,80,2048]{2,1,0:T(8,128)(2,1)} %get-tuple-element.70.refs_7_.refs_1_, ...), custom_call_target="tpu_custom_call" | custom-call | tf_op jit(solution)/shard_map/pallas_call | solution.py:1891
  826.3 0.0 copy-start.5
  826.3 0.0 copy-done.2
  826.3 0.0 copy-done.3
  826.3 0.0 copy-start.8
  826.3 0.0 copy-start.7
  826.3 0.0 copy-start.4
  826.3 2.6 fusion.1
  828.9 1.2 reduce_sum.9
  830.2 0.6 constant_dynamic-slice_fusion.1
  830.8 0.6 constant_dynamic-slice_fusion
  831.4 2.3 copy.42
  833.7 0.0 copy-done.5
  833.7 1.0 copy.43
  834.7 0.0 copy-done.8
  834.7 0.7 copy.44
  835.4 0.0 copy-done.7
  835.4 0.7 copy.45
  836.0 1.0 copy.46
  837.0 6.1 copy.47
  843.1 0.0 slice-done.3
  843.1 0.0 copy-start.1
  843.1 2.8 copy.48
  845.9 0.2 slice-done.1
  846.2 2.7 copy.49
  (21 shorter events, 0.1 us)
Async XLA Ops:
  0.6 6.9 copy-start
  0.7 6.9 copy-start.9
  0.7 6.9 copy-start.6
  701.1 125.2 %copy-start.2 = (f32[256,2048]{1,0:T(8,128)S(1)}, f32[256,2048]{1,0:T(8,128)}, u32[]{:S(2)}) copy-start(f32[256,2048]{1,0:T(8,128)} %get-tuple-element.51.refs_8_) | copy-start | bytes 6291460
  701.1 125.2 %copy-start.3 = (f32[256,1024]{1,0:T(8,128)S(1)}, f32[256,1024]{1,0:T(8,128)}, u32[]{:S(2)}) copy-start(f32[256,1024]{1,0:T(8,128)} %get-tuple-element.75) | copy-start | bytes 3145732
  826.3 7.5 copy-start.5
  826.3 8.4 copy-start.8
  826.3 9.1 %copy-start.7 = (f32[64,512]{1,0:T(8,128)S(1)}, f32[64,512]{1,0:T(8,128)}, u32[]{:S(2)}) copy-start(f32[64,512]{1,0:T(8,128)} %get-tuple-element.115) | copy-start | bytes 393220
  826.3 9.7 %copy-start.4 = (f32[128,2048]{1,0:T(8,128)S(1)}, f32[128,2048]{1,0:T(8,128)}, u32[]{:S(2)}) copy-start(f32[128,2048]{1,0:T(8,128)} %get-tuple-element.116) | copy-start | bytes 3145732
  833.7 9.3 %slice-start.2 = ((s8[6291456]{0:T(1024)(128)(4,1)}), s8[4194304]{0:T(1024)(128)(4,1)S(1)}, s32[]{:S(2)}) async-start(s8[6291456]{0:T(1024)(128)(4,1)} %bitcast.50), calls=%async_computation.2 | async-start | bytes 8388608
  837.0 6.1 slice-start.3
  837.0 8.9 %slice-start = ((s8[6291456]{0:T(1024)(128)(4,1)}), s8[4194304]{0:T(1024)(128)(4,1)S(1)}, s32[]{:S(2)}) async-start(s8[6291456]{0:T(1024)(128)(4,1)} %bitcast.47), calls=%async_computation | async-start | bytes 8388608
  843.1 3.1 slice-start.1
  843.1 5.8 copy-start.1
